TPU v7x, 32 devices: a whole 2x2x4 slice. The times are simulated.
32 devices in a mesh: row: 4 (over y, x), col: 8 (over z, core).
Axes of the slice: x: 2, y: 2, z: 4, core: 2. Of those that a mesh axis runs over, the one named last changes fastest.
Arguments:
- ancestor_inverse: float32 [8192, 8192], P('row', 'col'), may hold values from -6 to 6
- panel: float32 [6, 32, 256, 256], P(None, 'row', 'col'), may hold values from -0.09375 to 0.09375
- diag_inverse: float32 [6, 256, 256], replicated, as said below
- structure: int32 [6, 16], replicated, may hold values from 0 to 31, as said below
- block_slot: int32 [32], replicated, may hold values from 0 to 31, as said below
Outputs:
- off_block: float32 [6, 32, 256, 256], P(None, 'row', 'col')
- diag_block: float32 [6, 256, 256], replicated
Inputs may be any that keep to these rules, and one draw needn't show every extreme that they name: `structure`: the 16 entries of a supernode are distinct global row blocks. Mapped through block_slot, at most 6 of them fall into any aligned run of 8 storage slots, and for every supernode some run holds exactly 6. `block_slot`: A permutation of the 32 row blocks. `diag_inverse`: lower triangular with a positive diagonal.
All inputs are finite; a program needn't handle non-finite values.
Results may differ from a plain program's by a relative error of at most 0.0001.
Values sent between devices are 32-bit elements; how exact they have to be, the bound alone decides.
No kernel may reach another device: no remote copies, remote signals or barrier semaphores. Data moves between devices by JAX's collectives and lax.ppermute only.
A program may use at most 128 MiB of HBM per device.

v0:
```python
import jax
import jax.numpy as jnp
from jax import lax
from jax.sharding import PartitionSpec as P

CAP = 6


def spread(block, axis, owner):
    block = jnp.where(lax.axis_index(axis) == owner, block, jnp.zeros_like(block))
    return lax.psum(block, axis)


def gather_rows(normalized):
    return lax.all_gather(normalized, "col", axis=2, tiled=True)


def body(ancestor_inverse, panel, diag_inverse, structure, block_slot):
    highest = lax.Precision.HIGHEST
    row_count = lax.axis_size("row")
    col_count = lax.axis_size("col")
    row_index = lax.axis_index("row")
    col_index = lax.axis_index("col")
    node_count, slot_count, sub_rows, block_width = panel.shape
    total_slots = slot_count * row_count
    col_slots = total_slots // col_count
    slot_range = jnp.arange(total_slots, dtype=jnp.int32)
    lookup = (structure[:, :, None] == slot_range[None, None, :]).astype(jnp.int32)
    slot_ids = jnp.sum(lookup * block_slot[None, None, :], axis=2)
    chosen = jnp.any(slot_ids[:, :, None] == slot_range[None, None, :], axis=1).astype(jnp.int32)
    local_mask = lax.dynamic_slice_in_dim(chosen, row_index * slot_count, slot_count, 1)
    weight_mask = local_mask.astype(jnp.float32)[:, :, None, None]
    normalized = jnp.einsum("sqik,skw->sqiw", panel, diag_inverse, precision=highest) * weight_mask
    first_slot = col_index * col_slots
    owner_row = first_slot // slot_count
    row_panel = gather_rows(normalized)
    picked = lax.dynamic_slice_in_dim(row_panel, first_slot % slot_count, col_slots, 1)
    column_panel = spread(picked, "row", owner_row)
    column_rows = column_panel.reshape(node_count, col_slots * block_width, block_width)
    leading = jnp.einsum("sij,sik->sjk", diag_inverse, diag_inverse, precision=highest)
    position = jnp.cumsum(local_mask, axis=1) - 1
    onehot = (position[:, None, :] == jnp.arange(CAP, dtype=jnp.int32)[None, :, None]) & (
        local_mask[:, None, :] == 1
    )
    selector = onehot.astype(jnp.float32)
    pick_rows = jnp.sum(
        onehot.astype(jnp.int32) * jnp.arange(slot_count, dtype=jnp.int32)[None, None, :], axis=2
    )
    source = ancestor_inverse.reshape(slot_count, block_width, col_slots * block_width)
    packed_rows = jnp.take(source, pick_rows, axis=0)
    partial_value = jnp.einsum("skrc,scw->skrw", packed_rows, column_rows, precision=highest)
    summed = lax.psum_scatter(partial_value, "col", scatter_dimension=2, tiled=True)
    product = jnp.einsum("ska,skiw->saiw", selector, summed, precision=highest)
    diag_terms = jnp.einsum("saiw,saiv->swv", normalized, product, precision=highest)
    diag_sum = lax.psum(diag_terms, ("row", "col"))
    return (-product, leading + diag_sum)


def solution(mesh):
    in_specs = (P("row", "col"), P(None, "row", "col", None), P(), P(), P())
    out_specs = (P(None, "row", "col", None), P())
    return jax.shard_map(body, mesh=mesh, in_specs=in_specs, out_specs=out_specs, check_vma=False)
```

profile of v0, /device:TPU:0, one launch (start us, length us, event | category | flops | bytes accessed | tf_op | source)
XLA Modules:
  0.0 582.9 jit_solution(3590475211160836528)
XLA Ops:
  7.2 1.1 select_reduce_fusion
  8.3 0.1 fusion.17
  8.4 0.1 fusion.24
  8.5 0.1 copy-done
  8.6 4.2 fusion.14
  12.8 0.0 all-reduce.3.cloned.1.call-start
  12.9 119.5 %all-gather.2.cloned.1.call-done = f32[6,8,256,256]{3,2,1,0:T(8,128)} async-done(((f32[6,8,32,256]{3,2,1,0:T(8,128)}), f32[6,8,256,256]{3,2,1,0:T(8,128)}) %all-gather.2.cloned.1.call-update) | async-done | bytes 12582928 | tf_op jit(solution)/shard_map/all_gather | solution.py:15
  132.4 6.1 %dynamic-slice_select_fusion = f32[6,4,256,256]{3,2,1,0:T(8,128)} fusion(f32[6,8,256,256]{3,2,1,0:T(8,128)} %all-gather.2.cloned.1.call-done, s32[]{:T(128)S(6)} %select_n.52, pred[]{:T(512)S(6)} %eq.62), kind=kLoop, calls=%fused_computation.7 | loop fusion | flops 1572864 | bytes 12582917 | tf_op jit(solution)/shard_map/jit(_where)/select_n | solution.py:10
  138.5 0.2 reduce_window_sum.11
  138.7 0.1 select_reduce_fusion.1
  138.8 0.1 reshape.45
  138.9 18.3 %gather_fusion = f32[36,256,1024]{2,1,0:T(8,128)} fusion(f32[8,256,1024]{2,1,0:T(8,128)} %bitcast.42, s32[1024]{0:T(1024)S(1)} %pad_clamp_fusion), kind=kCustom, calls=%fused_computation | custom fusion | bytes 75497616 | tf_op jit(solution)/shard_map/jit(_take)/gather | solution.py:50
  157.2 118.1 %all-reduce.3.cloned.1.call-done = f32[6,1024,256]{2,1,0:T(8,128)} async-done(((f32[6,1024,256]{2,1,0:T(8,128)}), f32[6,1024,256]{2,1,0:T(8,128)}) %all-reduce.3.cloned.1.call-update) | async-done | bytes 6291472 | tf_op jit(solution)/shard_map/psum | solution.py:11
  275.3 34.2 %fusion = f32[6,6,256,256]{3,2,1,0:T(8,128)S(1)} fusion(f32[6,6,256,1024]{3,2,1,0:T(8,128)} %bitcast.43, pred[6,6]{1,0:T(8,128)(4,1)S(1)} %compare_and_fusion, f32[6,1024,256]{2,1,0:T(8,128)} %all-reduce.3.cloned.1.call-done), kind=kOutput, calls=%fused_computation.1 | convolution fusion | flops 29000466432 | bytes 53477412 | tf_op jit(solution)/shard_map/skrc,scw->skrw/dot_general | solution.py:51
  309.5 10.2 %copy.38 = f32[6,6,256,256]{3,1,0,2:T(8,128)} copy(f32[6,6,256,256]{3,2,1,0:T(8,128)S(1)} %fusion) | data formatting | bytes 18874368
  319.8 11.4 %reshape.56 = f32[256,9216]{1,0:T(8,128)} reshape(f32[256,6,6,256]{3,2,1,0:T(8,128)} %bitcast.44) | data formatting | bytes 18874368
  331.2 0.3 all-reduce.5.cloned.1.call-start
  331.5 99.4 %reduce-scatter.4.cloned.1.call-done = f32[32,9216]{1,0:T(8,128)} async-done(((f32[256,9216]{1,0:T(8,128)}), f32[32,9216]{1,0:T(8,128)}) %reduce-scatter.4.cloned.1.call-update) | async-done | bytes 1179664
  430.9 3.0 reshape.57
  433.9 2.4 fusion.25
  436.3 4.3 fusion.11
  440.6 1.6 copy.20
  442.2 128.9 %all-reduce.5.cloned.1.call-done = f32[6,256,256]{2,1,0:T(8,128)} async-done(((f32[6,256,256]{2,1,0:T(8,128)}), f32[6,256,256]{2,1,0:T(8,128)}) %all-reduce.5.cloned.1.call-update) | async-done | bytes 1572880 | tf_op jit(solution)/shard_map/psum | solution.py:55
  571.2 5.2 convolution_add_fusion
  (15 shorter events, 0.2 us)
Async XLA Ops:
  7.2 1.4 copy-start
  7.2 125.2 %all-gather.2.cloned.1.call-start = ((), (), s32[]{:S(2)}) async-start(), calls=%async_computation.1 | async-start | bytes 14155776 | tf_op jit(solution)/shard_map/all_gather | solution.py:15
  12.8 262.5 %all-reduce.3.cloned.1.call-start = ((), (), s32[]{:S(2)}) async-start(), calls=%async_computation.2 | async-start | bytes 12582912 | tf_op jit(solution)/shard_map/psum | solution.py:11
  138.5 292.4 %reduce-scatter.4.cloned.1.call-start = ((), (), s32[]{:S(2)}) async-start(), calls=%async_computation.4 | async-start | bytes 10616832
  331.2 240.0 %all-reduce.5.cloned.1.call-start = ((), (), s32[]{:S(2)}) async-start(), calls=%async_computation.3 | async-start | bytes 3145728 | tf_op jit(solution)/shard_map/psum | solution.py:55
  433.9 2.4 copy-start.1
Sparse Core Ops, SparseCore 0:
  12.9 119.4 all-gather.1
  138.6 136.6 all-reduce.2
  331.3 99.5 reduce-scatter.3
  440.7 130.4 all-reduce.4
where the time goes:
time: 583 us
  waiting for transfers between devices  466 us (80%)
  matrix products  50.3 us (9%)
  local copies, waits for them, and re-layouts  44.8 us (8%)
  between operations  13.9 us (2%)
  other arithmetic  7.6 us (1%)
    psum x1, waiting for transfers between devices, body(): diag_sum = lax.psum(diag_terms, ('row', 'col'))  129 us
    all_gather x1, waiting for transfers between devices, gather_rows(): return lax.all_gather(normalized, 'col', axis=2, tiled=True)  120 us
    psum x1, waiting for transfers between devices, spread(): return lax.psum(block, axis)  118 us
    unnamed x5, waiting for transfers between devices  99.5 us
    dot_general x1, matrix products, body(): jnp.einsum('skrc,scw->skrw', packed_rows, column_rows, precision=highest)  34.2 us
    unnamed x8, local copies, waits for them, and re-layouts  26.4 us
    gather x1, local copies, waits for them, and re-layouts, body(): packed_rows = jnp.take(source, pick_rows, axis=0)  18.3 us
  transfers between devices with their start and end apart: 4, of which 4 were waited for; matrix products, arithmetic and copies ran while one was open for 3% of the time, Pallas kernels for 0%

commit v1 on v0

v1 whole, which is shorter than its diff:
```python
import functools

import jax
import jax.numpy as jnp
from jax import lax
from jax.experimental import pallas as pl
from jax.experimental.pallas import tpu as pltpu
from jax.sharding import PartitionSpec as P

CAP = 6
BATCHES = (2, 2, 2)
F32 = jnp.float32
BF16 = jnp.bfloat16
VMEM_LIMIT = 48 * 1024 * 1024

COUNT, SLOT = 0, 1
FIRST, OWN, OWN_SLOT = SLOT + CAP + 1, SLOT + CAP + 2, SLOT + CAP + 3


def split(x):
    high = x.astype(BF16)
    return high, (x - high.astype(F32)).astype(BF16)


def dot3(a, b, dims):
    dot = functools.partial(lax.dot_general, dimension_numbers=(dims, ((), ())), preferred_element_type=F32)
    return dot(a[0], b[1]) + dot(a[1], b[0]) + dot(a[0], b[0])


def prepare_kernel(n, g, batches, ids, structure, block_slot, panel, dinv, table, packed, *rest):
    pieces, gathered = rest[:-1], rest[-1]
    r, z, c = ids[0], ids[1], ids[2]
    node_count, slot_count, sub, width = panel.shape
    col_slots = slot_count // g
    piece = sub // n
    pos_base = OWN_SLOT + col_slots + 1
    place = [(b, i) for b, count in enumerate(batches) for i in range(count)]
    for s in range(node_count):
        row_bits = jnp.int32(0)
        col_bits = jnp.int32(0)
        for k in range(structure.shape[1]):
            slot = block_slot[structure[s, k]]
            for which in range(2):
                at = slot - (r, z)[which] * slot_count
                inside = (at >= 0) & (at < slot_count)
                bit = jnp.where(inside, jnp.left_shift(jnp.int32(1), jnp.where(inside, at, 0)), 0)
                if which == 0:
                    row_bits = row_bits | bit
                else:
                    col_bits = col_bits | bit
        for k in range(CAP + 1):
            table[s, SLOT + k] = 0
        for k in range(col_slots + 1):
            table[s, OWN_SLOT + k] = 0
        count = jnp.int32(0)
        for q in range(slot_count):
            bit = (row_bits >> q) & 1
            table[s, SLOT + jnp.minimum(count, CAP)] = q
            table[s, pos_base + q] = jnp.where(bit == 1, count, -1)
            count = count + bit
        table[s, COUNT] = count
        first, own = jnp.int32(0), jnp.int32(0)
        for q in range(slot_count):
            bit = (col_bits >> q) & 1
            mine = (q // col_slots) == c
            table[s, OWN_SLOT + own] = q % col_slots
            own = own + jnp.where(mine, bit, 0)
            first = first + jnp.where(q // col_slots < c, bit, 0)
        table[s, FIRST] = first
        table[s, OWN] = own
        for k in range(CAP):
            gathered[pl.ds(k * sub, sub), :] = jnp.where(k < count, panel[s, table[s, SLOT + k]], 0.0)
        rows = dot3(split(gathered[...]), split(dinv[s]), ((1,), (0,))).reshape(CAP, sub, width)
        packed[s] = rows
        b, i = place[s]
        for k in range(n):
            part = rows[:, :piece]
            for j in range(1, n):
                part = jnp.where((r ^ k) == j, rows[:, j * piece : (j + 1) * piece], part)
            pieces[b * n + k][pl.ds(i * CAP, CAP)] = part


def product_kernel(n, g, start, ids, table, ancestor, *rest):
    parts, outs = rest[: n * g], rest[n * g : n * g + g]
    blocks, gathered, acc, sems = rest[n * g + g :]
    r, c = ids[0], ids[2]
    node_count, col_slots = blocks.shape[:2]
    width = gathered.shape[0]
    sub = width // (n * g)
    piece = sub // n

    def copy(i, j, k):
        rows = pl.multiple_of(table[start + i, SLOT + k] * width, width)
        cols = pl.multiple_of(table[start + i, OWN_SLOT + j] * width, width)
        source = ancestor.at[pl.ds(rows, width), pl.ds(cols, width)]
        return pltpu.make_async_copy(source, blocks.at[i, j, k], sems.at[i, j, k])

    def each(i, j, what):
        lax.fori_loop(0, table[start + i, COUNT], lambda k, _: what(i, j, k), None)

    for i in range(node_count):
        lax.fori_loop(0, table[start + i, OWN], lambda j, _: each(i, j, lambda *at: copy(*at).start()), None)

    for i in range(node_count):
        rows, own, first = table[start + i, COUNT], table[start + i, OWN], table[start + i, FIRST]

        def column(j, _):
            entry = i * CAP + first + j
            for jk in range(n):
                for kc in range(g):
                    for zz in range(n):
                        at = zz * (g * sub) + (c ^ kc) * sub + (r ^ jk) * piece
                        gathered[pl.ds(pl.multiple_of(at, piece), piece), :] = parts[jk * g + kc][zz, entry]
            right = split(gathered[...])

            def row(i, j, k):
                copy(i, j, k).wait()
                value = dot3(split(blocks[i, j, k]), right, ((1,), (0,)))
                acc[k] = jnp.where(j == 0, value, acc[k] + value)

            each(i, j, row)

        lax.fori_loop(0, own, column, None)
        for k in range(CAP):
            live = (k < rows) & (own > 0)
            for kc in range(g):
                for zz in range(n):
                    part = acc[k, pl.ds(zz * g * sub, sub), :]
                    for j in range(1, g):
                        part = jnp.where((c ^ kc) == j, acc[k, pl.ds((zz * g + j) * sub, sub), :], part)
                    outs[kc][zz, i * CAP + k] = jnp.where(live, part, 0.0)


def finish_kernel(g, start, ids, table, base, *rest):
    received, (packed, dinv, _, off), rest = rest[: -g - 5], rest[-g - 5 : -g - 1], rest[-g - 1 :]
    diags, product = rest[:g], rest[g]
    c = ids[2]
    s = start + pl.program_id(0)
    slot_count, sub, width = off.shape[1:]
    pos_base = OWN_SLOT + slot_count // g + 1
    total = base[0]
    for more in received:
        total = total + more[0]
    product[...] = total
    for q in range(slot_count):
        at = table[s, pos_base + q]
        block = product[jnp.maximum(at, 0)]
        off[0, q] = jnp.where(at >= 0, -block, 0.0)
    mine = packed[0].reshape(CAP * sub, width)
    dims = ((0,), (0,))
    diag = dot3(split(mine), split(product[...].reshape(CAP * sub, width)), dims)

    def store(value):
        half = width // g
        for kc in range(g):
            part = value[:half]
            for j in range(1, g):
                part = jnp.where((c ^ kc) == j, value[j * half : (j + 1) * half], part)
            diags[kc][0] = part

    store(diag)

    @pl.when((ids[0] == 0) & (ids[1] == 0) & (c == 0))
    def _():
        factor = split(dinv[0])
        store(diag + dot3(factor, factor, dims))


def tree_sum(terms):
    while len(terms) > 1:
        terms = [terms[i] + terms[i + 1] for i in range(0, len(terms), 2)]
    return terms[0]


def pick(arrays, index):
    value = arrays[0]
    for k in range(1, len(arrays)):
        value = jnp.where(index == k, arrays[k], value)
    return value


def after(x):
    return list(lax.optimization_barrier(x))


def body(ancestor, panel, dinv, structure, block_slot):
    n = lax.axis_size("row")
    g = lax.axis_size("col") // n
    r = lax.axis_index("row")
    col = lax.axis_index("col")
    z, c = col // g, col % g
    node_count, slot_count, sub, width = panel.shape
    col_slots = slot_count // g
    piece = sub // n
    ids = jnp.stack([r, z, c]).astype(jnp.int32)
    table_width = OWN_SLOT + col_slots + 1 + slot_count
    batches = BATCHES
    smem = pl.BlockSpec(memory_space=pltpu.SMEM)
    vmem = pl.BlockSpec(memory_space=pltpu.VMEM)
    params = pltpu.CompilerParams(vmem_limit_bytes=VMEM_LIMIT)

    def along_row(x, k):
        return lax.ppermute(x, "row", [(i, i ^ k) for i in range(n)])

    def along_z(x, m):
        return lax.ppermute(x, "col", [(i * g + j, (i ^ m) * g + j) for i in range(n) for j in range(g)])

    def along_core(x, k):
        return lax.ppermute(x, "col", [(i * g + j, i * g + (j ^ k)) for i in range(n) for j in range(g)])

    out = pl.pallas_call(
        functools.partial(prepare_kernel, n, g, batches),
        out_shape=[
            jax.ShapeDtypeStruct((node_count, table_width), jnp.int32),
            jax.ShapeDtypeStruct((node_count, CAP, sub, width), F32),
        ]
        + [jax.ShapeDtypeStruct((count * CAP, piece, width), F32) for count in batches for _ in range(n)],
        in_specs=[smem, smem, smem, vmem, vmem],
        out_specs=[smem] + [vmem] * (1 + n * len(batches)),
        scratch_shapes=[pltpu.VMEM((CAP * sub, width), F32)],
        compiler_params=params,
        name="prepare",
    )(ids, structure, block_slot, panel, dinv)
    table, packed, pieces = out[0], out[1], out[2:]

    starts = [sum(batches[:b]) for b in range(len(batches))]
    halvings = n.bit_length() - 1

    def spread_stage(b, own):
        return [own[0]] + [along_row(own[k], k) for k in range(1, n)]

    def cross_stage(b, spread):
        got = [pick(spread, r ^ z ^ m) for m in range(n)]
        return [got[0]] + [along_z(got[m], m) for m in range(1, n)]

    def plane_stage(b, got):
        run = jnp.stack([pick(got, z ^ i) for i in range(n)])
        return [run] + [along_row(run, k) for k in range(1, n)]

    def product_stage(b, plane):
        start, count = starts[b], batches[b]
        total = count * CAP
        parts = [x if k == 0 else along_core(x, k) for x in plane for k in range(g)]
        outs = pl.pallas_call(
            functools.partial(product_kernel, n, g, start),
            out_shape=[jax.ShapeDtypeStruct((n, total, sub, width), F32)] * g,
            in_specs=[smem, smem, pl.BlockSpec(memory_space=pl.ANY)] + [vmem] * (n * g),
            out_specs=[vmem] * g,
            scratch_shapes=[
                pltpu.VMEM((count, col_slots, CAP, width, width), F32),
                pltpu.VMEM((width, width), F32),
                pltpu.VMEM((CAP, width, width), F32),
                pltpu.SemaphoreType.DMA((count, col_slots, CAP)),
            ],
            compiler_params=params,
            cost_estimate=pl.CostEstimate(flops=1, bytes_accessed=1, transcendentals=0),
            name="product",
        )(ids, table, ancestor, *parts)
        return outs

    def halving_stage(i, b, held):
        if i == 0:
            base = held[0]
            for k in range(1, g):
                base = base + along_core(held[k], k)
            held = [base]
        high, low, bit = n >> (i + 1), 1 << i, (z >> i) & 1
        send = None
        for at, array in enumerate(held):
            inner = low >> at
            split_up = array.reshape((high, 2, inner) + array.shape[1:])
            start_at = (0, 1 - bit, (z >> at) & (inner - 1)) + (0,) * (array.ndim - 1)
            part = lax.dynamic_slice(split_up, start_at, (high, 1, 1) + array.shape[1:])
            part = part.reshape((high,) + array.shape[1:])
            send = part if send is None else send + part
        return held + [along_z(send, low)]

    stages = [spread_stage, cross_stage, plane_stage, product_stage]
    stages += [functools.partial(halving_stage, i) for i in range(halvings)]
    state = [pieces[b * n : (b + 1) * n] for b in range(len(batches))]
    half = width // g
    off = jnp.zeros((node_count, slot_count, sub, width), F32)
    diag_list = []
    for phase in range(len(batches) + len(stages)):
        state = after(state)
        done = phase - len(stages)
        for b in range(len(batches)):
            if 0 <= phase - b < len(stages):
                state[b] = stages[phase - b](b, state[b])
        if done < 0:
            continue
        start, count = starts[done], batches[done]
        of_node = lambda i, ids, table, start=start: (start + i, 0, 0, 0)
        of_dest = lambda at: lambda i, ids, table: (ids[1] >> at, i, 0, 0)
        result = pl.pallas_call(
            functools.partial(finish_kernel, g, start),
            out_shape=[jax.ShapeDtypeStruct(off.shape, F32)]
            + [jax.ShapeDtypeStruct((count, half, width), F32)] * g,
            grid_spec=pltpu.PrefetchScalarGridSpec(
                num_scalar_prefetch=2,
                grid=(count,),
                in_specs=[pl.BlockSpec((1, CAP, sub, width), of_dest(at)) for at in range(halvings + 1)]
                + [
                    pl.BlockSpec((1, CAP, sub, width), of_node),
                    pl.BlockSpec((1, width, width), lambda i, ids, table, start=start: (start + i, 0, 0)),
                    pl.BlockSpec(memory_space=pl.ANY),
                ],
                out_specs=[pl.BlockSpec((1, slot_count, sub, width), of_node)]
                + [pl.BlockSpec((1, half, width), lambda i, ids, table: (i, 0, 0))] * g,
                scratch_shapes=[pltpu.VMEM((CAP, sub, width), F32)],
            ),
            input_output_aliases={5 + halvings: 0},
            compiler_params=params,
            cost_estimate=pl.CostEstimate(flops=1, bytes_accessed=1, transcendentals=0),
            name="finish",
        )(ids, table, *state[done], packed, dinv, off)
        off, shares = result[0], result[1:]
        state[done] = []

        share = shares[0]
        for k in range(1, g):
            share = share + along_core(shares[k], k)
        quarter = half // n
        cut = [lax.dynamic_slice_in_dim(share, (r ^ k) * quarter, quarter, 1) for k in range(n)]
        part = tree_sum([cut[0]] + [along_row(cut[k], k) for k in range(1, n)])
        part = tree_sum([part] + [along_z(part, m) for m in range(1, n)])
        parts = [part] + [along_row(part, k) for k in range(1, n)]
        mine = jnp.concatenate([pick(parts, r ^ j) for j in range(n)], axis=1)
        halves = [mine] + [along_core(mine, k) for k in range(1, g)]
        diag_list.append(jnp.concatenate([pick(halves, c ^ j) for j in range(g)], axis=1))
    return off, jnp.concatenate(diag_list, axis=0)


def solution(mesh):
    in_specs = (P("row", "col"), P(None, "row", "col", None), P(), P(), P())
    out_specs = (P(None, "row", "col", None), P())
    return jax.shard_map(body, mesh=mesh, in_specs=in_specs, out_specs=out_specs, check_vma=False)
```

time: 583 us -> 249 us (0.43)
  waiting for transfers between devices: 466 us -> 90.5 us
  starting transfers between devices: 0.39 us -> 82.1 us
  matrix products: 50.3 us -> 0 us
  Pallas kernels: 0 us -> 46.7 us
  local copies, waits for them, and re-layouts: 44.8 us -> 14 us
  between operations: 13.9 us -> 1.25 us
    psum x2 -> x0, waiting for transfers between devices: 247 us -> none  [the longest x1 129 us: body(): diag_sum = lax.psum(diag_terms, ('row', 'col'))]
    all_gather x1 -> x0, waiting for transfers between devices: 120 us -> none  [gather_rows(): return lax.all_gather(normalized, 'col', axis=2, tiled=True)]
    unnamed x5 -> x0, waiting for transfers between devices: 99.5 us -> none
    ppermute x0 -> x81, waiting for transfers between devices: none -> 90.5 us  [the longest x24 50.4 us: along_z(): lax.ppermute(x, 'col', [(i * g + j, (i ^ m) * g + j) for i in range(n) fo...]
    ppermute x0 -> x81, starting transfers between devices: none -> 82.1 us  [the longest x36 41.4 us: along_row(): return lax.ppermute(x, 'row', [(i, i ^ k) for i in range(n)])]
    dot_general x5 -> x0, matrix products: 50.3 us -> none  [the longest x1 34.2 us: body(): jnp.einsum('skrc,scw->skrw', packed_rows, column_rows, precision=highest)]
    pallas_call x0 -> x7, Pallas kernels: none -> 46.7 us  [the longest x3 34.1 us: product_stage(): pl.pallas_call(functools.partial(product_kernel, n, g, start), out_shape=...]
    gather x1 -> x0, local copies, waits for them, and re-layouts: 18.3 us -> none  [body(): packed_rows = jnp.take(source, pick_rows, axis=0)]
  transfers between devices with their start and end apart: 4 -> 81, of which waited for: 4 -> 35; matrix products, arithmetic and copies ran while one was open for 3% -> 6% of each run, Pallas kernels for 0% -> 18%
where the time goes in v1:
time: 249 us; the launch traced here: 247 us
  waiting for transfers between devices  90.5 us (36%)
  starting transfers between devices  82.1 us (33%)
  Pallas kernels  46.7 us (19%)
  local copies, waits for them, and re-layouts  14 us (6%)
  other arithmetic  12.8 us (5%)
    ppermute x24, waiting for transfers between devices, along_z(): lax.ppermute(x, 'col', [(i * g + j, (i ^ m) * g + j) for i in range(n) fo...  50.4 us
    ppermute x36, starting transfers between devices, along_row(): return lax.ppermute(x, 'row', [(i, i ^ k) for i in range(n)])  41.4 us
    ppermute x24, starting transfers between devices, along_z(): lax.ppermute(x, 'col', [(i * g + j, (i ^ m) * g + j) for i in range(n) fo...  36.7 us
    pallas_call x3, Pallas kernels, product_stage(): pl.pallas_call(functools.partial(product_kernel, n, g, start), out_shape=...  34.1 us
    ppermute x36, waiting for transfers between devices, along_row(): return lax.ppermute(x, 'row', [(i, i ^ k) for i in range(n)])  30 us
    unnamed x54, local copies, waits for them, and re-layouts  10.7 us
    pallas_call x3, Pallas kernels, body(): pl.pallas_call(functools.partial(finish_kernel, g, start), out_shape=[jax...  10.1 us
    ppermute x21, waiting for transfers between devices, along_core(): lax.ppermute(x, 'col', [(i * g + j, i * g + (j ^ k)) for i in range(n) fo...  10.1 us
  transfers between devices with their start and end apart: 81, of which 35 were waited for; matrix products, arithmetic and copies ran while one was open for 6% of the time, Pallas kernels for 18%

profile of v1, /device:TPU:0, one launch (start us, length us, event | category | flops | bytes accessed | tf_op | source)
XLA Modules:
  0.0 247.3 jit_solution(16838666360185411866)
XLA Ops:
  8.4 2.9 %collective-permute-start = (f32[12,8,256]{2,1,0:T(8,128)S(1)}, f32[12,8,256]{2,1,0:T(8,128)S(1)}, u32[]{:S(2)}, u32[]{:S(2)}) collective-permute-start(f32[12,8,256]{2,1,0:T(8,128)S(1)} %get-tuple-element.126), channel_id=1, source_target_pairs={{0,8},{8,0},{16,24},{24,16},{1,9},{9,1},{17,25},{25,17},{2,10},{10... | collective-permute-start | bytes 294920 | tf_op jit(solution)/shard_map/ppermute | solution.py:203
  14.4 2.6 %collective-permute-done.1 = f32[12,8,256]{2,1,0:T(8,128)S(1)} collective-permute-done((f32[12,8,256]{2,1,0:T(8,128)S(1)}, f32[12,8,256]{2,1,0:T(8,128)S(1)}, u32[]{:S(2)}, u32[]{:S(2)}) %collective-permute-start.1) | collective-permute-done | bytes 98336 | tf_op jit(solution)/shard_map/ppermute | solution.py:203
  20.0 2.6 %collective-permute-start.4 = (f32[12,8,256]{2,1,0:T(8,128)S(1)}, f32[12,8,256]{2,1,0:T(8,128)S(1)}, u32[]{:S(2)}, u32[]{:S(2)}) collective-permute-start(f32[12,8,256]{2,1,0:T(8,128)S(1)} %get-tuple-element.249), channel_id=1, source_target_pairs={{0,4},{1,5},{2,6},{3,7},{4,0},{5,1},{6,2},{7,3},{8,12},{9,13},{10,... | collective-permute-start | bytes 294920 | tf_op jit(solution)/shard_map/ppermute | solution.py:206
  35.3 2.7 %collective-permute-start.13 = (f32[12,8,256]{2,1,0:T(8,128)S(1)}, f32[12,8,256]{2,1,0:T(8,128)S(1)}, u32[]{:S(2)}, u32[]{:S(2)}) collective-permute-start(f32[12,8,256]{2,1,0:T(8,128)S(1)} %get-tuple-element.241), channel_id=1, source_target_pairs={{0,4},{1,5},{2,6},{3,7},{4,0},{5,1},{6,2},{7,3},{8,12},{9,13},{10,... | collective-permute-start | bytes 294920 | tf_op jit(solution)/shard_map/ppermute | solution.py:206
  38.5 5.5 %collective-permute-start.14 = (f32[12,8,256]{2,1,0:T(8,128)S(1)}, f32[12,8,256]{2,1,0:T(8,128)S(1)}, u32[]{:S(2)}, u32[]{:S(2)}) collective-permute-start(f32[12,8,256]{2,1,0:T(8,128)S(1)} %get-tuple-element.240), channel_id=1, source_target_pairs={{0,6},{1,7},{2,4},{3,5},{4,2},{5,3},{6,0},{7,1},{8,14},{9,15},{10,... | collective-permute-start | bytes 294920 | tf_op jit(solution)/shard_map/ppermute | solution.py:206
  51.4 3.7 %collective-permute-done.17 = f32[12,8,256]{2,1,0:T(8,128)S(1)} collective-permute-done((f32[12,8,256]{2,1,0:T(8,128)S(1)}, f32[12,8,256]{2,1,0:T(8,128)S(1)}, u32[]{:S(2)}, u32[]{:S(2)}) %collective-permute-start.17) | collective-permute-done | bytes 98336 | tf_op jit(solution)/shard_map/ppermute | solution.py:203
  58.4 3.3 %collective-permute-done.25 = f32[12,8,256]{2,1,0:T(8,128)S(1)} collective-permute-done((f32[12,8,256]{2,1,0:T(8,128)S(1)}, f32[12,8,256]{2,1,0:T(8,128)S(1)}, u32[]{:S(2)}, u32[]{:S(2)}) %collective-permute-start.25) | collective-permute-done | bytes 98336 | tf_op jit(solution)/shard_map/ppermute | solution.py:206
  69.5 13.7 %product.3 = (f32[4,12,32,256]{3,2,1,0:T(8,128)S(1)}, f32[4,12,32,256]{3,2,1,0:T(8,128)}) custom-call(s32[3]{0:T(128)S(1)} %pad_add_fusion.ids, s32[6,23]{1,0:T(8,128)S(1)} %get-tuple-element.112.table, f32[2048,1024]{1,0:T(8,128)} %ancestor.5, f32[4,12,8,256]{3,2,1,0:T(8,128)S(1)} %pad_maximum_fusion.rest_0_, ...), custom_call_target="tpu_custom_call" | custom-call | flops 1 | bytes 1 | tf_op jit(solution)/shard_map/product/pallas_call | solution.py:244
  85.1 4.2 %collective-permute-done.28 = f32[4,12,32,256]{3,2,1,0:T(8,128)} collective-permute-done((f32[4,12,32,256]{3,2,1,0:T(8,128)}, f32[4,12,32,256]{3,2,1,0:T(8,128)}, u32[]{:S(2)}, u32[]{:S(2)}) %collective-permute-start.28) | collective-permute-done | bytes 1572896 | tf_op jit(solution)/shard_map/ppermute | solution.py:209
  93.8 2.5 %collective-permute-start.36 = (f32[4,12,8,256]{3,2,1,0:T(8,128)S(1)}, f32[4,12,8,256]{3,2,1,0:T(8,128)}, u32[]{:S(2)}, u32[]{:S(2)}) collective-permute-start(f32[4,12,8,256]{3,2,1,0:T(8,128)S(1)} %pad_maximum_fusion.2.rest_0_), channel_id=1, source_target_pairs={{0,24},{8,16},{16,8},{24,0},{1,25},{9,17},{17,9},{25,1},{2,26},{10... | collective-permute-start | bytes 1179656 | tf_op jit(solution)/shard_map/ppermute | solution.py:203
  96.3 5.7 %product.4 = (f32[4,12,32,256]{3,2,1,0:T(8,128)S(1)}, f32[4,12,32,256]{3,2,1,0:T(8,128)}) custom-call(s32[3]{0:T(128)S(1)} %pad_add_fusion.ids, s32[6,23]{1,0:T(8,128)S(1)} %get-tuple-element.112.table, f32[2048,1024]{1,0:T(8,128)} %ancestor.5, f32[4,12,8,256]{3,2,1,0:T(8,128)S(1)} %pad_maximum_fusion.1.rest_0_, ...), custom_call_target="tpu_custom_call" | custom-call | flops 1 | bytes 1 | tf_op jit(solution)/shard_map/product/pallas_call | solution.py:244
  102.0 2.7 %collective-permute-done.34.rest_2_ = f32[4,12,8,256]{3,2,1,0:T(8,128)S(1)} collective-permute-done((f32[4,12,8,256]{3,2,1,0:T(8,128)S(1)}, f32[4,12,8,256]{3,2,1,0:T(8,128)S(1)}, u32[]{:S(2)}, u32[]{:S(2)}) %collective-permute-start.34) | collective-permute-done | bytes 393248 | tf_op jit(solution)/shard_map/ppermute | solution.py:203
  104.8 7.8 %collective-permute-done.35.rest_4_ = f32[4,12,8,256]{3,2,1,0:T(8,128)} collective-permute-done((f32[4,12,8,256]{3,2,1,0:T(8,128)S(1)}, f32[4,12,8,256]{3,2,1,0:T(8,128)}, u32[]{:S(2)}, u32[]{:S(2)}) %collective-permute-start.35) | collective-permute-done | bytes 393248 | tf_op jit(solution)/shard_map/ppermute | solution.py:203
  113.2 3.7 %collective-permute-done.38 = f32[4,12,32,256]{3,2,1,0:T(8,128)S(1)} collective-permute-done((f32[4,12,32,256]{3,2,1,0:T(8,128)}, f32[4,12,32,256]{3,2,1,0:T(8,128)S(1)}, u32[]{:S(2)}, u32[]{:S(2)}) %collective-permute-start.38) | collective-permute-done | bytes 1572896 | tf_op jit(solution)/shard_map/ppermute | solution.py:209
  123.5 14.7 %product.5 = (f32[4,12,32,256]{3,2,1,0:T(8,128)S(1)}, f32[4,12,32,256]{3,2,1,0:T(8,128)}) custom-call(s32[3]{0:T(128)S(1)} %pad_add_fusion.ids, s32[6,23]{1,0:T(8,128)S(1)} %get-tuple-element.112.table, f32[2048,1024]{1,0:T(8,128)} %ancestor.5, f32[4,12,8,256]{3,2,1,0:T(8,128)S(1)} %pad_maximum_fusion.2.rest_0_, ...), custom_call_target="tpu_custom_call" | custom-call | flops 1 | bytes 1 | tf_op jit(solution)/shard_map/product/pallas_call | solution.py:244
  138.2 6.5 %collective-permute-done.37.rest_1_ = f32[1,12,32,256]{3,2,1,0:T(8,128)S(1)} collective-permute-done((f32[1,12,32,256]{3,2,1,0:T(8,128)S(1)}, f32[1,12,32,256]{3,2,1,0:T(8,128)S(1)}, u32[]{:S(2)}, u32[]{:S(2)}) %collective-permute-start.37) | collective-permute-done | bytes 393248 | tf_op jit(solution)/shard_map/ppermute | solution.py:206
  147.8 2.7 %finish.3 = (f32[6,8,32,256]{3,2,1,0:T(8,128)}, f32[2,128,256]{2,1,0:T(8,128)S(1)}, f32[2,128,256]{2,1,0:T(8,128)}) custom-call(s32[3]{0:T(128)S(1)} %pad_add_fusion.ids, s32[6,23]{1,0:T(8,128)S(1)} %get-tuple-element.112.table, f32[4,12,32,256]{3,2,1,0:T(8,128)S(1)} %copy-done.5, ...), custom_call_target="tpu_custom_call", output_to_operand_aliasing={{0}: (7, {})} | custom-call | flops 1 | bytes 1 | tf_op jit(solution)/shard_map/finish/pallas_call | solution.py:295
  165.8 16.4 %collective-permute-done.53 = f32[2,32,256]{2,1,0:T(8,128)S(1)} collective-permute-done((f32[2,32,256]{2,1,0:T(8,128)S(1)}, f32[2,32,256]{2,1,0:T(8,128)S(1)}, u32[]{:S(2)}, u32[]{:S(2)}) %collective-permute-start.53) | collective-permute-done | bytes 65568 | tf_op jit(solution)/shard_map/ppermute | solution.py:206
  182.2 3.4 %collective-permute-done.54 = f32[2,32,256]{2,1,0:T(8,128)S(1)} collective-permute-done((f32[2,32,256]{2,1,0:T(8,128)S(1)}, f32[2,32,256]{2,1,0:T(8,128)S(1)}, u32[]{:S(2)}, u32[]{:S(2)}) %collective-permute-start.54) | collective-permute-done | bytes 65568 | tf_op jit(solution)/shard_map/ppermute | solution.py:206
  192.8 3.7 %finish.4 = (f32[6,8,32,256]{3,2,1,0:T(8,128)}, f32[2,128,256]{2,1,0:T(8,128)S(1)}, f32[2,128,256]{2,1,0:T(8,128)}) custom-call(s32[3]{0:T(128)S(1)} %pad_add_fusion.ids, s32[6,23]{1,0:T(8,128)S(1)} %get-tuple-element.112.table, f32[4,12,32,256]{3,2,1,0:T(8,128)S(1)} %add.138.base, ...), custom_call_target="tpu_custom_call", output_to_operand_aliasing={{0}: (7, {})} | custom-call | flops 1 | bytes 1 | tf_op jit(solution)/shard_map/finish/pallas_call | solution.py:295
  203.8 6.8 %collective-permute-done.47.rest_1_ = f32[1,12,32,256]{3,2,1,0:T(8,128)S(1)} collective-permute-done((f32[1,12,32,256]{3,2,1,0:T(8,128)}, f32[1,12,32,256]{3,2,1,0:T(8,128)S(1)}, u32[]{:S(2)}, u32[]{:S(2)}) %collective-permute-start.47) | collective-permute-done | bytes 393248 | tf_op jit(solution)/shard_map/ppermute | solution.py:206
  211.9 3.7 %finish.5 = (f32[6,8,32,256]{3,2,1,0:T(8,128)}, f32[2,128,256]{2,1,0:T(8,128)S(1)}, f32[2,128,256]{2,1,0:T(8,128)S(1)}) custom-call(s32[3]{0:T(128)S(1)} %pad_add_fusion.ids, s32[6,23]{1,0:T(8,128)S(1)} %get-tuple-element.112.table, f32[4,12,32,256]{3,2,1,0:T(8,128)S(1)} %copy-done.3, ...), custom_call_target="tpu_custom_call", output_to_operand_aliasing={{0}: (7, {})} | custom-call | flops 1 | bytes 1 | tf_op jit(solution)/shard_map/finish/pallas_call | solution.py:295
  216.6 3.1 %collective-permute-start.63 = (f32[2,32,256]{2,1,0:T(8,128)S(1)}, f32[2,32,256]{2,1,0:T(8,128)S(1)}, u32[]{:S(2)}, u32[]{:S(2)}) collective-permute-start(f32[2,32,256]{2,1,0:T(8,128)S(1)} %add_add_fusion.3), channel_id=1, source_target_pairs={{0,2},{1,3},{2,0},{3,1},{4,6},{5,7},{6,4},{7,5},{8,10},{9,11},{10,... | collective-permute-start | bytes 196616 | tf_op jit(solution)/shard_map/ppermute | solution.py:206
  219.9 3.4 %collective-permute-done.64 = f32[2,32,256]{2,1,0:T(8,128)S(1)} collective-permute-done((f32[2,32,256]{2,1,0:T(8,128)S(1)}, f32[2,32,256]{2,1,0:T(8,128)S(1)}, u32[]{:S(2)}, u32[]{:S(2)}) %collective-permute-start.64) | collective-permute-done | bytes 65568 | tf_op jit(solution)/shard_map/ppermute | solution.py:206
  (241 shorter events, 117.8 us)
Async XLA Ops:
  30.0 25.1 %collective-permute-start.9 = (f32[4,12,8,256]{3,2,1,0:T(8,128)S(1)}, f32[4,12,8,256]{3,2,1,0:T(8,128)S(1)}, u32[]{:S(2)}, u32[]{:S(2)}) collective-permute-start(f32[4,12,8,256]{3,2,1,0:T(8,128)S(1)} %pad_maximum_fusion.rest_0_), channel_id=1, source_target_pairs={{0,8},{8,0},{16,24},{24,16},{1,9},{9,1},{17,25},{25,17},{2,10},{10... | collective-permute-start | bytes 1179656 | tf_op jit(solution)/shard_map/ppermute | solution.py:203
  31.9 23.2 %collective-permute-start.10 = (f32[4,12,8,256]{3,2,1,0:T(8,128)S(1)}, f32[4,12,8,256]{3,2,1,0:T(8,128)S(1)}, u32[]{:S(2)}, u32[]{:S(2)}) collective-permute-start(f32[4,12,8,256]{3,2,1,0:T(8,128)S(1)} %pad_maximum_fusion.rest_0_), channel_id=1, source_target_pairs={{0,16},{8,24},{16,0},{24,8},{1,17},{9,25},{17,1},{25,9},{2,18},{10... | collective-permute-start | bytes 1179656 | tf_op jit(solution)/shard_map/ppermute | solution.py:203
  32.8 22.3 %collective-permute-start.11 = (f32[4,12,8,256]{3,2,1,0:T(8,128)S(1)}, f32[4,12,8,256]{3,2,1,0:T(8,128)S(1)}, u32[]{:S(2)}, u32[]{:S(2)}) collective-permute-start(f32[4,12,8,256]{3,2,1,0:T(8,128)S(1)} %pad_maximum_fusion.rest_0_), channel_id=1, source_target_pairs={{0,24},{8,16},{16,8},{24,0},{1,25},{9,17},{17,9},{25,1},{2,26},{10... | collective-permute-start | bytes 1179656 | tf_op jit(solution)/shard_map/ppermute | solution.py:203
  61.7 21.6 %collective-permute-start.22 = (f32[4,12,8,256]{3,2,1,0:T(8,128)S(1)}, f32[4,12,8,256]{3,2,1,0:T(8,128)}, u32[]{:S(2)}, u32[]{:S(2)}) collective-permute-start(f32[4,12,8,256]{3,2,1,0:T(8,128)S(1)} %pad_maximum_fusion.1.rest_0_), channel_id=1, source_target_pairs={{0,8},{8,0},{16,24},{24,16},{1,9},{9,1},{17,25},{25,17},{2,10},{10... | collective-permute-start | bytes 1179656 | tf_op jit(solution)/shard_map/ppermute | solution.py:203
  63.8 19.4 %collective-permute-start.23 = (f32[4,12,8,256]{3,2,1,0:T(8,128)S(1)}, f32[4,12,8,256]{3,2,1,0:T(8,128)}, u32[]{:S(2)}, u32[]{:S(2)}) collective-permute-start(f32[4,12,8,256]{3,2,1,0:T(8,128)S(1)} %pad_maximum_fusion.1.rest_0_), channel_id=1, source_target_pairs={{0,16},{8,24},{16,0},{24,8},{1,17},{9,25},{17,1},{25,9},{2,18},{10... | collective-permute-start | bytes 1179656 | tf_op jit(solution)/shard_map/ppermute | solution.py:203
  64.0 19.2 %collective-permute-start.24 = (f32[4,12,8,256]{3,2,1,0:T(8,128)S(1)}, f32[4,12,8,256]{3,2,1,0:T(8,128)S(1)}, u32[]{:S(2)}, u32[]{:S(2)}) collective-permute-start(f32[4,12,8,256]{3,2,1,0:T(8,128)S(1)} %pad_maximum_fusion.1.rest_0_), channel_id=1, source_target_pairs={{0,24},{8,16},{16,8},{24,0},{1,25},{9,17},{17,9},{25,1},{2,26},{10... | collective-permute-start | bytes 1179656 | tf_op jit(solution)/shard_map/ppermute | solution.py:203
  65.4 17.8 %collective-permute-start.26 = (f32[12,8,256]{2,1,0:T(8,128)S(1)}, f32[12,8,256]{2,1,0:T(8,128)S(1)}, u32[]{:S(2)}, u32[]{:S(2)}) collective-permute-start(f32[12,8,256]{2,1,0:T(8,128)S(1)} %get-tuple-element.233), channel_id=1, source_target_pairs={{0,4},{1,5},{2,6},{3,7},{4,0},{5,1},{6,2},{7,3},{8,12},{9,13},{10,... | collective-permute-start | bytes 294920 | tf_op jit(solution)/shard_map/ppermute | solution.py:206
  67.6 15.6 %collective-permute-start.27 = (f32[12,8,256]{2,1,0:T(8,128)S(1)}, f32[12,8,256]{2,1,0:T(8,128)S(1)}, u32[]{:S(2)}, u32[]{:S(2)}) collective-permute-start(f32[12,8,256]{2,1,0:T(8,128)S(1)} %get-tuple-element.232), channel_id=1, source_target_pairs={{0,6},{1,7},{2,4},{3,5},{4,2},{5,3},{6,0},{7,1},{8,14},{9,15},{10,... | collective-permute-start | bytes 294920 | tf_op jit(solution)/shard_map/ppermute | solution.py:206
  91.1 21.5 %collective-permute-start.29 = (f32[2,12,32,256]{3,2,1,0:T(8,128)S(1)}, f32[2,12,32,256]{3,2,1,0:T(8,128)S(1)}, u32[]{:S(2)}, u32[]{:S(2)}) collective-permute-start(f32[2,12,32,256]{3,2,1,0:T(8,128)S(1)} %dynamic-slice_bitcast_fusion.2), channel_id=1, source_target_pairs={{0,2},{1,3},{2,0},{3,1},{4,6},{5,7},{6,4},{7,5},{8,10},{9,11},{10,... | collective-permute-start | bytes 2359304 | tf_op jit(solution)/shard_map/ppermute | solution.py:206
  92.8 12.0 %collective-permute-start.34 = (f32[4,12,8,256]{3,2,1,0:T(8,128)S(1)}, f32[4,12,8,256]{3,2,1,0:T(8,128)S(1)}, u32[]{:S(2)}, u32[]{:S(2)}) collective-permute-start(f32[4,12,8,256]{3,2,1,0:T(8,128)S(1)} %pad_maximum_fusion.2.rest_0_), channel_id=1, source_target_pairs={{0,8},{8,0},{16,24},{24,16},{1,9},{9,1},{17,25},{25,17},{2,10},{10... | collective-permute-start | bytes 1179656 | tf_op jit(solution)/shard_map/ppermute | solution.py:203
  92.9 19.8 %collective-permute-start.35 = (f32[4,12,8,256]{3,2,1,0:T(8,128)S(1)}, f32[4,12,8,256]{3,2,1,0:T(8,128)}, u32[]{:S(2)}, u32[]{:S(2)}) collective-permute-start(f32[4,12,8,256]{3,2,1,0:T(8,128)S(1)} %pad_maximum_fusion.2.rest_0_), channel_id=1, source_target_pairs={{0,16},{8,24},{16,0},{24,8},{1,17},{9,25},{17,1},{25,9},{2,18},{10... | collective-permute-start | bytes 1179656 | tf_op jit(solution)/shard_map/ppermute | solution.py:203
  93.8 18.8 %collective-permute-start.36 = (f32[4,12,8,256]{3,2,1,0:T(8,128)S(1)}, f32[4,12,8,256]{3,2,1,0:T(8,128)}, u32[]{:S(2)}, u32[]{:S(2)}) collective-permute-start(f32[4,12,8,256]{3,2,1,0:T(8,128)S(1)} %pad_maximum_fusion.2.rest_0_), channel_id=1, source_target_pairs={{0,24},{8,16},{16,8},{24,0},{1,25},{9,17},{17,9},{25,1},{2,26},{10... | collective-permute-start | bytes 1179656 | tf_op jit(solution)/shard_map/ppermute | solution.py:203
  118.1 28.3 %collective-permute-start.39 = (f32[2,12,32,256]{3,2,1,0:T(8,128)}, f32[2,12,32,256]{3,2,1,0:T(8,128)}, u32[]{:S(2)}, u32[]{:S(2)}) collective-permute-start(f32[2,12,32,256]{3,2,1,0:T(8,128)} %dynamic-slice_bitcast_fusion.1), channel_id=1, source_target_pairs={{0,2},{1,3},{2,0},{3,1},{4,6},{5,7},{6,4},{7,5},{8,10},{9,11},{10,... | collective-permute-start | bytes 2359304 | tf_op jit(solution)/shard_map/ppermute | solution.py:206
  120.6 24.2 %collective-permute-start.37 = (f32[1,12,32,256]{3,2,1,0:T(8,128)S(1)}, f32[1,12,32,256]{3,2,1,0:T(8,128)S(1)}, u32[]{:S(2)}, u32[]{:S(2)}) collective-permute-start(f32[1,12,32,256]{3,2,1,0:T(8,128)S(1)} %bitcast_add_fusion.2), channel_id=1, source_target_pairs={{0,4},{1,5},{2,6},{3,7},{4,0},{5,1},{6,2},{7,3},{8,12},{9,13},{10,... | collective-permute-start | bytes 1179656 | tf_op jit(solution)/shard_map/ppermute | solution.py:206
  152.8 36.9 %collective-permute-start.46 = (f32[2,12,32,256]{3,2,1,0:T(8,128)}, f32[2,12,32,256]{3,2,1,0:T(8,128)}, u32[]{:S(2)}, u32[]{:S(2)}) collective-permute-start(f32[2,12,32,256]{3,2,1,0:T(8,128)} %dynamic-slice_bitcast_fusion), channel_id=1, source_target_pairs={{0,2},{1,3},{2,0},{3,1},{4,6},{5,7},{6,4},{7,5},{8,10},{9,11},{10,... | collective-permute-start | bytes 2359304 | tf_op jit(solution)/shard_map/ppermute | solution.py:206
  159.9 29.9 %collective-permute-start.44 = (f32[1,12,32,256]{3,2,1,0:T(8,128)S(1)}, f32[1,12,32,256]{3,2,1,0:T(8,128)S(1)}, u32[]{:S(2)}, u32[]{:S(2)}) collective-permute-start(f32[1,12,32,256]{3,2,1,0:T(8,128)S(1)} %bitcast_add_fusion.1), channel_id=1, source_target_pairs={{0,4},{1,5},{2,6},{3,7},{4,0},{5,1},{6,2},{7,3},{8,12},{9,13},{10,... | collective-permute-start | bytes 1179656 | tf_op jit(solution)/shard_map/ppermute | solution.py:206
  162.2 20.0 %collective-permute-start.53 = (f32[2,32,256]{2,1,0:T(8,128)S(1)}, f32[2,32,256]{2,1,0:T(8,128)S(1)}, u32[]{:S(2)}, u32[]{:S(2)}) collective-permute-start(f32[2,32,256]{2,1,0:T(8,128)S(1)} %add_add_fusion.5), channel_id=1, source_target_pairs={{0,4},{1,5},{2,6},{3,7},{4,0},{5,1},{6,2},{7,3},{8,12},{9,13},{10,... | collective-permute-start | bytes 196616 | tf_op jit(solution)/shard_map/ppermute | solution.py:206
  163.5 22.1 %collective-permute-start.54 = (f32[2,32,256]{2,1,0:T(8,128)S(1)}, f32[2,32,256]{2,1,0:T(8,128)S(1)}, u32[]{:S(2)}, u32[]{:S(2)}) collective-permute-start(f32[2,32,256]{2,1,0:T(8,128)S(1)} %add_add_fusion.5), channel_id=1, source_target_pairs={{0,6},{1,7},{2,4},{3,5},{4,2},{5,3},{6,0},{7,1},{8,14},{9,15},{10,... | collective-permute-start | bytes 196616 | tf_op jit(solution)/shard_map/ppermute | solution.py:206
  165.6 20.0 %collective-permute-start.52 = (f32[2,32,256]{2,1,0:T(8,128)S(1)}, f32[2,32,256]{2,1,0:T(8,128)S(1)}, u32[]{:S(2)}, u32[]{:S(2)}) collective-permute-start(f32[2,32,256]{2,1,0:T(8,128)S(1)} %add_add_fusion.5), channel_id=1, source_target_pairs={{0,2},{1,3},{2,0},{3,1},{4,6},{5,7},{6,4},{7,5},{8,10},{9,11},{10,... | collective-permute-start | bytes 196616 | tf_op jit(solution)/shard_map/ppermute | solution.py:206
  191.7 18.9 %collective-permute-start.47 = (f32[1,12,32,256]{3,2,1,0:T(8,128)}, f32[1,12,32,256]{3,2,1,0:T(8,128)S(1)}, u32[]{:S(2)}, u32[]{:S(2)}) collective-permute-start(f32[1,12,32,256]{3,2,1,0:T(8,128)} %bitcast_add_fusion), channel_id=1, source_target_pairs={{0,4},{1,5},{2,6},{3,7},{4,0},{5,1},{6,2},{7,3},{8,12},{9,13},{10,... | collective-permute-start | bytes 1179656 | tf_op jit(solution)/shard_map/ppermute | solution.py:206
  200.2 15.9 %collective-permute-start.61 = (f32[2,32,256]{2,1,0:T(8,128)S(1)}, f32[2,32,256]{2,1,0:T(8,128)S(1)}, u32[]{:S(2)}, u32[]{:S(2)}) collective-permute-start(f32[2,32,256]{2,1,0:T(8,128)S(1)} %get-tuple-element.265), channel_id=1, source_target_pairs={{0,16},{8,24},{16,0},{24,8},{1,17},{9,25},{17,1},{25,9},{2,18},{10... | collective-permute-start | bytes 196616 | tf_op jit(solution)/shard_map/ppermute | solution.py:203
  200.9 15.2 %collective-permute-start.62 = (f32[2,32,256]{2,1,0:T(8,128)S(1)}, f32[2,32,256]{2,1,0:T(8,128)S(1)}, u32[]{:S(2)}, u32[]{:S(2)}) collective-permute-start(f32[2,32,256]{2,1,0:T(8,128)S(1)} %get-tuple-element.264), channel_id=1, source_target_pairs={{0,24},{8,16},{16,8},{24,0},{1,25},{9,17},{17,9},{25,1},{2,26},{10... | collective-permute-start | bytes 196616 | tf_op jit(solution)/shard_map/ppermute | solution.py:203
  202.7 13.4 %collective-permute-start.60 = (f32[2,32,256]{2,1,0:T(8,128)S(1)}, f32[2,32,256]{2,1,0:T(8,128)S(1)}, u32[]{:S(2)}, u32[]{:S(2)}) collective-permute-start(f32[2,32,256]{2,1,0:T(8,128)S(1)} %get-tuple-element.263), channel_id=1, source_target_pairs={{0,8},{8,0},{16,24},{24,16},{1,9},{9,1},{17,25},{25,17},{2,10},{10... | collective-permute-start | bytes 196616 | tf_op jit(solution)/shard_map/ppermute | solution.py:203
  215.6 28.9 %collective-permute-start.58 = (f32[2,128,256]{2,1,0:T(8,128)S(1)}, f32[2,128,256]{2,1,0:T(8,128)S(1)}, u32[]{:S(2)}, u32[]{:S(2)}) collective-permute-start(f32[2,128,256]{2,1,0:T(8,128)S(1)} %pad_maximum_fusion.3), channel_id=1, source_target_pairs={{0,1},{1,0},{2,3},{3,2},{4,5},{5,4},{6,7},{7,6},{8,9},{9,8},{10,11... | collective-permute-start | bytes 786440 | tf_op jit(solution)/shard_map/ppermute | solution.py:209
  (84 other events, 565.0 us)

commit v2 on v1

v2 whole, which is shorter than its diff:
```python
import functools

import jax
import jax.numpy as jnp
from jax import lax
from jax.experimental import pallas as pl
from jax.experimental.pallas import tpu as pltpu
from jax.sharding import PartitionSpec as P

CAP = 6
BATCHES = (2, 2, 2)
F32 = jnp.float32
BF16 = jnp.bfloat16
VMEM_LIMIT = 60 * 1024 * 1024
PRODUCT_VMEM = 56 * 1024 * 1024

COUNT, SLOT = 0, 1
RUN_COUNT, RUN_SLOT = SLOT + CAP + 1, SLOT + CAP + 2
PLACE = RUN_SLOT + CAP + 1


def split(x):
    high = x.astype(BF16)
    return high, (x - high.astype(F32)).astype(BF16)


def dot3(a, b, dims):
    dot = functools.partial(lax.dot_general, dimension_numbers=(dims, ((), ())), preferred_element_type=F32)
    return dot(a[0], b[1]) + dot(a[1], b[0]) + dot(a[0], b[0])


def prepare_kernel(n, g, groups, ids, structure, block_slot, panel, dinv, table, packed, *rest):
    pieces, gathered = rest[:-1], rest[-1]
    r, z, c = ids[0], ids[1], ids[2]
    node_count, slot_count, sub, width = panel.shape
    piece = sub // n
    place = [(b, i) for b, count in enumerate(groups) for i in range(count)]
    for s in range(node_count):
        row_bits = jnp.int32(0)
        col_bits = jnp.int32(0)
        for k in range(structure.shape[1]):
            slot = block_slot[structure[s, k]]
            for which in range(2):
                at = slot - (r, z)[which] * slot_count
                inside = (at >= 0) & (at < slot_count)
                bit = jnp.where(inside, jnp.left_shift(jnp.int32(1), jnp.where(inside, at, 0)), 0)
                if which == 0:
                    row_bits = row_bits | bit
                else:
                    col_bits = col_bits | bit
        counts = []
        for bits, first in ((row_bits, SLOT), (col_bits, RUN_SLOT)):
            for k in range(CAP + 1):
                table[s, first + k] = 0
            count = jnp.int32(0)
            for q in range(slot_count):
                bit = (bits >> q) & 1
                table[s, first + jnp.minimum(count, CAP)] = q
                if first == SLOT:
                    table[s, PLACE + q] = jnp.where(bit == 1, count, -1)
                count = count + bit
            table[s, first - 1] = count
            counts.append(count)
        count = counts[0]
        for k in range(CAP):
            gathered[pl.ds(k * sub, sub), :] = jnp.where(k < count, panel[s, table[s, SLOT + k]], 0.0)
        rows = dot3(split(gathered[...]), split(dinv[s]), ((1,), (0,))).reshape(CAP, sub, width)
        packed[s] = rows
        b, i = place[s]
        for k in range(n):
            part = rows[:, :piece]
            for j in range(1, n):
                part = jnp.where((r ^ k) == j, rows[:, j * piece : (j + 1) * piece], part)
            pieces[b * n + k][pl.ds(i * CAP, CAP)] = part


def product_kernel(n, g, start, ids, table, *rest):
    sources, parts, (keep, send) = rest[:g], rest[g : g + n * g], rest[g + n * g : g + n * g + 2]
    blocks, run, acc, sems, run_sems = rest[g + n * g + 2 :]
    r, z, c = ids[0], ids[1], ids[2]
    node_count = blocks.shape[0]
    sub = blocks.shape[-2]
    width = acc.shape[-1]
    col_slots = sources[0].shape[-1] // width
    tall = n * sub

    def copy(i, j, k, which):
        slot = table[start + i, RUN_SLOT + j]
        cols = pl.ds(pl.multiple_of((slot % col_slots) * width, width), width)
        q = table[start + i, SLOT + k]
        source = sources[0].at[q, :, c, :, cols] if which == 0 else sources[which].at[q, :, :, cols]
        return pltpu.make_async_copy(source, blocks.at[i, j, k], sems.at[i, j, k])

    def begin(i, j, k):
        owner = table[start + i, RUN_SLOT + j] // col_slots
        for which in range(g):

            @pl.when((c ^ owner) == which)
            def _():
                copy(i, j, k, which).start()

    pieces = [
        pltpu.make_async_copy(parts[jk * g + kc], run.at[:, c ^ kc, r ^ jk], run_sems.at[jk * g + kc])
        for jk in range(n)
        for kc in range(g)
    ]
    for piece in pieces:
        piece.start()
    for i in range(node_count):

        def column_blocks(j, _):
            lax.fori_loop(0, table[start + i, COUNT], lambda k, _: begin(i, j, k), None)

        lax.fori_loop(0, table[start + i, RUN_COUNT], column_blocks, None)
    for piece in pieces:
        piece.wait()

    for i in range(node_count):
        rows, columns = table[start + i, COUNT], table[start + i, RUN_COUNT]

        def column(j, _):
            high, low = split(run[:, :, :, i * CAP + j].reshape(width, width))
            right = jnp.concatenate([high, high, low], axis=0)
            lax.fori_loop(0, rows, lambda k, _: copy(i, j, k, 0).wait(), None)
            for few, many in ((0, 2), (2, 4), (4, CAP)):

                @pl.when((rows > few) & (rows <= many))
                def _():
                    high, low = split(blocks[i, j, :many].reshape(many * tall, width))
                    left = jnp.concatenate([high, low, high], axis=1)
                    value = jnp.dot(left, right, preferred_element_type=F32)
                    at = pl.ds(0, many * tall)
                    acc[at] = jnp.where(j == 0, value, acc[at] + value)

        lax.fori_loop(0, columns, column, None)
        for k in range(CAP):
            live = (k < rows) & (columns > 0)
            for h in range(n // 2):
                even, odd = [
                    jnp.where(live, acc[pl.ds((k * n + 2 * h + bit) * sub, sub)], 0.0) for bit in range(2)
                ]
                keep[h, i * CAP + k] = jnp.where((z & 1) == 0, even, odd)
                send[h, i * CAP + k] = jnp.where((z & 1) == 0, odd, even)


def finish_kernel(g, halvings, start, ids, table, base, *rest):
    received, packed, dinv = rest[:halvings], rest[halvings], rest[halvings + 1]
    off, diags, product = rest[-g - 2], rest[-g - 1 : -1], rest[-1]
    c = ids[2]
    s = start + pl.program_id(0)
    slot_count, sub, width = off.shape[1:]
    total = base[0]
    for more in received:
        total = total + more[0]
    product[...] = total
    for q in range(slot_count):
        at = table[s, PLACE + q]
        block = product[jnp.maximum(at, 0)]
        off[0, q] = jnp.where(at >= 0, -block, 0.0)
    mine = packed[0].reshape(CAP * sub, width)
    dims = ((0,), (0,))
    diag = dot3(split(mine), split(product[...].reshape(CAP * sub, width)), dims)

    def store(value):
        half = width // g
        for kc in range(g):
            part = value[:half]
            for j in range(1, g):
                part = jnp.where((c ^ kc) == j, value[j * half : (j + 1) * half], part)
            diags[kc][0] = part

    store(diag)

    @pl.when((ids[0] == 0) & (ids[1] == 0) & (c == 0))
    def _():
        factor = split(dinv[0])
        store(diag + dot3(factor, factor, dims))


def tree_sum(terms):
    while len(terms) > 1:
        terms = [terms[i] + terms[i + 1] for i in range(0, len(terms), 2)]
    return terms[0]


def pick(arrays, index):
    value = arrays[0]
    for k in range(1, len(arrays)):
        value = jnp.where(index == k, arrays[k], value)
    return value


def after(x):
    return lax.optimization_barrier(x)


def body(ancestor, panel, dinv, structure, block_slot):
    n = lax.axis_size("row")
    g = lax.axis_size("col") // n
    r = lax.axis_index("row")
    col = lax.axis_index("col")
    z, c = col // g, col % g
    node_count, slot_count, sub, width = panel.shape
    col_slots = slot_count // g
    piece = sub // n
    ids = jnp.stack([r, z, c]).astype(jnp.int32)
    table_width = PLACE + slot_count
    batches = BATCHES
    groups = (batches[0], sum(batches[1:]))
    smem = pl.BlockSpec(memory_space=pltpu.SMEM)
    vmem = pl.BlockSpec(memory_space=pltpu.VMEM)
    params = pltpu.CompilerParams(vmem_limit_bytes=VMEM_LIMIT)

    def along_row(x, k):
        return lax.ppermute(x, "row", [(i, i ^ k) for i in range(n)])

    def along_z(x, m):
        return lax.ppermute(x, "col", [(i * g + j, (i ^ m) * g + j) for i in range(n) for j in range(g)])

    def along_core(x, k):
        return lax.ppermute(x, "col", [(i * g + j, i * g + (j ^ k)) for i in range(n) for j in range(g)])

    out = pl.pallas_call(
        functools.partial(prepare_kernel, n, g, groups),
        out_shape=[
            jax.ShapeDtypeStruct((node_count, table_width), jnp.int32),
            jax.ShapeDtypeStruct((node_count, CAP, sub, width), F32),
        ]
        + [jax.ShapeDtypeStruct((count * CAP, piece, width), F32) for count in groups for _ in range(n)],
        in_specs=[smem, smem, smem, vmem, vmem],
        out_specs=[smem] + [vmem] * (1 + n * len(groups)),
        scratch_shapes=[pltpu.VMEM((CAP * sub, width), F32)],
        compiler_params=params,
        name="prepare",
    )(ids, structure, block_slot, panel, dinv)
    table, packed, pieces = out[0], out[1], out[2:]

    starts = [sum(batches[:b]) for b in range(len(batches))]
    halvings = n.bit_length() - 1

    def nothing_before(b, held):
        return held

    def spread_stage(b, own):
        return [own[0]] + [along_row(own[k], k) for k in range(1, n)]

    def before_cross(b, spread):
        return [pick(spread, r ^ z ^ m) for m in range(n)]

    def cross_stage(b, got):
        return [got[0]] + [along_z(got[m], m) for m in range(1, n)]

    def before_plane(b, got):
        return [jnp.stack([pick(got, z ^ i) for i in range(n)])]

    def plane_stage(b, run):
        return run + [along_row(run[0], k) for k in range(1, n)]

    def product_stage(b, plane):
        start, count = starts[b], batches[b]
        total = count * CAP
        parts = [x if k == 0 else along_core(x, k) for x in plane for k in range(g)]
        return pl.pallas_call(
            functools.partial(product_kernel, n, g, start),
            out_shape=[jax.ShapeDtypeStruct((n // 2, total, sub, width), F32)] * 2,
            in_specs=[smem, smem] + [pl.BlockSpec(memory_space=pltpu.HBM)] * (g + n * g),
            out_specs=[vmem] * 2,
            scratch_shapes=[
                pltpu.VMEM((count, CAP, CAP, n, sub, width), F32),
                pltpu.VMEM((n, g, n, total, piece, width), F32),
                pltpu.VMEM((CAP * n * sub, width), F32),
                pltpu.SemaphoreType.DMA((count, CAP, CAP)),
                pltpu.SemaphoreType.DMA((n * g,)),
            ],
            compiler_params=pltpu.CompilerParams(vmem_limit_bytes=PRODUCT_VMEM),
            cost_estimate=pl.CostEstimate(flops=1, bytes_accessed=1, transcendentals=0),
            name="product",
        )(ids, table, blocks, *shared, *parts)

    levels = [1] + list(range(1, halvings + 1))

    def before_halving(i, b, held):
        if i == 0:
            return held
        high, bit = n >> (i + 1), (z >> i) & 1
        send = None
        for level, array in zip(levels, held):
            inner = 1 << (i - level)
            split_up = array.reshape((high, 2, inner) + array.shape[1:])
            start_at = (0, 1 - bit, (z >> level) & (inner - 1)) + (0,) * (array.ndim - 1)
            part = lax.dynamic_slice(split_up, start_at, (high, 1, 1) + array.shape[1:])
            part = part.reshape((high,) + array.shape[1:])
            send = part if send is None else send + part
        return list(held) + [send]

    def halving_stage(i, b, held):
        return list(held[:-1]) + [along_z(held[-1], 1 << i)]

    stages = [
        (before_plane, plane_stage),
        (nothing_before, product_stage),
    ]
    stages += [(functools.partial(before_halving, i), functools.partial(halving_stage, i)) for i in range(halvings)]
    state = [[] for _ in batches]
    cross_stages = [(nothing_before, spread_stage), (before_cross, cross_stage)]
    crossing = [list(pieces[:n]), list(pieces[n:])]
    blocks = ancestor.reshape(slot_count, n, g, sub, col_slots * width)
    shared = [blocks] * (g - 1)
    half = width // g
    quarter = half // n

    def plane_diag(shares):
        share = shares[0]
        for k in range(1, g):
            share = share + along_core(shares[k], k)
        cut = [lax.dynamic_slice_in_dim(share, (r ^ k) * quarter, quarter, 1) for k in range(n)]
        return tree_sum([cut[0]] + [along_row(cut[k], k) for k in range(1, n)])

    def whole_diag(part):
        part = tree_sum([part] + [along_z(part, m) for m in range(1, n)])
        parts = [part] + [along_row(part, k) for k in range(1, n)]
        mine = jnp.concatenate([pick(parts, r ^ j) for j in range(n)], axis=1)
        halves = [mine] + [along_core(mine, k) for k in range(1, g)]
        return jnp.concatenate([pick(halves, c ^ j) for j in range(g)], axis=1)

    off, first_diag = None, None
    last = len(batches) - 1
    for phase in range(2 + len(stages) + last + 1):
        done = phase - 2 - len(stages)
        now = [(b, phase - 2 - b) for b in range(last + 1) if 0 <= phase - 2 - b < len(stages)]
        now_crossing = [(group, phase - group) for group in range(2) if 0 <= phase - group < 2]
        for b, stage in now:
            if stage == 0:
                at = 0 if b == 0 else (starts[b] - batches[0]) * CAP
                state[b] = [array[at : at + batches[b] * CAP] for array in crossing[min(b, 1)]]
            state[b] = stages[stage][0](b, state[b])
        for group, stage in now_crossing:
            crossing[group] = cross_stages[stage][0](group, crossing[group])
        if done < last:
            state, crossing, shared = after((state, crossing, shared))
        for b, stage in now:
            state[b] = stages[stage][1](b, state[b])
        for group, stage in now_crossing:
            crossing[group] = cross_stages[stage][1](group, crossing[group])
        if phase == 0:
            shared = [lax.dynamic_index_in_dim(shared[k - 1], c ^ k, 2, keepdims=False) for k in range(1, g)]
        elif phase == 1:
            shared = [along_core(shared[k - 1], k) for k in range(1, g)]
        if done < 0:
            state, crossing, shared = after((state, crossing, shared))
            continue
        start, count = starts[done], batches[done]
        of_node = lambda i, ids, table, start=start: (start + i, 0, 0, 0)
        of_dest = lambda level: lambda i, ids, table: (ids[1] >> level, i, 0, 0)
        result = pl.pallas_call(
            functools.partial(finish_kernel, g, halvings, start),
            out_shape=[jax.ShapeDtypeStruct((node_count, slot_count, sub, width), F32)]
            + [jax.ShapeDtypeStruct((count, half, width), F32)] * g,
            grid_spec=pltpu.PrefetchScalarGridSpec(
                num_scalar_prefetch=2,
                grid=(count,),
                in_specs=[pl.BlockSpec((1, CAP, sub, width), of_dest(level)) for level in levels]
                + [
                    pl.BlockSpec((1, CAP, sub, width), of_node),
                    pl.BlockSpec((1, width, width), lambda i, ids, table, start=start: (start + i, 0, 0)),
                ]
                + [pl.BlockSpec(memory_space=pl.ANY)] * (off is not None),
                out_specs=[pl.BlockSpec((1, slot_count, sub, width), of_node)]
                + [pl.BlockSpec((1, half, width), lambda i, ids, table: (i, 0, 0))] * g,
                scratch_shapes=[pltpu.VMEM((CAP, sub, width), F32)],
            ),
            input_output_aliases={} if off is None else {5 + halvings: 0},
            compiler_params=params,
            cost_estimate=pl.CostEstimate(flops=1, bytes_accessed=1, transcendentals=0),
            name="finish",
        )(ids, table, *state[done], packed, dinv, *([] if off is None else [off]))
        off, state[done] = result[0], result[1:]
        if done < last - 1:
            state = after(state)
        elif done == last - 1:
            first_diag = plane_diag([jnp.concatenate([held[k] for held in state[:last]]) for k in range(g)])
            state[last], first_diag = after((state[last], first_diag))
    diag = [whole_diag(first_diag)] if last else []
    return off, jnp.concatenate(diag + [whole_diag(plane_diag(state[last]))], axis=0)


def solution(mesh):
    in_specs = (P("row", "col"), P(None, "row", "col", None), P(), P(), P())
    out_specs = (P(None, "row", "col", None), P())
    return jax.shard_map(body, mesh=mesh, in_specs=in_specs, out_specs=out_specs, check_vma=False)
```

time: 249 us -> 223 us (0.90)
  starting transfers between devices: 82.1 us -> 64.8 us
  waiting for transfers between devices: 90.5 us -> 96.8 us
  other arithmetic: 12.8 us -> 6.7 us
  local copies, waits for them, and re-layouts: 14 us -> 8.4 us
  Pallas kernels: 46.7 us -> 44.2 us
    ppermute x24 -> x18, waiting for transfers between devices: 50.4 us -> 70.2 us  [along_z(): lax.ppermute(x, 'col', [(i * g + j, (i ^ m) * g + j) for i in range(n) fo...]
    ppermute x36 -> x27, starting transfers between devices: 41.4 us -> 31.3 us  [along_row(): return lax.ppermute(x, 'row', [(i, i ^ k) for i in range(n)])]
    ppermute x21 -> x17, waiting for transfers between devices: 10.1 us -> 2.47 us  [along_core(): lax.ppermute(x, 'col', [(i * g + j, i * g + (j ^ k)) for i in range(n) fo...]
    pallas_call x3, Pallas kernels: 34.1 us -> 26.7 us  [product_stage(): pl.pallas_call(functools.partial(product_kernel, n, g, start), out_shape=...]
    unnamed x54 -> x78, local copies, waits for them, and re-layouts: 10.7 us -> 3.47 us
    ppermute x24 -> x18, starting transfers between devices: 36.7 us -> 30.5 us  [along_z(): lax.ppermute(x, 'col', [(i * g + j, (i ^ m) * g + j) for i in range(n) fo...]
    ppermute x36 -> x27, waiting for transfers between devices: 30 us -> 24.2 us  [along_row(): return lax.ppermute(x, 'row', [(i, i ^ k) for i in range(n)])]
    add x9 -> x5, other arithmetic: 8.29 us -> 3.03 us  [the longest x2 2 us: plane_diag(): share = share + along_core(shares[k], k)]
  transfers between devices with their start and end apart: 81 -> 62, of which waited for: 35 -> 28; matrix products, arithmetic and copies ran while one was open for 6% -> 3% of each run, Pallas kernels for 18% -> 14%
where the time goes in v2:
time: 223 us; the launch traced here: 222 us
  waiting for transfers between devices  96.8 us (43%)
  starting transfers between devices  64.8 us (29%)
  Pallas kernels  44.2 us (20%)
  local copies, waits for them, and re-layouts  8.4 us (4%)
  other arithmetic  6.7 us (3%)
    ppermute x18, waiting for transfers between devices, along_z(): lax.ppermute(x, 'col', [(i * g + j, (i ^ m) * g + j) for i in range(n) fo...  70.2 us
    ppermute x27, starting transfers between devices, along_row(): return lax.ppermute(x, 'row', [(i, i ^ k) for i in range(n)])  31.3 us
    ppermute x18, starting transfers between devices, along_z(): lax.ppermute(x, 'col', [(i * g + j, (i ^ m) * g + j) for i in range(n) fo...  30.5 us
    pallas_call x3, Pallas kernels, product_stage(): pl.pallas_call(functools.partial(product_kernel, n, g, start), out_shape=...  26.7 us
    ppermute x27, waiting for transfers between devices, along_row(): return lax.ppermute(x, 'row', [(i, i ^ k) for i in range(n)])  24.2 us
    pallas_call x3, Pallas kernels, body(): pl.pallas_call(functools.partial(finish_kernel, g, halvings, start), out_...  13.1 us
    squeeze x1, local copies, waits for them, and re-layouts, body(): lax.dynamic_index_in_dim(shared[k - 1], c ^ k, 2, keepdims=False)  4.87 us
  transfers between devices with their start and end apart: 62, of which 28 were waited for; matrix products, arithmetic and copies ran while one was open for 3% of the time, Pallas kernels for 14%

profile of v2, /device:TPU:0, one launch (start us, length us, event | category | flops | bytes accessed | tf_op | source)
XLA Modules:
  0.0 222.2 jit_solution(7856492368101451786)
XLA Ops:
  1.3 4.4 %prepare.1 = (s32[6,24]{1,0:T(8,128)}, f32[6,6,32,256]{3,2,1,0:T(8,128)}, f32[12,8,256]{2,1,0:T(8,128)}, f32[12,8,256]{2,1,0:T(8,128)}, f32[12,8,256]{2,1,0:T(8,...) custom-call(s32[3]{0:T(128)} %pad_add_fusion.ids, ...), custom_call_target="tpu_custom_call" | custom-call | tf_op jit(solution)/shard_map/prepare/pallas_call | solution.py:223
  5.7 3.0 %collective-permute-start = (f32[12,8,256]{2,1,0:T(8,128)}, f32[12,8,256]{2,1,0:T(8,128)S(1)}, u32[]{:S(2)}, u32[]{:S(2)}) collective-permute-start(f32[12,8,256]{2,1,0:T(8,128)} %get-tuple-element.170), channel_id=1, source_target_pairs={{0,8},{8,0},{16,24},{24,16},{1,9},{9,1},{17,25},{25,17},{2,10},{10... | collective-permute-start | bytes 294920 | tf_op jit(solution)/shard_map/ppermute | solution.py:215
  10.3 4.9 %dynamic-slice_bitcast_fusion = f32[8,4,32,1024]{3,2,1,0:T(8,128)} fusion(f32[8,4,2,32,1024]{4,3,2,1,0:T(8,128)} %bitcast.30, s32[]{:T(128)S(6)} %select_n.535), kind=kLoop, calls=%fused_computation | loop fusion | bytes 8388612 | tf_op jit(solution)/shard_map/jit(dynamic_index_in_dim)/squeeze | solution.py:346
  17.7 2.6 %collective-permute-start.4 = (f32[12,8,256]{2,1,0:T(8,128)S(1)}, f32[12,8,256]{2,1,0:T(8,128)S(1)}, u32[]{:S(2)}, u32[]{:S(2)}) collective-permute-start(f32[12,8,256]{2,1,0:T(8,128)S(1)} %get-tuple-element.189), channel_id=1, source_target_pairs={{0,4},{1,5},{2,6},{3,7},{4,0},{5,1},{6,2},{7,3},{8,12},{9,13},{10,... | collective-permute-start | bytes 294920 | tf_op jit(solution)/shard_map/ppermute | solution.py:218
  28.1 3.9 %collective-permute-done.5 = f32[12,8,256]{2,1,0:T(8,128)S(1)} collective-permute-done((f32[12,8,256]{2,1,0:T(8,128)S(1)}, f32[12,8,256]{2,1,0:T(8,128)S(1)}, u32[]{:S(2)}, u32[]{:S(2)}) %collective-permute-start.5) | collective-permute-done | bytes 98336 | tf_op jit(solution)/shard_map/ppermute | solution.py:218
  36.3 2.6 %collective-permute-start.14 = (f32[24,8,256]{2,1,0:T(8,128)S(1)}, f32[24,8,256]{2,1,0:T(8,128)S(1)}, u32[]{:S(2)}, u32[]{:S(2)}) collective-permute-start(f32[24,8,256]{2,1,0:T(8,128)S(1)} %get-tuple-element.208), channel_id=1, source_target_pairs={{0,4},{1,5},{2,6},{3,7},{4,0},{5,1},{6,2},{7,3},{8,12},{9,13},{10,... | collective-permute-start | bytes 589832 | tf_op jit(solution)/shard_map/ppermute | solution.py:218
  39.1 2.5 %collective-permute-start.15 = (f32[24,8,256]{2,1,0:T(8,128)S(1)}, f32[24,8,256]{2,1,0:T(8,128)S(1)}, u32[]{:S(2)}, u32[]{:S(2)}) collective-permute-start(f32[24,8,256]{2,1,0:T(8,128)S(1)} %get-tuple-element.209), channel_id=1, source_target_pairs={{0,6},{1,7},{2,4},{3,5},{4,2},{5,3},{6,0},{7,1},{8,14},{9,15},{10,... | collective-permute-start | bytes 589832 | tf_op jit(solution)/shard_map/ppermute | solution.py:218
  41.7 9.6 %collective-permute-done.14 = f32[24,8,256]{2,1,0:T(8,128)S(1)} collective-permute-done((f32[24,8,256]{2,1,0:T(8,128)S(1)}, f32[24,8,256]{2,1,0:T(8,128)S(1)}, u32[]{:S(2)}, u32[]{:S(2)}) %collective-permute-start.14) | collective-permute-done | bytes 196640 | tf_op jit(solution)/shard_map/ppermute | solution.py:218
  57.6 9.6 %product.3 = (f32[2,12,32,256]{3,2,1,0:T(8,128)}, f32[2,12,32,256]{3,2,1,0:T(8,128)}) custom-call(s32[3]{0:T(128)} %pad_add_fusion.ids, s32[6,24]{1,0:T(8,128)} %get-tuple-element.160.table, f32[8,4,2,32,1024]{4,3,2,1,0:T(8,128)} %bitcast.31, f32[8,4,32,1024]{3,2,1,0:T(8,128)} %collective-permute-done.9.rest_1_, f32[4,12,8,256]{3,2,1,0:T(8,128)} %copy-done.7, ...), custom_call_target="tpu_custom_call" | custom-call | flops 1 | bytes 1 | tf_op jit(solution)/shard_map/product/pallas_call | solution.py:263
  67.3 6.2 %collective-permute-done.21.rest_6_ = f32[4,12,8,256]{3,2,1,0:T(8,128)S(1)} collective-permute-done((f32[4,12,8,256]{3,2,1,0:T(8,128)S(1)}, f32[4,12,8,256]{3,2,1,0:T(8,128)S(1)}, u32[]{:S(2)}, u32[]{:S(2)}) %collective-permute-start.21) | collective-permute-done | bytes 393248 | tf_op jit(solution)/shard_map/ppermute | solution.py:215
  74.3 3.4 %collective-permute-start.23 = (f32[2,12,32,256]{3,2,1,0:T(8,128)}, f32[2,12,32,256]{3,2,1,0:T(8,128)S(1)}, u32[]{:S(2)}, u32[]{:S(2)}) collective-permute-start(f32[2,12,32,256]{3,2,1,0:T(8,128)} %get-tuple-element.244), channel_id=1, source_target_pairs={{0,2},{1,3},{2,0},{3,1},{4,6},{5,7},{6,4},{7,5},{8,10},{9,11},{10,... | collective-permute-start | bytes 2359304 | tf_op jit(solution)/shard_map/ppermute | solution.py:218
  82.2 8.9 %product.4 = (f32[2,12,32,256]{3,2,1,0:T(8,128)}, f32[2,12,32,256]{3,2,1,0:T(8,128)}) custom-call(s32[3]{0:T(128)} %pad_add_fusion.ids, s32[6,24]{1,0:T(8,128)} %get-tuple-element.160.table, f32[8,4,2,32,1024]{4,3,2,1,0:T(8,128)} %bitcast.32, f32[8,4,32,1024]{3,2,1,0:T(8,128)} %collective-permute-done.9.rest_1_, f32[4,12,8,256]{3,2,1,0:T(8,128)} %copy-done.6, ...), custom_call_target="tpu_custom_call" | custom-call | flops 1 | bytes 1 | tf_op jit(solution)/shard_map/product/pallas_call | solution.py:263
  91.1 7.3 %collective-permute-done.29.rest_6_ = f32[4,12,8,256]{3,2,1,0:T(8,128)S(1)} collective-permute-done((f32[4,12,8,256]{3,2,1,0:T(8,128)S(1)}, f32[4,12,8,256]{3,2,1,0:T(8,128)S(1)}, u32[]{:S(2)}, u32[]{:S(2)}) %collective-permute-start.29) | collective-permute-done | bytes 393248 | tf_op jit(solution)/shard_map/ppermute | solution.py:215
  103.3 8.1 %product.5 = (f32[2,12,32,256]{3,2,1,0:T(8,128)}, f32[2,12,32,256]{3,2,1,0:T(8,128)}) custom-call(s32[3]{0:T(128)} %pad_add_fusion.ids, s32[6,24]{1,0:T(8,128)} %get-tuple-element.160.table, f32[8,4,2,32,1024]{4,3,2,1,0:T(8,128)} %bitcast.33, f32[8,4,32,1024]{3,2,1,0:T(8,128)} %collective-permute-done.9.rest_1_, f32[4,12,8,256]{3,2,1,0:T(8,128)} %copy-done.8, ...), custom_call_target="tpu_custom_call" | custom-call | flops 1 | bytes 1 | tf_op jit(solution)/shard_map/product/pallas_call | solution.py:263
  111.4 14.1 %collective-permute-done.31.rest_1_ = f32[1,12,32,256]{3,2,1,0:T(8,128)S(1)} collective-permute-done((f32[1,12,32,256]{3,2,1,0:T(8,128)S(1)}, f32[1,12,32,256]{3,2,1,0:T(8,128)S(1)}, u32[]{:S(2)}, u32[]{:S(2)}) %collective-permute-start.31) | collective-permute-done | bytes 393248 | tf_op jit(solution)/shard_map/ppermute | solution.py:218
  130.4 4.4 %finish.3 = (f32[6,8,32,256]{3,2,1,0:T(8,128)}, f32[2,128,256]{2,1,0:T(8,128)}, f32[2,128,256]{2,1,0:T(8,128)}) custom-call(s32[3]{0:T(128)} %pad_add_fusion.ids, s32[6,24]{1,0:T(8,128)} %get-tuple-element.160.table, f32[2,12,32,256]{3,2,1,0:T(8,128)} %get-tuple-element.281.base, f32[2,12,32,256]{3,2,1,0:T(8,128)} %copy-done.2, ...), custom_call_target="tpu_custom_call" | custom-call | flops 1 | bytes 1 | tf_op jit(solution)/shard_map/finish/pallas_call | solution.py:355
  134.7 19.7 %collective-permute-done.37.rest_1_ = f32[1,12,32,256]{3,2,1,0:T(8,128)S(1)} collective-permute-done((f32[1,12,32,256]{3,2,1,0:T(8,128)}, f32[1,12,32,256]{3,2,1,0:T(8,128)S(1)}, u32[]{:S(2)}, u32[]{:S(2)}) %collective-permute-start.37) | collective-permute-done | bytes 393248 | tf_op jit(solution)/shard_map/ppermute | solution.py:218
  156.0 4.4 %finish.4 = (f32[6,8,32,256]{3,2,1,0:T(8,128)}, f32[2,128,256]{2,1,0:T(8,128)}, f32[2,128,256]{2,1,0:T(8,128)}) custom-call(s32[3]{0:T(128)} %pad_add_fusion.ids, s32[6,24]{1,0:T(8,128)} %get-tuple-element.160.table, f32[2,12,32,256]{3,2,1,0:T(8,128)} %get-tuple-element.303.base, f32[2,12,32,256]{3,2,1,0:T(8,128)} %copy-done.5, ...), custom_call_target="tpu_custom_call", output_to_operand_aliasing={{0}: (7, {})} | custom-call | flops 1 | bytes 1 | tf_op jit(solution)/shard_map/finish/pallas_call | solution.py:355
  168.1 4.6 %collective-permute-done.42 = f32[4,32,256]{2,1,0:T(8,128)S(1)} collective-permute-done((f32[4,32,256]{2,1,0:T(8,128)S(1)}, f32[4,32,256]{2,1,0:T(8,128)S(1)}, u32[]{:S(2)}, u32[]{:S(2)}) %collective-permute-start.42) | collective-permute-done | bytes 131104 | tf_op jit(solution)/shard_map/ppermute | solution.py:215
  174.2 8.2 %collective-permute-done.39.rest_1_ = f32[1,12,32,256]{3,2,1,0:T(8,128)S(1)} collective-permute-done((f32[1,12,32,256]{3,2,1,0:T(8,128)S(1)}, f32[1,12,32,256]{3,2,1,0:T(8,128)S(1)}, u32[]{:S(2)}, u32[]{:S(2)}) %collective-permute-start.39) | collective-permute-done | bytes 393248 | tf_op jit(solution)/shard_map/ppermute | solution.py:218
  183.1 4.3 %finish.5 = (f32[6,8,32,256]{3,2,1,0:T(8,128)}, f32[2,128,256]{2,1,0:T(8,128)}, f32[2,128,256]{2,1,0:T(8,128)}) custom-call(s32[3]{0:T(128)} %pad_add_fusion.ids, s32[6,24]{1,0:T(8,128)} %get-tuple-element.160.table, f32[2,12,32,256]{3,2,1,0:T(8,128)} %get-tuple-element.310.base, f32[2,12,32,256]{3,2,1,0:T(8,128)} %copy-done.3, ...), custom_call_target="tpu_custom_call", output_to_operand_aliasing={{0}: (7, {})} | custom-call | flops 1 | bytes 1 | tf_op jit(solution)/shard_map/finish/pallas_call | solution.py:355
  188.3 2.6 %collective-permute-start.44 = (f32[4,32,256]{2,1,0:T(8,128)S(1)}, f32[4,32,256]{2,1,0:T(8,128)S(1)}, u32[]{:S(2)}, u32[]{:S(2)}) collective-permute-start(f32[4,32,256]{2,1,0:T(8,128)S(1)} %add_add_fusion.1), channel_id=1, source_target_pairs={{0,2},{1,3},{2,0},{3,1},{4,6},{5,7},{6,4},{7,5},{8,10},{9,11},{10,... | collective-permute-start | bytes 393224 | tf_op jit(solution)/shard_map/ppermute | solution.py:218
  193.3 4.8 %collective-permute-done.45 = f32[4,32,256]{2,1,0:T(8,128)S(1)} collective-permute-done((f32[4,32,256]{2,1,0:T(8,128)S(1)}, f32[4,32,256]{2,1,0:T(8,128)S(1)}, u32[]{:S(2)}, u32[]{:S(2)}) %collective-permute-start.45) | collective-permute-done | bytes 131104 | tf_op jit(solution)/shard_map/ppermute | solution.py:218
  209.0 3.4 %collective-permute-done.57 = f32[2,32,256]{2,1,0:T(8,128)S(1)} collective-permute-done((f32[2,32,256]{2,1,0:T(8,128)S(1)}, f32[2,32,256]{2,1,0:T(8,128)S(1)}, u32[]{:S(2)}, u32[]{:S(2)}) %collective-permute-start.57) | collective-permute-done | bytes 65568 | tf_op jit(solution)/shard_map/ppermute | solution.py:218
  (216 shorter events, 73.2 us)
Async XLA Ops:
  16.0 16.1 %collective-permute-start.9 = (f32[8,4,32,1024]{3,2,1,0:T(8,128)}, f32[8,4,32,1024]{3,2,1,0:T(8,128)}, u32[]{:S(2)}, u32[]{:S(2)}) collective-permute-start(f32[8,4,32,1024]{3,2,1,0:T(8,128)} %dynamic-slice_bitcast_fusion), channel_id=1, source_target_pairs={{0,1},{1,0},{2,3},{3,2},{4,5},{5,4},{6,7},{7,6},{8,9},{9,8},{10,11... | collective-permute-start | bytes 12582920 | tf_op jit(solution)/shard_map/ppermute | solution.py:221
  20.3 11.7 %collective-permute-start.6 = (f32[24,8,256]{2,1,0:T(8,128)S(1)}, f32[24,8,256]{2,1,0:T(8,128)S(1)}, u32[]{:S(2)}, u32[]{:S(2)}) collective-permute-start(f32[24,8,256]{2,1,0:T(8,128)S(1)} %copy-done.38), channel_id=1, source_target_pairs={{0,8},{8,0},{16,24},{24,16},{1,9},{9,1},{17,25},{25,17},{2,10},{10... | collective-permute-start | bytes 589832 | tf_op jit(solution)/shard_map/ppermute | solution.py:215
  21.5 10.6 %collective-permute-start.7 = (f32[24,8,256]{2,1,0:T(8,128)S(1)}, f32[24,8,256]{2,1,0:T(8,128)S(1)}, u32[]{:S(2)}, u32[]{:S(2)}) collective-permute-start(f32[24,8,256]{2,1,0:T(8,128)S(1)} %copy-done.37), channel_id=1, source_target_pairs={{0,16},{8,24},{16,0},{24,8},{1,17},{9,25},{17,1},{25,9},{2,18},{10... | collective-permute-start | bytes 589832 | tf_op jit(solution)/shard_map/ppermute | solution.py:215
  32.9 18.5 %collective-permute-start.10 = (f32[4,12,8,256]{3,2,1,0:T(8,128)S(1)}, f32[4,12,8,256]{3,2,1,0:T(8,128)S(1)}, u32[]{:S(2)}, u32[]{:S(2)}) collective-permute-start(f32[4,12,8,256]{3,2,1,0:T(8,128)S(1)} %pad_maximum_fusion.2.rest_2_), channel_id=1, source_target_pairs={{0,8},{8,0},{16,24},{24,16},{1,9},{9,1},{17,25},{25,17},{2,10},{10... | collective-permute-start | bytes 1179656 | tf_op jit(solution)/shard_map/ppermute | solution.py:215
  34.1 17.9 %collective-permute-start.11 = (f32[4,12,8,256]{3,2,1,0:T(8,128)S(1)}, f32[4,12,8,256]{3,2,1,0:T(8,128)S(1)}, u32[]{:S(2)}, u32[]{:S(2)}) collective-permute-start(f32[4,12,8,256]{3,2,1,0:T(8,128)S(1)} %pad_maximum_fusion.2.rest_2_), channel_id=1, source_target_pairs={{0,16},{8,24},{16,0},{24,8},{1,17},{9,25},{17,1},{25,9},{2,18},{10... | collective-permute-start | bytes 1179656 | tf_op jit(solution)/shard_map/ppermute | solution.py:215
  35.1 16.9 %collective-permute-start.12 = (f32[4,12,8,256]{3,2,1,0:T(8,128)S(1)}, f32[4,12,8,256]{3,2,1,0:T(8,128)S(1)}, u32[]{:S(2)}, u32[]{:S(2)}) collective-permute-start(f32[4,12,8,256]{3,2,1,0:T(8,128)S(1)} %pad_maximum_fusion.2.rest_2_), channel_id=1, source_target_pairs={{0,24},{8,16},{16,8},{24,0},{1,25},{9,17},{17,9},{25,1},{2,26},{10... | collective-permute-start | bytes 1179656 | tf_op jit(solution)/shard_map/ppermute | solution.py:215
  36.3 15.0 %collective-permute-start.14 = (f32[24,8,256]{2,1,0:T(8,128)S(1)}, f32[24,8,256]{2,1,0:T(8,128)S(1)}, u32[]{:S(2)}, u32[]{:S(2)}) collective-permute-start(f32[24,8,256]{2,1,0:T(8,128)S(1)} %get-tuple-element.208), channel_id=1, source_target_pairs={{0,4},{1,5},{2,6},{3,7},{4,0},{5,1},{6,2},{7,3},{8,12},{9,13},{10,... | collective-permute-start | bytes 589832 | tf_op jit(solution)/shard_map/ppermute | solution.py:218
  39.1 12.2 %collective-permute-start.15 = (f32[24,8,256]{2,1,0:T(8,128)S(1)}, f32[24,8,256]{2,1,0:T(8,128)S(1)}, u32[]{:S(2)}, u32[]{:S(2)}) collective-permute-start(f32[24,8,256]{2,1,0:T(8,128)S(1)} %get-tuple-element.209), channel_id=1, source_target_pairs={{0,6},{1,7},{2,4},{3,5},{4,2},{5,3},{6,0},{7,1},{8,14},{9,15},{10,... | collective-permute-start | bytes 589832 | tf_op jit(solution)/shard_map/ppermute | solution.py:218
  53.2 14.1 %collective-permute-start.20 = (f32[4,12,8,256]{3,2,1,0:T(8,128)S(1)}, f32[4,12,8,256]{3,2,1,0:T(8,128)S(1)}, u32[]{:S(2)}, u32[]{:S(2)}) collective-permute-start(f32[4,12,8,256]{3,2,1,0:T(8,128)S(1)} %pad_maximum_fusion.3.rest_2_), channel_id=1, source_target_pairs={{0,8},{8,0},{16,24},{24,16},{1,9},{9,1},{17,25},{25,17},{2,10},{10... | collective-permute-start | bytes 1179656 | tf_op jit(solution)/shard_map/ppermute | solution.py:215
  54.1 19.4 %collective-permute-start.21 = (f32[4,12,8,256]{3,2,1,0:T(8,128)S(1)}, f32[4,12,8,256]{3,2,1,0:T(8,128)S(1)}, u32[]{:S(2)}, u32[]{:S(2)}) collective-permute-start(f32[4,12,8,256]{3,2,1,0:T(8,128)S(1)} %pad_maximum_fusion.3.rest_2_), channel_id=1, source_target_pairs={{0,16},{8,24},{16,0},{24,8},{1,17},{9,25},{17,1},{25,9},{2,18},{10... | collective-permute-start | bytes 1179656 | tf_op jit(solution)/shard_map/ppermute | solution.py:215
  55.3 18.2 %collective-permute-start.22 = (f32[4,12,8,256]{3,2,1,0:T(8,128)S(1)}, f32[4,12,8,256]{3,2,1,0:T(8,128)S(1)}, u32[]{:S(2)}, u32[]{:S(2)}) collective-permute-start(f32[4,12,8,256]{3,2,1,0:T(8,128)S(1)} %pad_maximum_fusion.3.rest_2_), channel_id=1, source_target_pairs={{0,24},{8,16},{16,8},{24,0},{1,25},{9,17},{17,9},{25,1},{2,26},{10... | collective-permute-start | bytes 1179656 | tf_op jit(solution)/shard_map/ppermute | solution.py:215
  74.3 24.2 %collective-permute-start.23 = (f32[2,12,32,256]{3,2,1,0:T(8,128)}, f32[2,12,32,256]{3,2,1,0:T(8,128)S(1)}, u32[]{:S(2)}, u32[]{:S(2)}) collective-permute-start(f32[2,12,32,256]{3,2,1,0:T(8,128)} %get-tuple-element.244), channel_id=1, source_target_pairs={{0,2},{1,3},{2,0},{3,1},{4,6},{5,7},{6,4},{7,5},{8,10},{9,11},{10,... | collective-permute-start | bytes 2359304 | tf_op jit(solution)/shard_map/ppermute | solution.py:218
  77.9 13.2 %collective-permute-start.28 = (f32[4,12,8,256]{3,2,1,0:T(8,128)S(1)}, f32[4,12,8,256]{3,2,1,0:T(8,128)S(1)}, u32[]{:S(2)}, u32[]{:S(2)}) collective-permute-start(f32[4,12,8,256]{3,2,1,0:T(8,128)S(1)} %pad_maximum_fusion.4.rest_2_), channel_id=1, source_target_pairs={{0,8},{8,0},{16,24},{24,16},{1,9},{9,1},{17,25},{25,17},{2,10},{10... | collective-permute-start | bytes 1179656 | tf_op jit(solution)/shard_map/ppermute | solution.py:215
  78.9 19.5 %collective-permute-start.29 = (f32[4,12,8,256]{3,2,1,0:T(8,128)S(1)}, f32[4,12,8,256]{3,2,1,0:T(8,128)S(1)}, u32[]{:S(2)}, u32[]{:S(2)}) collective-permute-start(f32[4,12,8,256]{3,2,1,0:T(8,128)S(1)} %pad_maximum_fusion.4.rest_2_), channel_id=1, source_target_pairs={{0,16},{8,24},{16,0},{24,8},{1,17},{9,25},{17,1},{25,9},{2,18},{10... | collective-permute-start | bytes 1179656 | tf_op jit(solution)/shard_map/ppermute | solution.py:215
  80.5 18.0 %collective-permute-start.30 = (f32[4,12,8,256]{3,2,1,0:T(8,128)S(1)}, f32[4,12,8,256]{3,2,1,0:T(8,128)S(1)}, u32[]{:S(2)}, u32[]{:S(2)}) collective-permute-start(f32[4,12,8,256]{3,2,1,0:T(8,128)S(1)} %pad_maximum_fusion.4.rest_2_), channel_id=1, source_target_pairs={{0,24},{8,16},{16,8},{24,0},{1,25},{9,17},{17,9},{25,1},{2,26},{10... | collective-permute-start | bytes 1179656 | tf_op jit(solution)/shard_map/ppermute | solution.py:215
  98.7 28.6 %collective-permute-start.32 = (f32[2,12,32,256]{3,2,1,0:T(8,128)}, f32[2,12,32,256]{3,2,1,0:T(8,128)S(1)}, u32[]{:S(2)}, u32[]{:S(2)}) collective-permute-start(f32[2,12,32,256]{3,2,1,0:T(8,128)} %get-tuple-element.266), channel_id=1, source_target_pairs={{0,2},{1,3},{2,0},{3,1},{4,6},{5,7},{6,4},{7,5},{8,10},{9,11},{10,... | collective-permute-start | bytes 2359304 | tf_op jit(solution)/shard_map/ppermute | solution.py:218
  100.4 25.2 %collective-permute-start.31 = (f32[1,12,32,256]{3,2,1,0:T(8,128)S(1)}, f32[1,12,32,256]{3,2,1,0:T(8,128)S(1)}, u32[]{:S(2)}, u32[]{:S(2)}) collective-permute-start(f32[1,12,32,256]{3,2,1,0:T(8,128)S(1)} %dynamic-slice_add_fusion.2), channel_id=1, source_target_pairs={{0,4},{1,5},{2,6},{3,7},{4,0},{5,1},{6,2},{7,3},{8,12},{9,13},{10,... | collective-permute-start | bytes 1179656 | tf_op jit(solution)/shard_map/ppermute | solution.py:218
  128.2 27.7 %collective-permute-start.38 = (f32[2,12,32,256]{3,2,1,0:T(8,128)}, f32[2,12,32,256]{3,2,1,0:T(8,128)S(1)}, u32[]{:S(2)}, u32[]{:S(2)}) collective-permute-start(f32[2,12,32,256]{3,2,1,0:T(8,128)} %get-tuple-element.291), channel_id=1, source_target_pairs={{0,2},{1,3},{2,0},{3,1},{4,6},{5,7},{6,4},{7,5},{8,10},{9,11},{10,... | collective-permute-start | bytes 2359304 | tf_op jit(solution)/shard_map/ppermute | solution.py:218
  129.1 25.4 %collective-permute-start.37 = (f32[1,12,32,256]{3,2,1,0:T(8,128)}, f32[1,12,32,256]{3,2,1,0:T(8,128)S(1)}, u32[]{:S(2)}, u32[]{:S(2)}) collective-permute-start(f32[1,12,32,256]{3,2,1,0:T(8,128)} %dynamic-slice_add_fusion.1), channel_id=1, source_target_pairs={{0,4},{1,5},{2,6},{3,7},{4,0},{5,1},{6,2},{7,3},{8,12},{9,13},{10,... | collective-permute-start | bytes 1179656 | tf_op jit(solution)/shard_map/ppermute | solution.py:218
  161.5 20.8 %collective-permute-start.39 = (f32[1,12,32,256]{3,2,1,0:T(8,128)S(1)}, f32[1,12,32,256]{3,2,1,0:T(8,128)S(1)}, u32[]{:S(2)}, u32[]{:S(2)}) collective-permute-start(f32[1,12,32,256]{3,2,1,0:T(8,128)S(1)} %dynamic-slice_add_fusion), channel_id=1, source_target_pairs={{0,4},{1,5},{2,6},{3,7},{4,0},{5,1},{6,2},{7,3},{8,12},{9,13},{10,... | collective-permute-start | bytes 1179656 | tf_op jit(solution)/shard_map/ppermute | solution.py:218
  187.4 10.6 %collective-permute-start.45 = (f32[4,32,256]{2,1,0:T(8,128)S(1)}, f32[4,32,256]{2,1,0:T(8,128)S(1)}, u32[]{:S(2)}, u32[]{:S(2)}) collective-permute-start(f32[4,32,256]{2,1,0:T(8,128)S(1)} %add_add_fusion.1), channel_id=1, source_target_pairs={{0,4},{1,5},{2,6},{3,7},{4,0},{5,1},{6,2},{7,3},{8,12},{9,13},{10,... | collective-permute-start | bytes 393224 | tf_op jit(solution)/shard_map/ppermute | solution.py:218
  187.5 11.5 %collective-permute-start.46 = (f32[4,32,256]{2,1,0:T(8,128)S(1)}, f32[4,32,256]{2,1,0:T(8,128)S(1)}, u32[]{:S(2)}, u32[]{:S(2)}) collective-permute-start(f32[4,32,256]{2,1,0:T(8,128)S(1)} %add_add_fusion.1), channel_id=1, source_target_pairs={{0,6},{1,7},{2,4},{3,5},{4,2},{5,3},{6,0},{7,1},{8,14},{9,15},{10,... | collective-permute-start | bytes 393224 | tf_op jit(solution)/shard_map/ppermute | solution.py:218
  188.3 11.8 %collective-permute-start.44 = (f32[4,32,256]{2,1,0:T(8,128)S(1)}, f32[4,32,256]{2,1,0:T(8,128)S(1)}, u32[]{:S(2)}, u32[]{:S(2)}) collective-permute-start(f32[4,32,256]{2,1,0:T(8,128)S(1)} %add_add_fusion.1), channel_id=1, source_target_pairs={{0,2},{1,3},{2,0},{3,1},{4,6},{5,7},{6,4},{7,5},{8,10},{9,11},{10,... | collective-permute-start | bytes 393224 | tf_op jit(solution)/shard_map/ppermute | solution.py:218
  192.1 11.6 %collective-permute-start.54 = (f32[2,32,256]{2,1,0:T(8,128)S(1)}, f32[2,32,256]{2,1,0:T(8,128)S(1)}, u32[]{:S(2)}, u32[]{:S(2)}) collective-permute-start(f32[2,32,256]{2,1,0:T(8,128)S(1)} %get-tuple-element.354), channel_id=1, source_target_pairs={{0,24},{8,16},{16,8},{24,0},{1,25},{9,17},{17,9},{25,1},{2,26},{10... | collective-permute-start | bytes 196616 | tf_op jit(solution)/shard_map/ppermute | solution.py:215
  (77 other events, 519.0 us)

commit v3 on v2

--- a/solution.py
+++ b/solution.py
@@ -25,11 +25,12 @@
 
 
 def dot3(a, b, dims):
-    dot = functools.partial(lax.dot_general, dimension_numbers=(dims, ((), ())), preferred_element_type=F32)
-    return dot(a[0], b[1]) + dot(a[1], b[0]) + dot(a[0], b[0])
-
-
-def prepare_kernel(n, g, groups, ids, structure, block_slot, panel, dinv, table, packed, *rest):
+    left = jnp.concatenate([a[0], a[1], a[0]], axis=dims[0][0])
+    right = jnp.concatenate([b[0], b[0], b[1]], axis=dims[1][0])
+    return lax.dot_general(left, right, dimension_numbers=(dims, ((), ())), preferred_element_type=F32)
+
+
+def prepare_kernel(n, g, groups, second, ids, structure, block_slot, panel, dinv, table, packed, line, *rest):
     pieces, gathered = rest[:-1], rest[-1]
     r, z, c = ids[0], ids[1], ids[2]
     node_count, slot_count, sub, width = panel.shape
@@ -66,6 +67,8 @@
             gathered[pl.ds(k * sub, sub), :] = jnp.where(k < count, panel[s, table[s, SLOT + k]], 0.0)
         rows = dot3(split(gathered[...]), split(dinv[s]), ((1,), (0,))).reshape(CAP, sub, width)
         packed[s] = rows
+        if s in second:
+            line[pl.ds((s - second[0]) * CAP, CAP)] = rows
         b, i = place[s]
         for k in range(n):
             part = rows[:, :piece]
@@ -75,8 +78,8 @@
 
 
 def product_kernel(n, g, start, ids, table, *rest):
-    sources, parts, (keep, send) = rest[:g], rest[g : g + n * g], rest[g + n * g : g + n * g + 2]
-    blocks, run, acc, sems, run_sems = rest[g + n * g + 2 :]
+    sources, near, far, (keep, send) = rest[:g], rest[g : g + n], rest[g + n : 2 * g + n - 1], rest[2 * g + n - 1 : 2 * g + n + 1]
+    blocks, run, acc, sems, run_sems = rest[2 * g + n + 1 :]
     r, z, c = ids[0], ids[1], ids[2]
     node_count = blocks.shape[0]
     sub = blocks.shape[-2]
@@ -100,7 +103,7 @@
                 copy(i, j, k, which).start()
 
     pieces = [
-        pltpu.make_async_copy(parts[jk * g + kc], run.at[:, c ^ kc, r ^ jk], run_sems.at[jk * g + kc])
+        pltpu.make_async_copy(far[kc - 1].at[jk] if kc else near[jk], run.at[:, c ^ kc, r ^ jk], run_sems.at[jk * g + kc])
         for jk in range(n)
         for kc in range(g)
     ]
@@ -143,38 +146,70 @@
                 send[h, i * CAP + k] = jnp.where((z & 1) == 0, odd, even)
 
 
-def finish_kernel(g, halvings, start, ids, table, base, *rest):
+def finish_kernel(g, halvings, with_off, with_diag, start, ids, table, base, *rest):
     received, packed, dinv = rest[:halvings], rest[halvings], rest[halvings + 1]
-    off, diags, product = rest[-g - 2], rest[-g - 1 : -1], rest[-1]
-    c = ids[2]
+    product, outs = rest[-1], rest[-1 - with_off - g * with_diag : -1]
     s = start + pl.program_id(0)
-    slot_count, sub, width = off.shape[1:]
     total = base[0]
     for more in received:
         total = total + more[0]
     product[...] = total
-    for q in range(slot_count):
-        at = table[s, PLACE + q]
-        block = product[jnp.maximum(at, 0)]
-        off[0, q] = jnp.where(at >= 0, -block, 0.0)
+    sub, width = product.shape[1:]
+    if with_off:
+        off = outs[0]
+        for q in range(off.shape[1]):
+            at = table[s, PLACE + q]
+            block = product[jnp.maximum(at, 0)]
+            off[0, q] = jnp.where(at >= 0, -block, 0.0)
+    if not with_diag:
+        return
     mine = packed[0].reshape(CAP * sub, width)
-    dims = ((0,), (0,))
-    diag = dot3(split(mine), split(product[...].reshape(CAP * sub, width)), dims)
-
+    diag = dot3(split(mine), split(product[...].reshape(CAP * sub, width)), ((0,), (0,)))
+    store_shares(diag, dinv, g, ids, outs[with_off:])
+
+
+def store_shares(diag, dinv, g, ids, shares):
     def store(value):
-        half = width // g
+        half = value.shape[0] // g
         for kc in range(g):
             part = value[:half]
             for j in range(1, g):
-                part = jnp.where((c ^ kc) == j, value[j * half : (j + 1) * half], part)
-            diags[kc][0] = part
+                part = jnp.where((ids[2] ^ kc) == j, value[j * half : (j + 1) * half], part)
+            shares[kc][0] = part
 
     store(diag)
 
-    @pl.when((ids[0] == 0) & (ids[1] == 0) & (c == 0))
+    @pl.when((ids[0] == 0) & (ids[1] == 0) & (ids[2] == 0))
     def _():
         factor = split(dinv[0])
-        store(diag + dot3(factor, factor, dims))
+        store(diag + dot3(factor, factor, ((0,), (0,))))
+
+
+def last_diag_kernel(g, halvings, ids, base, *rest):
+    received, packed, dinv, shares = rest[:halvings], rest[halvings], rest[halvings + 1], rest[halvings + 2 :]
+    width = dinv.shape[-1]
+    half = width // g
+    dims = ((0,), (0,))
+    for i in range(dinv.shape[0]):
+        at = pl.ds(i * CAP, CAP)
+        total = base[0, at]
+        for more in received:
+            total = total + more[0, at]
+        diag = dot3(split(packed[i].reshape(-1, width)), split(total.reshape(-1, width)), dims)
+
+        def store(value):
+            for kc in range(g):
+                part = value[:half]
+                for j in range(1, g):
+                    part = jnp.where((ids[2] ^ kc) == j, value[j * half : (j + 1) * half], part)
+                shares[kc][i] = part
+
+        store(diag)
+
+        @pl.when((ids[0] == 0) & (ids[1] == 0) & (ids[2] == 0))
+        def _():
+            factor = split(dinv[i])
+            store(diag + dot3(factor, factor, dims))
 
 
 def tree_sum(terms):
@@ -221,19 +256,20 @@
         return lax.ppermute(x, "col", [(i * g + j, i * g + (j ^ k)) for i in range(n) for j in range(g)])
 
     out = pl.pallas_call(
-        functools.partial(prepare_kernel, n, g, groups),
+        functools.partial(prepare_kernel, n, g, groups, range(batches[0], batches[0] + batches[1])),
         out_shape=[
             jax.ShapeDtypeStruct((node_count, table_width), jnp.int32),
             jax.ShapeDtypeStruct((node_count, CAP, sub, width), F32),
+            jax.ShapeDtypeStruct((batches[1] * CAP, sub, width), F32),
         ]
         + [jax.ShapeDtypeStruct((count * CAP, piece, width), F32) for count in groups for _ in range(n)],
         in_specs=[smem, smem, smem, vmem, vmem],
-        out_specs=[smem] + [vmem] * (1 + n * len(groups)),
+        out_specs=[smem] + [vmem] * (2 + n * len(groups)),
         scratch_shapes=[pltpu.VMEM((CAP * sub, width), F32)],
         compiler_params=params,
         name="prepare",
     )(ids, structure, block_slot, panel, dinv)
-    table, packed, pieces = out[0], out[1], out[2:]
+    table, packed, line, pieces = out[0], out[1], [out[2]], out[3:]
 
     starts = [sum(batches[:b]) for b in range(len(batches))]
     halvings = n.bit_length() - 1
@@ -259,11 +295,11 @@
     def product_stage(b, plane):
         start, count = starts[b], batches[b]
         total = count * CAP
-        parts = [x if k == 0 else along_core(x, k) for x in plane for k in range(g)]
+        parts = list(plane) + [along_core(jnp.stack(plane), k) for k in range(1, g)]
         return pl.pallas_call(
             functools.partial(product_kernel, n, g, start),
             out_shape=[jax.ShapeDtypeStruct((n // 2, total, sub, width), F32)] * 2,
-            in_specs=[smem, smem] + [pl.BlockSpec(memory_space=pltpu.HBM)] * (g + n * g),
+            in_specs=[smem, smem] + [pl.BlockSpec(memory_space=pltpu.HBM)] * (2 * g + n - 1),
             out_specs=[vmem] * 2,
             scratch_shapes=[
                 pltpu.VMEM((count, CAP, CAP, n, sub, width), F32),
@@ -309,23 +345,91 @@
     half = width // g
     quarter = half // n
 
-    def plane_diag(shares):
+    def core_sum(shares):
         share = shares[0]
         for k in range(1, g):
             share = share + along_core(shares[k], k)
+        return share
+
+    def plane_sum(share):
         cut = [lax.dynamic_slice_in_dim(share, (r ^ k) * quarter, quarter, 1) for k in range(n)]
         return tree_sum([cut[0]] + [along_row(cut[k], k) for k in range(1, n)])
 
-    def whole_diag(part):
-        part = tree_sum([part] + [along_z(part, m) for m in range(1, n)])
+    def plane_diag(shares):
+        return plane_sum(core_sum(shares))
+
+    def line_sum(part):
+        return tree_sum([part] + [along_z(part, m) for m in range(1, n)])
+
+    def plane_gather(part):
         parts = [part] + [along_row(part, k) for k in range(1, n)]
-        mine = jnp.concatenate([pick(parts, r ^ j) for j in range(n)], axis=1)
+        return jnp.concatenate([pick(parts, r ^ j) for j in range(n)], axis=1)
+
+    def core_gather(mine):
         halves = [mine] + [along_core(mine, k) for k in range(1, g)]
         return jnp.concatenate([pick(halves, c ^ j) for j in range(g)], axis=1)
 
-    off, first_diag = None, None
+    def joined(shares):
+        return [jnp.concatenate([held[k] for held in shares]) for k in range(g)]
+
+    def finish(b, off, with_off, with_diag):
+        start, count = starts[b], batches[b]
+        of_node = lambda i, ids, table: (start + i, 0, 0, 0)
+        of_dest = lambda level: lambda i, ids, table: (ids[1] >> level, i, 0, 0)
+        out_shape, out_specs = [], []
+        if with_off:
+            out_shape.append(jax.ShapeDtypeStruct((node_count, slot_count, sub, width), F32))
+            out_specs.append(pl.BlockSpec((1, slot_count, sub, width), of_node))
+        if with_diag:
+            out_shape += [jax.ShapeDtypeStruct((count, half, width), F32)] * g
+            out_specs += [pl.BlockSpec((1, half, width), lambda i, ids, table: (i, 0, 0))] * g
+        result = pl.pallas_call(
+            functools.partial(finish_kernel, g, halvings, with_off, with_diag, start),
+            out_shape=out_shape,
+            grid_spec=pltpu.PrefetchScalarGridSpec(
+                num_scalar_prefetch=2,
+                grid=(count,),
+                in_specs=[pl.BlockSpec((1, CAP, sub, width), of_dest(level)) for level in levels]
+                + [
+                    pl.BlockSpec((1, CAP, sub, width), of_node),
+                    pl.BlockSpec((1, width, width), lambda i, ids, table: (start + i, 0, 0)),
+                ]
+                + [pl.BlockSpec(memory_space=pl.ANY)] * (off is not None),
+                out_specs=out_specs,
+                scratch_shapes=[pltpu.VMEM((CAP, sub, width), F32)],
+            ),
+            input_output_aliases={} if off is None else {5 + halvings: 0},
+            compiler_params=params,
+            cost_estimate=pl.CostEstimate(flops=1, bytes_accessed=1, transcendentals=0),
+            name="finish",
+        )(ids, table, *state[b], packed, dinv, *([] if off is None else [off]))
+        return result[0], list(result[with_off:])
+
+    def last_diag():
+        count, total = batches[-1], batches[-1] * CAP
+        block = (node_count - count) // count
+        of_dest = lambda level: lambda i, ids: (ids[1] >> level, 0, 0, 0)
+        return pl.pallas_call(
+            functools.partial(last_diag_kernel, g, halvings),
+            out_shape=[jax.ShapeDtypeStruct((count, half, width), F32)] * g,
+            grid_spec=pltpu.PrefetchScalarGridSpec(
+                num_scalar_prefetch=1,
+                grid=(1,),
+                in_specs=[pl.BlockSpec((1, total, sub, width), of_dest(level)) for level in levels]
+                + [
+                    pl.BlockSpec((count, CAP, sub, width), lambda i, ids: (block, 0, 0, 0)),
+                    pl.BlockSpec((count, width, width), lambda i, ids: (block, 0, 0)),
+                ],
+                out_specs=[pl.BlockSpec((count, half, width), lambda i, ids: (0, 0, 0))] * g,
+            ),
+            compiler_params=params,
+            cost_estimate=pl.CostEstimate(flops=1, bytes_accessed=1, transcendentals=0),
+            name="last_diag",
+        )(ids, *state[last], packed, dinv)
+
+    off, early, first_diag = None, [], None
     last = len(batches) - 1
-    for phase in range(2 + len(stages) + last + 1):
+    for phase in range(2 + len(stages) + last):
         done = phase - 2 - len(stages)
         now = [(b, phase - 2 - b) for b in range(last + 1) if 0 <= phase - 2 - b < len(stages)]
         now_crossing = [(group, phase - group) for group in range(2) if 0 <= phase - group < 2]
@@ -336,8 +440,7 @@
             state[b] = stages[stage][0](b, state[b])
         for group, stage in now_crossing:
             crossing[group] = cross_stages[stage][0](group, crossing[group])
-        if done < last:
-            state, crossing, shared = after((state, crossing, shared))
+        state, crossing, shared, early = after((state, crossing, shared, early))
         for b, stage in now:
             state[b] = stages[stage][1](b, state[b])
         for group, stage in now_crossing:
@@ -346,42 +449,25 @@
             shared = [lax.dynamic_index_in_dim(shared[k - 1], c ^ k, 2, keepdims=False) for k in range(1, g)]
         elif phase == 1:
             shared = [along_core(shared[k - 1], k) for k in range(1, g)]
-        if done < 0:
-            state, crossing, shared = after((state, crossing, shared))
-            continue
-        start, count = starts[done], batches[done]
-        of_node = lambda i, ids, table, start=start: (start + i, 0, 0, 0)
-        of_dest = lambda level: lambda i, ids, table: (ids[1] >> level, i, 0, 0)
-        result = pl.pallas_call(
-            functools.partial(finish_kernel, g, halvings, start),
-            out_shape=[jax.ShapeDtypeStruct((node_count, slot_count, sub, width), F32)]
-            + [jax.ShapeDtypeStruct((count, half, width), F32)] * g,
-            grid_spec=pltpu.PrefetchScalarGridSpec(
-                num_scalar_prefetch=2,
-                grid=(count,),
-                in_specs=[pl.BlockSpec((1, CAP, sub, width), of_dest(level)) for level in levels]
-                + [
-                    pl.BlockSpec((1, CAP, sub, width), of_node),
-                    pl.BlockSpec((1, width, width), lambda i, ids, table, start=start: (start + i, 0, 0)),
-                ]
-                + [pl.BlockSpec(memory_space=pl.ANY)] * (off is not None),
-                out_specs=[pl.BlockSpec((1, slot_count, sub, width), of_node)]
-                + [pl.BlockSpec((1, half, width), lambda i, ids, table: (i, 0, 0))] * g,
-                scratch_shapes=[pltpu.VMEM((CAP, sub, width), F32)],
-            ),
-            input_output_aliases={} if off is None else {5 + halvings: 0},
-            compiler_params=params,
-            cost_estimate=pl.CostEstimate(flops=1, bytes_accessed=1, transcendentals=0),
-            name="finish",
-        )(ids, table, *state[done], packed, dinv, *([] if off is None else [off]))
-        off, state[done] = result[0], result[1:]
-        if done < last - 1:
-            state = after(state)
-        elif done == last - 1:
-            first_diag = plane_diag([jnp.concatenate([held[k] for held in state[:last]]) for k in range(g)])
-            state[last], first_diag = after((state[last], first_diag))
-    diag = [whole_diag(first_diag)] if last else []
-    return off, jnp.concatenate(diag + [whole_diag(plane_diag(state[last]))], axis=0)
+        if done == 0:
+            off, shares = finish(0, None, True, True)
+            early = [shares]
+            state[0] = []
+        elif done == 1:
+            first_diag = plane_diag(joined(early))
+            off, more = finish(1, off, True, True)
+            state[1] = early = []
+            state, first_diag, off, more = after((state, first_diag, off, more))
+            break
+        state, crossing, shared, early = after((state, crossing, shared, early))
+    shares = last_diag()
+    off, _ = finish(last, off, True, False)
+    first = line_sum(first_diag)
+    second = core_sum([jnp.concatenate(pair) for pair in zip(more, shares)])
+    first, second = plane_gather(first), plane_sum(second)
+    second, off = after((second, off))
+    first, second = core_gather(first), line_sum(second)
+    return off, jnp.concatenate([first, core_gather(plane_gather(second))], axis=0)
 
 
 def solution(mesh):

time: 223 us -> 221 us (level)
  waiting for transfers between devices: 96.8 us -> 85.6 us
  Pallas kernels: 44.2 us -> 52.8 us
    ppermute x18, waiting for transfers between devices: 70.2 us -> 63.2 us  [along_z(): lax.ppermute(x, 'col', [(i * g + j, (i ^ m) * g + j) for i in range(n) fo...]
    ppermute x27, waiting for transfers between devices: 24.2 us -> 18.5 us  [along_row(): return lax.ppermute(x, 'row', [(i, i ^ k) for i in range(n)])]
    pallas_call x3, Pallas kernels: 26.7 us -> 32.2 us  [product_stage(): pl.pallas_call(functools.partial(product_kernel, n, g, start), out_shape=...]
    pallas_call x4 -> x5, Pallas kernels: 17.5 us -> 20.6 us  [the longest x3 11.8 us: finish(): pl.pallas_call(functools.partial(finish_kernel, g, halvings, with_off, wi...]
    unnamed x78 -> x62, local copies, waits for them, and re-layouts: 3.47 us -> 5.19 us
  transfers between devices with their start and end apart: 62 -> 53, of which waited for: 28 -> 24; matrix products, arithmetic and copies ran while one was open for 3% -> 3% of each run, Pallas kernels for 14% -> 20%
where the time goes in v3:
time: 221 us; the launch traced here: 220 us
  waiting for transfers between devices  85.6 us (39%)
  starting transfers between devices  62.7 us (28%)
  Pallas kernels  52.8 us (24%)
  local copies, waits for them, and re-layouts  10.2 us (5%)
  other arithmetic  7.49 us (3%)
    ppermute x18, waiting for transfers between devices, along_z(): lax.ppermute(x, 'col', [(i * g + j, (i ^ m) * g + j) for i in range(n) fo...  63.2 us
    pallas_call x3, Pallas kernels, product_stage(): pl.pallas_call(functools.partial(product_kernel, n, g, start), out_shape=...  32.2 us
    ppermute x27, starting transfers between devices, along_row(): return lax.ppermute(x, 'row', [(i, i ^ k) for i in range(n)])  32.1 us
    ppermute x18, starting transfers between devices, along_z(): lax.ppermute(x, 'col', [(i * g + j, (i ^ m) * g + j) for i in range(n) fo...  29.7 us
    ppermute x27, waiting for transfers between devices, along_row(): return lax.ppermute(x, 'row', [(i, i ^ k) for i in range(n)])  18.5 us
    pallas_call x3, Pallas kernels, finish(): pl.pallas_call(functools.partial(finish_kernel, g, halvings, with_off, wi...  11.8 us
    unnamed x62, local copies, waits for them, and re-layouts  5.19 us
    squeeze x1, local copies, waits for them, and re-layouts, body(): lax.dynamic_index_in_dim(shared[k - 1], c ^ k, 2, keepdims=False)  4.91 us
  transfers between devices with their start and end apart: 53, of which 24 were waited for; matrix products, arithmetic and copies ran while one was open for 3% of the time, Pallas kernels for 20%

profile of v3, /device:TPU:0, one launch (start us, length us, event | category | flops | bytes accessed | tf_op | source)
XLA Modules:
  0.0 220.0 jit_solution(4665571422768665181)
XLA Ops:
  1.3 4.5 %prepare.1 = (s32[6,24]{1,0:T(8,128)}, f32[6,6,32,256]{3,2,1,0:T(8,128)}, f32[12,32,256]{2,1,0:T(8,128)}, f32[12,8,256]{2,1,0:T(8,128)}, f32[12,8,256]{2,1,0:T(8...) custom-call(s32[3]{0:T(128)} %pad_add_fusion.ids, ...), custom_call_target="tpu_custom_call" | custom-call | tf_op jit(solution)/shard_map/prepare/pallas_call | solution.py:258
  5.8 3.0 %collective-permute-start = (f32[12,8,256]{2,1,0:T(8,128)}, f32[12,8,256]{2,1,0:T(8,128)S(1)}, u32[]{:S(2)}, u32[]{:S(2)}) collective-permute-start(f32[12,8,256]{2,1,0:T(8,128)} %get-tuple-element.174), channel_id=1, source_target_pairs={{0,8},{8,0},{16,24},{24,16},{1,9},{9,1},{17,25},{25,17},{2,10},{10... | collective-permute-start | bytes 294920 | tf_op jit(solution)/shard_map/ppermute | solution.py:250
  10.4 4.9 %dynamic-slice_bitcast_fusion = f32[8,4,32,1024]{3,2,1,0:T(8,128)} fusion(f32[8,4,2,32,1024]{4,3,2,1,0:T(8,128)} %bitcast.42, s32[]{:T(128)S(6)} %select_n.535), kind=kLoop, calls=%fused_computation | loop fusion | bytes 8388612 | tf_op jit(solution)/shard_map/jit(dynamic_index_in_dim)/squeeze | solution.py:449
  17.8 2.6 %collective-permute-start.4 = (f32[12,8,256]{2,1,0:T(8,128)S(1)}, f32[12,8,256]{2,1,0:T(8,128)S(1)}, u32[]{:S(2)}, u32[]{:S(2)}) collective-permute-start(f32[12,8,256]{2,1,0:T(8,128)S(1)} %get-tuple-element.193), channel_id=1, source_target_pairs={{0,4},{1,5},{2,6},{3,7},{4,0},{5,1},{6,2},{7,3},{8,12},{9,13},{10,... | collective-permute-start | bytes 294920 | tf_op jit(solution)/shard_map/ppermute | solution.py:253
  25.7 2.5 %collective-permute-start.5 = (f32[12,8,256]{2,1,0:T(8,128)S(1)}, f32[12,8,256]{2,1,0:T(8,128)S(1)}, u32[]{:S(2)}, u32[]{:S(2)}) collective-permute-start(f32[12,8,256]{2,1,0:T(8,128)S(1)} %get-tuple-element.194), channel_id=1, source_target_pairs={{0,6},{1,7},{2,4},{3,5},{4,2},{5,3},{6,0},{7,1},{8,14},{9,15},{10,... | collective-permute-start | bytes 294920 | tf_op jit(solution)/shard_map/ppermute | solution.py:253
  28.2 3.9 %collective-permute-done.5 = f32[12,8,256]{2,1,0:T(8,128)S(1)} collective-permute-done((f32[12,8,256]{2,1,0:T(8,128)S(1)}, f32[12,8,256]{2,1,0:T(8,128)S(1)}, u32[]{:S(2)}, u32[]{:S(2)}) %collective-permute-start.5) | collective-permute-done | bytes 98336 | tf_op jit(solution)/shard_map/ppermute | solution.py:253
  36.5 2.5 %collective-permute-start.14 = (f32[24,8,256]{2,1,0:T(8,128)S(1)}, f32[24,8,256]{2,1,0:T(8,128)S(1)}, u32[]{:S(2)}, u32[]{:S(2)}) collective-permute-start(f32[24,8,256]{2,1,0:T(8,128)S(1)} %get-tuple-element.212), channel_id=1, source_target_pairs={{0,4},{1,5},{2,6},{3,7},{4,0},{5,1},{6,2},{7,3},{8,12},{9,13},{10,... | collective-permute-start | bytes 589832 | tf_op jit(solution)/shard_map/ppermute | solution.py:253
  39.3 2.5 %collective-permute-start.15 = (f32[24,8,256]{2,1,0:T(8,128)S(1)}, f32[24,8,256]{2,1,0:T(8,128)S(1)}, u32[]{:S(2)}, u32[]{:S(2)}) collective-permute-start(f32[24,8,256]{2,1,0:T(8,128)S(1)} %get-tuple-element.213), channel_id=1, source_target_pairs={{0,6},{1,7},{2,4},{3,5},{4,2},{5,3},{6,0},{7,1},{8,14},{9,15},{10,... | collective-permute-start | bytes 589832 | tf_op jit(solution)/shard_map/ppermute | solution.py:253
  41.8 9.7 %collective-permute-done.14 = f32[24,8,256]{2,1,0:T(8,128)S(1)} collective-permute-done((f32[24,8,256]{2,1,0:T(8,128)S(1)}, f32[24,8,256]{2,1,0:T(8,128)S(1)}, u32[]{:S(2)}, u32[]{:S(2)}) %collective-permute-start.14) | collective-permute-done | bytes 196640 | tf_op jit(solution)/shard_map/ppermute | solution.py:253
  57.7 7.1 %product.3 = (f32[2,12,32,256]{3,2,1,0:T(8,128)}, f32[2,12,32,256]{3,2,1,0:T(8,128)}) custom-call(s32[3]{0:T(128)} %pad_add_fusion.ids, s32[6,24]{1,0:T(8,128)} %get-tuple-element.164.table, f32[8,4,2,32,1024]{4,3,2,1,0:T(8,128)} %bitcast.43, f32[8,4,32,1024]{3,2,1,0:T(8,128)} %collective-permute-done.9.rest_1_, f32[4,12,8,256]{3,2,1,0:T(8,128)} %copy-done.3, ...), custom_call_target="tpu_custom_call" | custom-call | flops 1 | bytes 1 | tf_op jit(solution)/shard_map/product/pallas_call | solution.py:299
  65.0 8.8 %collective-permute-done.18.rest_4_ = f32[4,12,8,256]{3,2,1,0:T(8,128)S(1)} collective-permute-done((f32[4,12,8,256]{3,2,1,0:T(8,128)S(1)}, f32[4,12,8,256]{3,2,1,0:T(8,128)S(1)}, u32[]{:S(2)}, u32[]{:S(2)}) %collective-permute-start.18) | collective-permute-done | bytes 393248 | tf_op jit(solution)/shard_map/ppermute | solution.py:250
  75.3 3.7 %collective-permute-start.20 = (f32[2,12,32,256]{3,2,1,0:T(8,128)}, f32[2,12,32,256]{3,2,1,0:T(8,128)S(1)}, u32[]{:S(2)}, u32[]{:S(2)}) collective-permute-start(f32[2,12,32,256]{3,2,1,0:T(8,128)} %get-tuple-element.248), channel_id=1, source_target_pairs={{0,2},{1,3},{2,0},{3,1},{4,6},{5,7},{6,4},{7,5},{8,10},{9,11},{10,... | collective-permute-start | bytes 2359304 | tf_op jit(solution)/shard_map/ppermute | solution.py:253
  82.5 13.1 %product.4 = (f32[2,12,32,256]{3,2,1,0:T(8,128)}, f32[2,12,32,256]{3,2,1,0:T(8,128)}) custom-call(s32[3]{0:T(128)} %pad_add_fusion.ids, s32[6,24]{1,0:T(8,128)} %get-tuple-element.164.table, f32[8,4,2,32,1024]{4,3,2,1,0:T(8,128)} %bitcast.44, f32[8,4,32,1024]{3,2,1,0:T(8,128)} %collective-permute-done.9.rest_1_, f32[4,12,8,256]{3,2,1,0:T(8,128)} %copy-done.2, ...), custom_call_target="tpu_custom_call" | custom-call | flops 1 | bytes 1 | tf_op jit(solution)/shard_map/product/pallas_call | solution.py:299
  95.6 3.3 %collective-permute-done.23.rest_4_ = f32[4,12,8,256]{3,2,1,0:T(8,128)S(1)} collective-permute-done((f32[4,12,8,256]{3,2,1,0:T(8,128)S(1)}, f32[4,12,8,256]{3,2,1,0:T(8,128)S(1)}, u32[]{:S(2)}, u32[]{:S(2)}) %collective-permute-start.23) | collective-permute-done | bytes 393248 | tf_op jit(solution)/shard_map/ppermute | solution.py:250
  100.9 2.3 %collective-permute-start.25 = (f32[1,12,32,256]{3,2,1,0:T(8,128)S(1)}, f32[1,12,32,256]{3,2,1,0:T(8,128)S(1)}, u32[]{:S(2)}, u32[]{:S(2)}) collective-permute-start(f32[1,12,32,256]{3,2,1,0:T(8,128)S(1)} %dynamic-slice_add_fusion.2), channel_id=1, source_target_pairs={{0,4},{1,5},{2,6},{3,7},{4,0},{5,1},{6,2},{7,3},{8,12},{9,13},{10,... | collective-permute-start | bytes 1179656 | tf_op jit(solution)/shard_map/ppermute | solution.py:253
  104.7 12.0 %product.5 = (f32[2,12,32,256]{3,2,1,0:T(8,128)}, f32[2,12,32,256]{3,2,1,0:T(8,128)}) custom-call(s32[3]{0:T(128)} %pad_add_fusion.ids, s32[6,24]{1,0:T(8,128)} %get-tuple-element.164.table, f32[8,4,2,32,1024]{4,3,2,1,0:T(8,128)} %bitcast.45, f32[8,4,32,1024]{3,2,1,0:T(8,128)} %collective-permute-done.9.rest_1_, f32[4,12,8,256]{3,2,1,0:T(8,128)} %copy-done.4, ...), custom_call_target="tpu_custom_call" | custom-call | flops 1 | bytes 1 | tf_op jit(solution)/shard_map/product/pallas_call | solution.py:299
  116.7 9.6 %collective-permute-done.25.rest_1_ = f32[1,12,32,256]{3,2,1,0:T(8,128)S(1)} collective-permute-done((f32[1,12,32,256]{3,2,1,0:T(8,128)S(1)}, f32[1,12,32,256]{3,2,1,0:T(8,128)S(1)}, u32[]{:S(2)}, u32[]{:S(2)}) %collective-permute-start.25) | collective-permute-done | bytes 393248 | tf_op jit(solution)/shard_map/ppermute | solution.py:253
  131.2 4.4 %finish.3 = (f32[6,8,32,256]{3,2,1,0:T(8,128)}, f32[2,128,256]{2,1,0:T(8,128)}, f32[2,128,256]{2,1,0:T(8,128)}) custom-call(s32[3]{0:T(128)} %pad_add_fusion.ids, s32[6,24]{1,0:T(8,128)} %get-tuple-element.164.table, f32[2,12,32,256]{3,2,1,0:T(8,128)} %get-tuple-element.290.base, f32[2,12,32,256]{3,2,1,0:T(8,128)} %copy-done.8, ...), custom_call_target="tpu_custom_call" | custom-call | flops 1 | bytes 1 | tf_op jit(solution)/shard_map/finish/pallas_call | solution.py:386
  135.5 18.6 %collective-permute-done.28.rest_1_ = f32[1,12,32,256]{3,2,1,0:T(8,128)S(1)} collective-permute-done((f32[1,12,32,256]{3,2,1,0:T(8,128)S(1)}, f32[1,12,32,256]{3,2,1,0:T(8,128)S(1)}, u32[]{:S(2)}, u32[]{:S(2)}) %collective-permute-start.28) | collective-permute-done | bytes 393248 | tf_op jit(solution)/shard_map/ppermute | solution.py:253
  162.4 4.3 %finish.4 = (f32[6,8,32,256]{3,2,1,0:T(8,128)}, f32[2,128,256]{2,1,0:T(8,128)}, f32[2,128,256]{2,1,0:T(8,128)}) custom-call(s32[3]{0:T(128)} %pad_add_fusion.ids, s32[6,24]{1,0:T(8,128)} %get-tuple-element.164.table, f32[2,12,32,256]{3,2,1,0:T(8,128)} %get-tuple-element.308.base, f32[2,12,32,256]{3,2,1,0:T(8,128)} %copy-done.7, ...), custom_call_target="tpu_custom_call", output_to_operand_aliasing={{0}: (7, {})} | custom-call | flops 1 | bytes 1 | tf_op jit(solution)/shard_map/finish/pallas_call | solution.py:386
  166.7 10.1 %collective-permute-done.30.rest_1_ = f32[1,12,32,256]{3,2,1,0:T(8,128)S(1)} collective-permute-done((f32[1,12,32,256]{3,2,1,0:T(8,128)S(1)}, f32[1,12,32,256]{3,2,1,0:T(8,128)S(1)}, u32[]{:S(2)}, u32[]{:S(2)}) %collective-permute-start.30) | collective-permute-done | bytes 393248 | tf_op jit(solution)/shard_map/ppermute | solution.py:253
  177.6 4.4 %last_diag.1 = (f32[2,128,256]{2,1,0:T(8,128)}, f32[2,128,256]{2,1,0:T(8,128)}) custom-call(s32[3]{0:T(128)} %pad_add_fusion.ids, f32[2,12,32,256]{3,2,1,0:T(8,128)} %get-tuple-element.316.base, f32[2,12,32,256]{3,2,1,0:T(8,128)} %copy-done.1, f32[1,12,32,256]{3,2,1,0:T(8,128)} %copy-done.9, f32[6,6,32,256]{3,2,1,0:T(8,128)} %get-tuple-element.293.rest_2_, ...), custom_call_target="tpu_custom_call" | custom-call | flops 1 | bytes 1 | tf_op jit(solution)/shard_map/last_diag/pallas_call | solution.py:412
  190.9 3.1 %finish.5 = f32[6,8,32,256]{3,2,1,0:T(8,128)} custom-call(s32[3]{0:T(128)} %pad_add_fusion.ids, s32[6,24]{1,0:T(8,128)} %get-tuple-element.164.table, f32[2,12,32,256]{3,2,1,0:T(8,128)} %get-tuple-element.316.base, f32[2,12,32,256]{3,2,1,0:T(8,128)} %copy-done.1, f32[1,12,32,256]{3,2,1,0:T(8,128)} %copy-done.9, ...), custom_call_target="tpu_custom_call", output_to_operand_aliasing={{}: (7, {})} | custom-call | flops 1 | bytes 1 | tf_op jit(solution)/shard_map/finish/pallas_call | solution.py:386
  202.1 5.4 %collective-permute-done.47 = f32[4,32,256]{2,1,0:T(8,128)S(1)} collective-permute-done((f32[4,32,256]{2,1,0:T(8,128)S(1)}, f32[4,32,256]{2,1,0:T(8,128)S(1)}, u32[]{:S(2)}, u32[]{:S(2)}) %collective-permute-start.47) | collective-permute-done | bytes 131104 | tf_op jit(solution)/shard_map/ppermute | solution.py:253
  (186 shorter events, 72.6 us)
Async XLA Ops:
  16.1 16.1 %collective-permute-start.9 = (f32[8,4,32,1024]{3,2,1,0:T(8,128)}, f32[8,4,32,1024]{3,2,1,0:T(8,128)}, u32[]{:S(2)}, u32[]{:S(2)}) collective-permute-start(f32[8,4,32,1024]{3,2,1,0:T(8,128)} %dynamic-slice_bitcast_fusion), channel_id=1, source_target_pairs={{0,1},{1,0},{2,3},{3,2},{4,5},{5,4},{6,7},{7,6},{8,9},{9,8},{10,11... | collective-permute-start | bytes 12582920 | tf_op jit(solution)/shard_map/ppermute | solution.py:256
  20.4 11.7 %collective-permute-start.6 = (f32[24,8,256]{2,1,0:T(8,128)S(1)}, f32[24,8,256]{2,1,0:T(8,128)S(1)}, u32[]{:S(2)}, u32[]{:S(2)}) collective-permute-start(f32[24,8,256]{2,1,0:T(8,128)S(1)} %copy-done.30), channel_id=1, source_target_pairs={{0,8},{8,0},{16,24},{24,16},{1,9},{9,1},{17,25},{25,17},{2,10},{10... | collective-permute-start | bytes 589832 | tf_op jit(solution)/shard_map/ppermute | solution.py:250
  21.6 10.6 %collective-permute-start.7 = (f32[24,8,256]{2,1,0:T(8,128)S(1)}, f32[24,8,256]{2,1,0:T(8,128)S(1)}, u32[]{:S(2)}, u32[]{:S(2)}) collective-permute-start(f32[24,8,256]{2,1,0:T(8,128)S(1)} %copy-done.29), channel_id=1, source_target_pairs={{0,16},{8,24},{16,0},{24,8},{1,17},{9,25},{17,1},{25,9},{2,18},{10... | collective-permute-start | bytes 589832 | tf_op jit(solution)/shard_map/ppermute | solution.py:250
  33.0 18.5 %collective-permute-start.10 = (f32[4,12,8,256]{3,2,1,0:T(8,128)S(1)}, f32[4,12,8,256]{3,2,1,0:T(8,128)S(1)}, u32[]{:S(2)}, u32[]{:S(2)}) collective-permute-start(f32[4,12,8,256]{3,2,1,0:T(8,128)S(1)} %pad_maximum_fusion.5.rest_2_), channel_id=1, source_target_pairs={{0,8},{8,0},{16,24},{24,16},{1,9},{9,1},{17,25},{25,17},{2,10},{10... | collective-permute-start | bytes 1179656 | tf_op jit(solution)/shard_map/ppermute | solution.py:250
  34.2 17.9 %collective-permute-start.11 = (f32[4,12,8,256]{3,2,1,0:T(8,128)S(1)}, f32[4,12,8,256]{3,2,1,0:T(8,128)S(1)}, u32[]{:S(2)}, u32[]{:S(2)}) collective-permute-start(f32[4,12,8,256]{3,2,1,0:T(8,128)S(1)} %pad_maximum_fusion.5.rest_2_), channel_id=1, source_target_pairs={{0,16},{8,24},{16,0},{24,8},{1,17},{9,25},{17,1},{25,9},{2,18},{10... | collective-permute-start | bytes 1179656 | tf_op jit(solution)/shard_map/ppermute | solution.py:250
  35.2 16.9 %collective-permute-start.12 = (f32[4,12,8,256]{3,2,1,0:T(8,128)S(1)}, f32[4,12,8,256]{3,2,1,0:T(8,128)S(1)}, u32[]{:S(2)}, u32[]{:S(2)}) collective-permute-start(f32[4,12,8,256]{3,2,1,0:T(8,128)S(1)} %pad_maximum_fusion.5.rest_2_), channel_id=1, source_target_pairs={{0,24},{8,16},{16,8},{24,0},{1,25},{9,17},{17,9},{25,1},{2,26},{10... | collective-permute-start | bytes 1179656 | tf_op jit(solution)/shard_map/ppermute | solution.py:250
  36.5 15.0 %collective-permute-start.14 = (f32[24,8,256]{2,1,0:T(8,128)S(1)}, f32[24,8,256]{2,1,0:T(8,128)S(1)}, u32[]{:S(2)}, u32[]{:S(2)}) collective-permute-start(f32[24,8,256]{2,1,0:T(8,128)S(1)} %get-tuple-element.212), channel_id=1, source_target_pairs={{0,4},{1,5},{2,6},{3,7},{4,0},{5,1},{6,2},{7,3},{8,12},{9,13},{10,... | collective-permute-start | bytes 589832 | tf_op jit(solution)/shard_map/ppermute | solution.py:253
  39.3 12.2 %collective-permute-start.15 = (f32[24,8,256]{2,1,0:T(8,128)S(1)}, f32[24,8,256]{2,1,0:T(8,128)S(1)}, u32[]{:S(2)}, u32[]{:S(2)}) collective-permute-start(f32[24,8,256]{2,1,0:T(8,128)S(1)} %get-tuple-element.213), channel_id=1, source_target_pairs={{0,6},{1,7},{2,4},{3,5},{4,2},{5,3},{6,0},{7,1},{8,14},{9,15},{10,... | collective-permute-start | bytes 589832 | tf_op jit(solution)/shard_map/ppermute | solution.py:253
  53.0 11.9 %collective-permute-start.17 = (f32[4,12,8,256]{3,2,1,0:T(8,128)S(1)}, f32[4,12,8,256]{3,2,1,0:T(8,128)S(1)}, u32[]{:S(2)}, u32[]{:S(2)}) collective-permute-start(f32[4,12,8,256]{3,2,1,0:T(8,128)S(1)} %pad_maximum_fusion.6.rest_2_), channel_id=1, source_target_pairs={{0,8},{8,0},{16,24},{24,16},{1,9},{9,1},{17,25},{25,17},{2,10},{10... | collective-permute-start | bytes 1179656 | tf_op jit(solution)/shard_map/ppermute | solution.py:250
  54.0 19.7 %collective-permute-start.18 = (f32[4,12,8,256]{3,2,1,0:T(8,128)S(1)}, f32[4,12,8,256]{3,2,1,0:T(8,128)S(1)}, u32[]{:S(2)}, u32[]{:S(2)}) collective-permute-start(f32[4,12,8,256]{3,2,1,0:T(8,128)S(1)} %pad_maximum_fusion.6.rest_2_), channel_id=1, source_target_pairs={{0,16},{8,24},{16,0},{24,8},{1,17},{9,25},{17,1},{25,9},{2,18},{10... | collective-permute-start | bytes 1179656 | tf_op jit(solution)/shard_map/ppermute | solution.py:250
  55.3 18.5 %collective-permute-start.19 = (f32[4,12,8,256]{3,2,1,0:T(8,128)S(1)}, f32[4,12,8,256]{3,2,1,0:T(8,128)S(1)}, u32[]{:S(2)}, u32[]{:S(2)}) collective-permute-start(f32[4,12,8,256]{3,2,1,0:T(8,128)S(1)} %pad_maximum_fusion.6.rest_2_), channel_id=1, source_target_pairs={{0,24},{8,16},{16,8},{24,0},{1,25},{9,17},{17,9},{25,1},{2,26},{10... | collective-permute-start | bytes 1179656 | tf_op jit(solution)/shard_map/ppermute | solution.py:250
  75.3 23.6 %collective-permute-start.20 = (f32[2,12,32,256]{3,2,1,0:T(8,128)}, f32[2,12,32,256]{3,2,1,0:T(8,128)S(1)}, u32[]{:S(2)}, u32[]{:S(2)}) collective-permute-start(f32[2,12,32,256]{3,2,1,0:T(8,128)} %get-tuple-element.248), channel_id=1, source_target_pairs={{0,2},{1,3},{2,0},{3,1},{4,6},{5,7},{6,4},{7,5},{8,10},{9,11},{10,... | collective-permute-start | bytes 2359304 | tf_op jit(solution)/shard_map/ppermute | solution.py:253
  79.0 16.6 %collective-permute-start.22 = (f32[4,12,8,256]{3,2,1,0:T(8,128)S(1)}, f32[4,12,8,256]{3,2,1,0:T(8,128)S(1)}, u32[]{:S(2)}, u32[]{:S(2)}) collective-permute-start(f32[4,12,8,256]{3,2,1,0:T(8,128)S(1)} %pad_maximum_fusion.7.rest_2_), channel_id=1, source_target_pairs={{0,8},{8,0},{16,24},{24,16},{1,9},{9,1},{17,25},{25,17},{2,10},{10... | collective-permute-start | bytes 1179656 | tf_op jit(solution)/shard_map/ppermute | solution.py:250
  79.6 19.3 %collective-permute-start.23 = (f32[4,12,8,256]{3,2,1,0:T(8,128)S(1)}, f32[4,12,8,256]{3,2,1,0:T(8,128)S(1)}, u32[]{:S(2)}, u32[]{:S(2)}) collective-permute-start(f32[4,12,8,256]{3,2,1,0:T(8,128)S(1)} %pad_maximum_fusion.7.rest_2_), channel_id=1, source_target_pairs={{0,16},{8,24},{16,0},{24,8},{1,17},{9,25},{17,1},{25,9},{2,18},{10... | collective-permute-start | bytes 1179656 | tf_op jit(solution)/shard_map/ppermute | solution.py:250
  80.7 18.3 %collective-permute-start.24 = (f32[4,12,8,256]{3,2,1,0:T(8,128)S(1)}, f32[4,12,8,256]{3,2,1,0:T(8,128)S(1)}, u32[]{:S(2)}, u32[]{:S(2)}) collective-permute-start(f32[4,12,8,256]{3,2,1,0:T(8,128)S(1)} %pad_maximum_fusion.7.rest_2_), channel_id=1, source_target_pairs={{0,24},{8,16},{16,8},{24,0},{1,25},{9,17},{17,9},{25,1},{2,26},{10... | collective-permute-start | bytes 1179656 | tf_op jit(solution)/shard_map/ppermute | solution.py:250
  100.7 27.8 %collective-permute-start.26 = (f32[2,12,32,256]{3,2,1,0:T(8,128)S(1)}, f32[2,12,32,256]{3,2,1,0:T(8,128)S(1)}, u32[]{:S(2)}, u32[]{:S(2)}) collective-permute-start(f32[2,12,32,256]{3,2,1,0:T(8,128)S(1)} %copy-done.27), channel_id=1, source_target_pairs={{0,2},{1,3},{2,0},{3,1},{4,6},{5,7},{6,4},{7,5},{8,10},{9,11},{10,... | collective-permute-start | bytes 2359304 | tf_op jit(solution)/shard_map/ppermute | solution.py:253
  100.9 25.4 %collective-permute-start.25 = (f32[1,12,32,256]{3,2,1,0:T(8,128)S(1)}, f32[1,12,32,256]{3,2,1,0:T(8,128)S(1)}, u32[]{:S(2)}, u32[]{:S(2)}) collective-permute-start(f32[1,12,32,256]{3,2,1,0:T(8,128)S(1)} %dynamic-slice_add_fusion.2), channel_id=1, source_target_pairs={{0,4},{1,5},{2,6},{3,7},{4,0},{5,1},{6,2},{7,3},{8,12},{9,13},{10,... | collective-permute-start | bytes 1179656 | tf_op jit(solution)/shard_map/ppermute | solution.py:253
  128.5 27.3 %collective-permute-start.29 = (f32[2,12,32,256]{3,2,1,0:T(8,128)}, f32[2,12,32,256]{3,2,1,0:T(8,128)S(1)}, u32[]{:S(2)}, u32[]{:S(2)}) collective-permute-start(f32[2,12,32,256]{3,2,1,0:T(8,128)} %get-tuple-element.289), channel_id=1, source_target_pairs={{0,2},{1,3},{2,0},{3,1},{4,6},{5,7},{6,4},{7,5},{8,10},{9,11},{10,... | collective-permute-start | bytes 2359304 | tf_op jit(solution)/shard_map/ppermute | solution.py:253
  129.4 24.7 %collective-permute-start.28 = (f32[1,12,32,256]{3,2,1,0:T(8,128)S(1)}, f32[1,12,32,256]{3,2,1,0:T(8,128)S(1)}, u32[]{:S(2)}, u32[]{:S(2)}) collective-permute-start(f32[1,12,32,256]{3,2,1,0:T(8,128)S(1)} %dynamic-slice_add_fusion.1), channel_id=1, source_target_pairs={{0,4},{1,5},{2,6},{3,7},{4,0},{5,1},{6,2},{7,3},{8,12},{9,13},{10,... | collective-permute-start | bytes 1179656 | tf_op jit(solution)/shard_map/ppermute | solution.py:253
  156.0 20.8 %collective-permute-start.30 = (f32[1,12,32,256]{3,2,1,0:T(8,128)S(1)}, f32[1,12,32,256]{3,2,1,0:T(8,128)S(1)}, u32[]{:S(2)}, u32[]{:S(2)}) collective-permute-start(f32[1,12,32,256]{3,2,1,0:T(8,128)S(1)} %dynamic-slice_add_fusion), channel_id=1, source_target_pairs={{0,4},{1,5},{2,6},{3,7},{4,0},{5,1},{6,2},{7,3},{8,12},{9,13},{10,... | collective-permute-start | bytes 1179656 | tf_op jit(solution)/shard_map/ppermute | solution.py:253
  196.2 11.3 %collective-permute-start.47 = (f32[4,32,256]{2,1,0:T(8,128)S(1)}, f32[4,32,256]{2,1,0:T(8,128)S(1)}, u32[]{:S(2)}, u32[]{:S(2)}) collective-permute-start(f32[4,32,256]{2,1,0:T(8,128)S(1)} %add_add_fusion.1), channel_id=1, source_target_pairs={{0,4},{1,5},{2,6},{3,7},{4,0},{5,1},{6,2},{7,3},{8,12},{9,13},{10,... | collective-permute-start | bytes 393224 | tf_op jit(solution)/shard_map/ppermute | solution.py:253
  197.2 10.9 %collective-permute-start.48 = (f32[4,32,256]{2,1,0:T(8,128)S(1)}, f32[4,32,256]{2,1,0:T(8,128)S(1)}, u32[]{:S(2)}, u32[]{:S(2)}) collective-permute-start(f32[4,32,256]{2,1,0:T(8,128)S(1)} %add_add_fusion.1), channel_id=1, source_target_pairs={{0,6},{1,7},{2,4},{3,5},{4,2},{5,3},{6,0},{7,1},{8,14},{9,15},{10,... | collective-permute-start | bytes 393224 | tf_op jit(solution)/shard_map/ppermute | solution.py:253
  199.8 11.3 %collective-permute-start.42 = (f32[2,32,256]{2,1,0:T(8,128)S(1)}, f32[2,32,256]{2,1,0:T(8,128)S(1)}, u32[]{:S(2)}, u32[]{:S(2)}) collective-permute-start(f32[2,32,256]{2,1,0:T(8,128)S(1)} %add_add_fusion.2), channel_id=1, source_target_pairs={{0,24},{8,16},{16,8},{24,0},{1,25},{9,17},{17,9},{25,1},{2,26},{10... | collective-permute-start | bytes 196616 | tf_op jit(solution)/shard_map/ppermute | solution.py:250
  200.8 10.9 %collective-permute-start.43 = (f32[2,32,256]{2,1,0:T(8,128)S(1)}, f32[2,32,256]{2,1,0:T(8,128)S(1)}, u32[]{:S(2)}, u32[]{:S(2)}) collective-permute-start(f32[2,32,256]{2,1,0:T(8,128)S(1)} %add_add_fusion.2), channel_id=1, source_target_pairs={{0,16},{8,24},{16,0},{24,8},{1,17},{9,25},{17,1},{25,9},{2,18},{10... | collective-permute-start | bytes 196616 | tf_op jit(solution)/shard_map/ppermute | solution.py:250
  (60 other events, 446.8 us)

commit v4 on v3

--- a/solution.py
+++ b/solution.py
@@ -30,7 +30,7 @@
     return lax.dot_general(left, right, dimension_numbers=(dims, ((), ())), preferred_element_type=F32)
 
 
-def prepare_kernel(n, g, groups, second, ids, structure, block_slot, panel, dinv, table, packed, line, *rest):
+def prepare_kernel(n, g, groups, ids, structure, block_slot, panel, dinv, table, packed, *rest):
     pieces, gathered = rest[:-1], rest[-1]
     r, z, c = ids[0], ids[1], ids[2]
     node_count, slot_count, sub, width = panel.shape
@@ -67,8 +67,6 @@
             gathered[pl.ds(k * sub, sub), :] = jnp.where(k < count, panel[s, table[s, SLOT + k]], 0.0)
         rows = dot3(split(gathered[...]), split(dinv[s]), ((1,), (0,))).reshape(CAP, sub, width)
         packed[s] = rows
-        if s in second:
-            line[pl.ds((s - second[0]) * CAP, CAP)] = rows
         b, i = place[s]
         for k in range(n):
             part = rows[:, :piece]
@@ -256,20 +254,19 @@
         return lax.ppermute(x, "col", [(i * g + j, i * g + (j ^ k)) for i in range(n) for j in range(g)])
 
     out = pl.pallas_call(
-        functools.partial(prepare_kernel, n, g, groups, range(batches[0], batches[0] + batches[1])),
+        functools.partial(prepare_kernel, n, g, groups),
         out_shape=[
             jax.ShapeDtypeStruct((node_count, table_width), jnp.int32),
             jax.ShapeDtypeStruct((node_count, CAP, sub, width), F32),
-            jax.ShapeDtypeStruct((batches[1] * CAP, sub, width), F32),
         ]
         + [jax.ShapeDtypeStruct((count * CAP, piece, width), F32) for count in groups for _ in range(n)],
         in_specs=[smem, smem, smem, vmem, vmem],
-        out_specs=[smem] + [vmem] * (2 + n * len(groups)),
+        out_specs=[smem] + [vmem] * (1 + n * len(groups)),
         scratch_shapes=[pltpu.VMEM((CAP * sub, width), F32)],
         compiler_params=params,
         name="prepare",
     )(ids, structure, block_slot, panel, dinv)
-    table, packed, line, pieces = out[0], out[1], [out[2]], out[3:]
+    table, packed, pieces = out[0], out[1], out[2:]
 
     starts = [sum(batches[:b]) for b in range(len(batches))]
     halvings = n.bit_length() - 1

time: 221 us -> 221 us (level)
  Pallas kernels: 52.8 us -> 49.8 us
  waiting for transfers between devices: 85.6 us -> 88.6 us
    pallas_call x3, Pallas kernels: 32.2 us -> 29.2 us  [product_stage(): pl.pallas_call(functools.partial(product_kernel, n, g, start), out_shape=...]
    ppermute x18, waiting for transfers between devices: 63.2 us -> 66.1 us  [along_z(): lax.ppermute(x, 'col', [(i * g + j, (i ^ m) * g + j) for i in range(n) fo...]
  transfers between devices with their start and end apart: 53 -> 53, of which waited for: 24 -> 24; matrix products, arithmetic and copies ran while one was open for 3% -> 3% of each run, Pallas kernels for 20% -> 19%
where the time goes in v4:
time: 221 us; the launch traced here: 220 us
  waiting for transfers between devices  88.6 us (40%)
  starting transfers between devices  62.7 us (28%)
  Pallas kernels  49.8 us (23%)
  local copies, waits for them, and re-layouts  10.2 us (5%)
  other arithmetic  7.49 us (3%)
    ppermute x18, waiting for transfers between devices, along_z(): lax.ppermute(x, 'col', [(i * g + j, (i ^ m) * g + j) for i in range(n) fo...  66.1 us
    ppermute x27, starting transfers between devices, along_row(): return lax.ppermute(x, 'row', [(i, i ^ k) for i in range(n)])  32.1 us
    ppermute x18, starting transfers between devices, along_z(): lax.ppermute(x, 'col', [(i * g + j, (i ^ m) * g + j) for i in range(n) fo...  29.7 us
    pallas_call x3, Pallas kernels, product_stage(): pl.pallas_call(functools.partial(product_kernel, n, g, start), out_shape=...  29.2 us
    ppermute x27, waiting for transfers between devices, along_row(): return lax.ppermute(x, 'row', [(i, i ^ k) for i in range(n)])  18.7 us
    pallas_call x3, Pallas kernels, finish(): pl.pallas_call(functools.partial(finish_kernel, g, halvings, with_off, wi...  11.7 us
    unnamed x62, local copies, waits for them, and re-layouts  5.19 us
    squeeze x1, local copies, waits for them, and re-layouts, body(): lax.dynamic_index_in_dim(shared[k - 1], c ^ k, 2, keepdims=False)  4.91 us
  transfers between devices with their start and end apart: 53, of which 24 were waited for; matrix products, arithmetic and copies ran while one was open for 3% of the time, Pallas kernels for 19%

profile of v4, /device:TPU:0, one launch (start us, length us, event | category | flops | bytes accessed | tf_op | source)
XLA Modules:
  0.0 219.9 jit_solution(6606578091874567615)
XLA Ops:
  1.3 4.5 %prepare.1 = (s32[6,24]{1,0:T(8,128)}, f32[6,6,32,256]{3,2,1,0:T(8,128)}, f32[12,8,256]{2,1,0:T(8,128)}, f32[12,8,256]{2,1,0:T(8,128)}, f32[12,8,256]{2,1,0:T(8,...) custom-call(s32[3]{0:T(128)} %pad_add_fusion.ids, ...), custom_call_target="tpu_custom_call" | custom-call | tf_op jit(solution)/shard_map/prepare/pallas_call | solution.py:256
  5.8 3.0 %collective-permute-start = (f32[12,8,256]{2,1,0:T(8,128)}, f32[12,8,256]{2,1,0:T(8,128)S(1)}, u32[]{:S(2)}, u32[]{:S(2)}) collective-permute-start(f32[12,8,256]{2,1,0:T(8,128)} %get-tuple-element.174), channel_id=1, source_target_pairs={{0,8},{8,0},{16,24},{24,16},{1,9},{9,1},{17,25},{25,17},{2,10},{10... | collective-permute-start | bytes 294920 | tf_op jit(solution)/shard_map/ppermute | solution.py:248
  10.4 4.9 %dynamic-slice_bitcast_fusion = f32[8,4,32,1024]{3,2,1,0:T(8,128)} fusion(f32[8,4,2,32,1024]{4,3,2,1,0:T(8,128)} %bitcast.42, s32[]{:T(128)S(6)} %select_n.535), kind=kLoop, calls=%fused_computation | loop fusion | bytes 8388612 | tf_op jit(solution)/shard_map/jit(dynamic_index_in_dim)/squeeze | solution.py:446
  17.8 2.6 %collective-permute-start.4 = (f32[12,8,256]{2,1,0:T(8,128)S(1)}, f32[12,8,256]{2,1,0:T(8,128)S(1)}, u32[]{:S(2)}, u32[]{:S(2)}) collective-permute-start(f32[12,8,256]{2,1,0:T(8,128)S(1)} %get-tuple-element.193), channel_id=1, source_target_pairs={{0,4},{1,5},{2,6},{3,7},{4,0},{5,1},{6,2},{7,3},{8,12},{9,13},{10,... | collective-permute-start | bytes 294920 | tf_op jit(solution)/shard_map/ppermute | solution.py:251
  25.7 2.5 %collective-permute-start.5 = (f32[12,8,256]{2,1,0:T(8,128)S(1)}, f32[12,8,256]{2,1,0:T(8,128)S(1)}, u32[]{:S(2)}, u32[]{:S(2)}) collective-permute-start(f32[12,8,256]{2,1,0:T(8,128)S(1)} %get-tuple-element.194), channel_id=1, source_target_pairs={{0,6},{1,7},{2,4},{3,5},{4,2},{5,3},{6,0},{7,1},{8,14},{9,15},{10,... | collective-permute-start | bytes 294920 | tf_op jit(solution)/shard_map/ppermute | solution.py:251
  28.2 3.9 %collective-permute-done.5 = f32[12,8,256]{2,1,0:T(8,128)S(1)} collective-permute-done((f32[12,8,256]{2,1,0:T(8,128)S(1)}, f32[12,8,256]{2,1,0:T(8,128)S(1)}, u32[]{:S(2)}, u32[]{:S(2)}) %collective-permute-start.5) | collective-permute-done | bytes 98336 | tf_op jit(solution)/shard_map/ppermute | solution.py:251
  36.5 2.5 %collective-permute-start.14 = (f32[24,8,256]{2,1,0:T(8,128)S(1)}, f32[24,8,256]{2,1,0:T(8,128)S(1)}, u32[]{:S(2)}, u32[]{:S(2)}) collective-permute-start(f32[24,8,256]{2,1,0:T(8,128)S(1)} %get-tuple-element.212), channel_id=1, source_target_pairs={{0,4},{1,5},{2,6},{3,7},{4,0},{5,1},{6,2},{7,3},{8,12},{9,13},{10,... | collective-permute-start | bytes 589832 | tf_op jit(solution)/shard_map/ppermute | solution.py:251
  39.3 2.5 %collective-permute-start.15 = (f32[24,8,256]{2,1,0:T(8,128)S(1)}, f32[24,8,256]{2,1,0:T(8,128)S(1)}, u32[]{:S(2)}, u32[]{:S(2)}) collective-permute-start(f32[24,8,256]{2,1,0:T(8,128)S(1)} %get-tuple-element.213), channel_id=1, source_target_pairs={{0,6},{1,7},{2,4},{3,5},{4,2},{5,3},{6,0},{7,1},{8,14},{9,15},{10,... | collective-permute-start | bytes 589832 | tf_op jit(solution)/shard_map/ppermute | solution.py:251
  41.8 9.7 %collective-permute-done.14 = f32[24,8,256]{2,1,0:T(8,128)S(1)} collective-permute-done((f32[24,8,256]{2,1,0:T(8,128)S(1)}, f32[24,8,256]{2,1,0:T(8,128)S(1)}, u32[]{:S(2)}, u32[]{:S(2)}) %collective-permute-start.14) | collective-permute-done | bytes 196640 | tf_op jit(solution)/shard_map/ppermute | solution.py:251
  57.7 12.8 %product.3 = (f32[2,12,32,256]{3,2,1,0:T(8,128)}, f32[2,12,32,256]{3,2,1,0:T(8,128)}) custom-call(s32[3]{0:T(128)} %pad_add_fusion.ids, s32[6,24]{1,0:T(8,128)} %get-tuple-element.164.table, f32[8,4,2,32,1024]{4,3,2,1,0:T(8,128)} %bitcast.43, f32[8,4,32,1024]{3,2,1,0:T(8,128)} %collective-permute-done.9.rest_1_, f32[4,12,8,256]{3,2,1,0:T(8,128)} %copy-done.3, ...), custom_call_target="tpu_custom_call" | custom-call | flops 1 | bytes 1 | tf_op jit(solution)/shard_map/product/pallas_call | solution.py:296
  70.5 3.2 %collective-permute-done.18.rest_4_ = f32[4,12,8,256]{3,2,1,0:T(8,128)S(1)} collective-permute-done((f32[4,12,8,256]{3,2,1,0:T(8,128)S(1)}, f32[4,12,8,256]{3,2,1,0:T(8,128)S(1)}, u32[]{:S(2)}, u32[]{:S(2)}) %collective-permute-start.18) | collective-permute-done | bytes 393248 | tf_op jit(solution)/shard_map/ppermute | solution.py:248
  75.3 3.7 %collective-permute-start.20 = (f32[2,12,32,256]{3,2,1,0:T(8,128)}, f32[2,12,32,256]{3,2,1,0:T(8,128)S(1)}, u32[]{:S(2)}, u32[]{:S(2)}) collective-permute-start(f32[2,12,32,256]{3,2,1,0:T(8,128)} %get-tuple-element.248), channel_id=1, source_target_pairs={{0,2},{1,3},{2,0},{3,1},{4,6},{5,7},{6,4},{7,5},{8,10},{9,11},{10,... | collective-permute-start | bytes 2359304 | tf_op jit(solution)/shard_map/ppermute | solution.py:251
  82.5 7.2 %product.4 = (f32[2,12,32,256]{3,2,1,0:T(8,128)}, f32[2,12,32,256]{3,2,1,0:T(8,128)}) custom-call(s32[3]{0:T(128)} %pad_add_fusion.ids, s32[6,24]{1,0:T(8,128)} %get-tuple-element.164.table, f32[8,4,2,32,1024]{4,3,2,1,0:T(8,128)} %bitcast.44, f32[8,4,32,1024]{3,2,1,0:T(8,128)} %collective-permute-done.9.rest_1_, f32[4,12,8,256]{3,2,1,0:T(8,128)} %copy-done.2, ...), custom_call_target="tpu_custom_call" | custom-call | flops 1 | bytes 1 | tf_op jit(solution)/shard_map/product/pallas_call | solution.py:296
  91.0 7.9 %collective-permute-done.23.rest_4_ = f32[4,12,8,256]{3,2,1,0:T(8,128)S(1)} collective-permute-done((f32[4,12,8,256]{3,2,1,0:T(8,128)S(1)}, f32[4,12,8,256]{3,2,1,0:T(8,128)S(1)}, u32[]{:S(2)}, u32[]{:S(2)}) %collective-permute-start.23) | collective-permute-done | bytes 393248 | tf_op jit(solution)/shard_map/ppermute | solution.py:248
  100.9 2.3 %collective-permute-start.25 = (f32[1,12,32,256]{3,2,1,0:T(8,128)S(1)}, f32[1,12,32,256]{3,2,1,0:T(8,128)S(1)}, u32[]{:S(2)}, u32[]{:S(2)}) collective-permute-start(f32[1,12,32,256]{3,2,1,0:T(8,128)S(1)} %dynamic-slice_add_fusion.2), channel_id=1, source_target_pairs={{0,4},{1,5},{2,6},{3,7},{4,0},{5,1},{6,2},{7,3},{8,12},{9,13},{10,... | collective-permute-start | bytes 1179656 | tf_op jit(solution)/shard_map/ppermute | solution.py:251
  104.6 9.1 %product.5 = (f32[2,12,32,256]{3,2,1,0:T(8,128)}, f32[2,12,32,256]{3,2,1,0:T(8,128)}) custom-call(s32[3]{0:T(128)} %pad_add_fusion.ids, s32[6,24]{1,0:T(8,128)} %get-tuple-element.164.table, f32[8,4,2,32,1024]{4,3,2,1,0:T(8,128)} %bitcast.45, f32[8,4,32,1024]{3,2,1,0:T(8,128)} %collective-permute-done.9.rest_1_, f32[4,12,8,256]{3,2,1,0:T(8,128)} %copy-done.4, ...), custom_call_target="tpu_custom_call" | custom-call | flops 1 | bytes 1 | tf_op jit(solution)/shard_map/product/pallas_call | solution.py:296
  113.8 12.5 %collective-permute-done.25.rest_1_ = f32[1,12,32,256]{3,2,1,0:T(8,128)S(1)} collective-permute-done((f32[1,12,32,256]{3,2,1,0:T(8,128)S(1)}, f32[1,12,32,256]{3,2,1,0:T(8,128)S(1)}, u32[]{:S(2)}, u32[]{:S(2)}) %collective-permute-start.25) | collective-permute-done | bytes 393248 | tf_op jit(solution)/shard_map/ppermute | solution.py:251
  131.2 4.4 %finish.3 = (f32[6,8,32,256]{3,2,1,0:T(8,128)}, f32[2,128,256]{2,1,0:T(8,128)}, f32[2,128,256]{2,1,0:T(8,128)}) custom-call(s32[3]{0:T(128)} %pad_add_fusion.ids, s32[6,24]{1,0:T(8,128)} %get-tuple-element.164.table, f32[2,12,32,256]{3,2,1,0:T(8,128)} %get-tuple-element.290.base, f32[2,12,32,256]{3,2,1,0:T(8,128)} %copy-done.8, ...), custom_call_target="tpu_custom_call" | custom-call | flops 1 | bytes 1 | tf_op jit(solution)/shard_map/finish/pallas_call | solution.py:383
  135.5 18.6 %collective-permute-done.28.rest_1_ = f32[1,12,32,256]{3,2,1,0:T(8,128)S(1)} collective-permute-done((f32[1,12,32,256]{3,2,1,0:T(8,128)S(1)}, f32[1,12,32,256]{3,2,1,0:T(8,128)S(1)}, u32[]{:S(2)}, u32[]{:S(2)}) %collective-permute-start.28) | collective-permute-done | bytes 393248 | tf_op jit(solution)/shard_map/ppermute | solution.py:251
  162.4 4.3 %finish.4 = (f32[6,8,32,256]{3,2,1,0:T(8,128)}, f32[2,128,256]{2,1,0:T(8,128)}, f32[2,128,256]{2,1,0:T(8,128)}) custom-call(s32[3]{0:T(128)} %pad_add_fusion.ids, s32[6,24]{1,0:T(8,128)} %get-tuple-element.164.table, f32[2,12,32,256]{3,2,1,0:T(8,128)} %get-tuple-element.308.base, f32[2,12,32,256]{3,2,1,0:T(8,128)} %copy-done.7, ...), custom_call_target="tpu_custom_call", output_to_operand_aliasing={{0}: (7, {})} | custom-call | flops 1 | bytes 1 | tf_op jit(solution)/shard_map/finish/pallas_call | solution.py:383
  166.7 10.1 %collective-permute-done.30.rest_1_ = f32[1,12,32,256]{3,2,1,0:T(8,128)S(1)} collective-permute-done((f32[1,12,32,256]{3,2,1,0:T(8,128)S(1)}, f32[1,12,32,256]{3,2,1,0:T(8,128)S(1)}, u32[]{:S(2)}, u32[]{:S(2)}) %collective-permute-start.30) | collective-permute-done | bytes 393248 | tf_op jit(solution)/shard_map/ppermute | solution.py:251
  177.6 4.4 %last_diag.1 = (f32[2,128,256]{2,1,0:T(8,128)}, f32[2,128,256]{2,1,0:T(8,128)}) custom-call(s32[3]{0:T(128)} %pad_add_fusion.ids, f32[2,12,32,256]{3,2,1,0:T(8,128)} %get-tuple-element.316.base, f32[2,12,32,256]{3,2,1,0:T(8,128)} %copy-done.1, f32[1,12,32,256]{3,2,1,0:T(8,128)} %copy-done.9, f32[6,6,32,256]{3,2,1,0:T(8,128)} %get-tuple-element.293.rest_2_, ...), custom_call_target="tpu_custom_call" | custom-call | flops 1 | bytes 1 | tf_op jit(solution)/shard_map/last_diag/pallas_call | solution.py:409
  190.9 3.1 %finish.5 = f32[6,8,32,256]{3,2,1,0:T(8,128)} custom-call(s32[3]{0:T(128)} %pad_add_fusion.ids, s32[6,24]{1,0:T(8,128)} %get-tuple-element.164.table, f32[2,12,32,256]{3,2,1,0:T(8,128)} %get-tuple-element.316.base, f32[2,12,32,256]{3,2,1,0:T(8,128)} %copy-done.1, f32[1,12,32,256]{3,2,1,0:T(8,128)} %copy-done.9, ...), custom_call_target="tpu_custom_call", output_to_operand_aliasing={{}: (7, {})} | custom-call | flops 1 | bytes 1 | tf_op jit(solution)/shard_map/finish/pallas_call | solution.py:383
  202.1 5.4 %collective-permute-done.47 = f32[4,32,256]{2,1,0:T(8,128)S(1)} collective-permute-done((f32[4,32,256]{2,1,0:T(8,128)S(1)}, f32[4,32,256]{2,1,0:T(8,128)S(1)}, u32[]{:S(2)}, u32[]{:S(2)}) %collective-permute-start.47) | collective-permute-done | bytes 131104 | tf_op jit(solution)/shard_map/ppermute | solution.py:251
  (186 shorter events, 73.6 us)
Async XLA Ops:
  16.1 16.2 %collective-permute-start.9 = (f32[8,4,32,1024]{3,2,1,0:T(8,128)}, f32[8,4,32,1024]{3,2,1,0:T(8,128)}, u32[]{:S(2)}, u32[]{:S(2)}) collective-permute-start(f32[8,4,32,1024]{3,2,1,0:T(8,128)} %dynamic-slice_bitcast_fusion), channel_id=1, source_target_pairs={{0,1},{1,0},{2,3},{3,2},{4,5},{5,4},{6,7},{7,6},{8,9},{9,8},{10,11... | collective-permute-start | bytes 12582920 | tf_op jit(solution)/shard_map/ppermute | solution.py:254
  20.4 11.7 %collective-permute-start.6 = (f32[24,8,256]{2,1,0:T(8,128)S(1)}, f32[24,8,256]{2,1,0:T(8,128)S(1)}, u32[]{:S(2)}, u32[]{:S(2)}) collective-permute-start(f32[24,8,256]{2,1,0:T(8,128)S(1)} %copy-done.30), channel_id=1, source_target_pairs={{0,8},{8,0},{16,24},{24,16},{1,9},{9,1},{17,25},{25,17},{2,10},{10... | collective-permute-start | bytes 589832 | tf_op jit(solution)/shard_map/ppermute | solution.py:248
  21.6 10.6 %collective-permute-start.7 = (f32[24,8,256]{2,1,0:T(8,128)S(1)}, f32[24,8,256]{2,1,0:T(8,128)S(1)}, u32[]{:S(2)}, u32[]{:S(2)}) collective-permute-start(f32[24,8,256]{2,1,0:T(8,128)S(1)} %copy-done.29), channel_id=1, source_target_pairs={{0,16},{8,24},{16,0},{24,8},{1,17},{9,25},{17,1},{25,9},{2,18},{10... | collective-permute-start | bytes 589832 | tf_op jit(solution)/shard_map/ppermute | solution.py:248
  33.0 18.5 %collective-permute-start.10 = (f32[4,12,8,256]{3,2,1,0:T(8,128)S(1)}, f32[4,12,8,256]{3,2,1,0:T(8,128)S(1)}, u32[]{:S(2)}, u32[]{:S(2)}) collective-permute-start(f32[4,12,8,256]{3,2,1,0:T(8,128)S(1)} %pad_maximum_fusion.5.rest_2_), channel_id=1, source_target_pairs={{0,8},{8,0},{16,24},{24,16},{1,9},{9,1},{17,25},{25,17},{2,10},{10... | collective-permute-start | bytes 1179656 | tf_op jit(solution)/shard_map/ppermute | solution.py:248
  34.2 17.9 %collective-permute-start.11 = (f32[4,12,8,256]{3,2,1,0:T(8,128)S(1)}, f32[4,12,8,256]{3,2,1,0:T(8,128)S(1)}, u32[]{:S(2)}, u32[]{:S(2)}) collective-permute-start(f32[4,12,8,256]{3,2,1,0:T(8,128)S(1)} %pad_maximum_fusion.5.rest_2_), channel_id=1, source_target_pairs={{0,16},{8,24},{16,0},{24,8},{1,17},{9,25},{17,1},{25,9},{2,18},{10... | collective-permute-start | bytes 1179656 | tf_op jit(solution)/shard_map/ppermute | solution.py:248
  35.2 16.9 %collective-permute-start.12 = (f32[4,12,8,256]{3,2,1,0:T(8,128)S(1)}, f32[4,12,8,256]{3,2,1,0:T(8,128)S(1)}, u32[]{:S(2)}, u32[]{:S(2)}) collective-permute-start(f32[4,12,8,256]{3,2,1,0:T(8,128)S(1)} %pad_maximum_fusion.5.rest_2_), channel_id=1, source_target_pairs={{0,24},{8,16},{16,8},{24,0},{1,25},{9,17},{17,9},{25,1},{2,26},{10... | collective-permute-start | bytes 1179656 | tf_op jit(solution)/shard_map/ppermute | solution.py:248
  36.5 15.0 %collective-permute-start.14 = (f32[24,8,256]{2,1,0:T(8,128)S(1)}, f32[24,8,256]{2,1,0:T(8,128)S(1)}, u32[]{:S(2)}, u32[]{:S(2)}) collective-permute-start(f32[24,8,256]{2,1,0:T(8,128)S(1)} %get-tuple-element.212), channel_id=1, source_target_pairs={{0,4},{1,5},{2,6},{3,7},{4,0},{5,1},{6,2},{7,3},{8,12},{9,13},{10,... | collective-permute-start | bytes 589832 | tf_op jit(solution)/shard_map/ppermute | solution.py:251
  39.3 12.2 %collective-permute-start.15 = (f32[24,8,256]{2,1,0:T(8,128)S(1)}, f32[24,8,256]{2,1,0:T(8,128)S(1)}, u32[]{:S(2)}, u32[]{:S(2)}) collective-permute-start(f32[24,8,256]{2,1,0:T(8,128)S(1)} %get-tuple-element.213), channel_id=1, source_target_pairs={{0,6},{1,7},{2,4},{3,5},{4,2},{5,3},{6,0},{7,1},{8,14},{9,15},{10,... | collective-permute-start | bytes 589832 | tf_op jit(solution)/shard_map/ppermute | solution.py:251
  53.0 17.5 %collective-permute-start.17 = (f32[4,12,8,256]{3,2,1,0:T(8,128)S(1)}, f32[4,12,8,256]{3,2,1,0:T(8,128)S(1)}, u32[]{:S(2)}, u32[]{:S(2)}) collective-permute-start(f32[4,12,8,256]{3,2,1,0:T(8,128)S(1)} %pad_maximum_fusion.6.rest_2_), channel_id=1, source_target_pairs={{0,8},{8,0},{16,24},{24,16},{1,9},{9,1},{17,25},{25,17},{2,10},{10... | collective-permute-start | bytes 1179656 | tf_op jit(solution)/shard_map/ppermute | solution.py:248
  54.0 19.7 %collective-permute-start.18 = (f32[4,12,8,256]{3,2,1,0:T(8,128)S(1)}, f32[4,12,8,256]{3,2,1,0:T(8,128)S(1)}, u32[]{:S(2)}, u32[]{:S(2)}) collective-permute-start(f32[4,12,8,256]{3,2,1,0:T(8,128)S(1)} %pad_maximum_fusion.6.rest_2_), channel_id=1, source_target_pairs={{0,16},{8,24},{16,0},{24,8},{1,17},{9,25},{17,1},{25,9},{2,18},{10... | collective-permute-start | bytes 1179656 | tf_op jit(solution)/shard_map/ppermute | solution.py:248
  55.2 18.5 %collective-permute-start.19 = (f32[4,12,8,256]{3,2,1,0:T(8,128)S(1)}, f32[4,12,8,256]{3,2,1,0:T(8,128)S(1)}, u32[]{:S(2)}, u32[]{:S(2)}) collective-permute-start(f32[4,12,8,256]{3,2,1,0:T(8,128)S(1)} %pad_maximum_fusion.6.rest_2_), channel_id=1, source_target_pairs={{0,24},{8,16},{16,8},{24,0},{1,25},{9,17},{17,9},{25,1},{2,26},{10... | collective-permute-start | bytes 1179656 | tf_op jit(solution)/shard_map/ppermute | solution.py:248
  75.3 23.6 %collective-permute-start.20 = (f32[2,12,32,256]{3,2,1,0:T(8,128)}, f32[2,12,32,256]{3,2,1,0:T(8,128)S(1)}, u32[]{:S(2)}, u32[]{:S(2)}) collective-permute-start(f32[2,12,32,256]{3,2,1,0:T(8,128)} %get-tuple-element.248), channel_id=1, source_target_pairs={{0,2},{1,3},{2,0},{3,1},{4,6},{5,7},{6,4},{7,5},{8,10},{9,11},{10,... | collective-permute-start | bytes 2359304 | tf_op jit(solution)/shard_map/ppermute | solution.py:251
  79.0 12.0 %collective-permute-start.22 = (f32[4,12,8,256]{3,2,1,0:T(8,128)S(1)}, f32[4,12,8,256]{3,2,1,0:T(8,128)S(1)}, u32[]{:S(2)}, u32[]{:S(2)}) collective-permute-start(f32[4,12,8,256]{3,2,1,0:T(8,128)S(1)} %pad_maximum_fusion.7.rest_2_), channel_id=1, source_target_pairs={{0,8},{8,0},{16,24},{24,16},{1,9},{9,1},{17,25},{25,17},{2,10},{10... | collective-permute-start | bytes 1179656 | tf_op jit(solution)/shard_map/ppermute | solution.py:248
  79.6 19.3 %collective-permute-start.23 = (f32[4,12,8,256]{3,2,1,0:T(8,128)S(1)}, f32[4,12,8,256]{3,2,1,0:T(8,128)S(1)}, u32[]{:S(2)}, u32[]{:S(2)}) collective-permute-start(f32[4,12,8,256]{3,2,1,0:T(8,128)S(1)} %pad_maximum_fusion.7.rest_2_), channel_id=1, source_target_pairs={{0,16},{8,24},{16,0},{24,8},{1,17},{9,25},{17,1},{25,9},{2,18},{10... | collective-permute-start | bytes 1179656 | tf_op jit(solution)/shard_map/ppermute | solution.py:248
  80.7 18.3 %collective-permute-start.24 = (f32[4,12,8,256]{3,2,1,0:T(8,128)S(1)}, f32[4,12,8,256]{3,2,1,0:T(8,128)S(1)}, u32[]{:S(2)}, u32[]{:S(2)}) collective-permute-start(f32[4,12,8,256]{3,2,1,0:T(8,128)S(1)} %pad_maximum_fusion.7.rest_2_), channel_id=1, source_target_pairs={{0,24},{8,16},{16,8},{24,0},{1,25},{9,17},{17,9},{25,1},{2,26},{10... | collective-permute-start | bytes 1179656 | tf_op jit(solution)/shard_map/ppermute | solution.py:248
  100.7 27.8 %collective-permute-start.26 = (f32[2,12,32,256]{3,2,1,0:T(8,128)S(1)}, f32[2,12,32,256]{3,2,1,0:T(8,128)S(1)}, u32[]{:S(2)}, u32[]{:S(2)}) collective-permute-start(f32[2,12,32,256]{3,2,1,0:T(8,128)S(1)} %copy-done.27), channel_id=1, source_target_pairs={{0,2},{1,3},{2,0},{3,1},{4,6},{5,7},{6,4},{7,5},{8,10},{9,11},{10,... | collective-permute-start | bytes 2359304 | tf_op jit(solution)/shard_map/ppermute | solution.py:251
  100.9 25.4 %collective-permute-start.25 = (f32[1,12,32,256]{3,2,1,0:T(8,128)S(1)}, f32[1,12,32,256]{3,2,1,0:T(8,128)S(1)}, u32[]{:S(2)}, u32[]{:S(2)}) collective-permute-start(f32[1,12,32,256]{3,2,1,0:T(8,128)S(1)} %dynamic-slice_add_fusion.2), channel_id=1, source_target_pairs={{0,4},{1,5},{2,6},{3,7},{4,0},{5,1},{6,2},{7,3},{8,12},{9,13},{10,... | collective-permute-start | bytes 1179656 | tf_op jit(solution)/shard_map/ppermute | solution.py:251
  128.5 27.3 %collective-permute-start.29 = (f32[2,12,32,256]{3,2,1,0:T(8,128)}, f32[2,12,32,256]{3,2,1,0:T(8,128)S(1)}, u32[]{:S(2)}, u32[]{:S(2)}) collective-permute-start(f32[2,12,32,256]{3,2,1,0:T(8,128)} %get-tuple-element.289), channel_id=1, source_target_pairs={{0,2},{1,3},{2,0},{3,1},{4,6},{5,7},{6,4},{7,5},{8,10},{9,11},{10,... | collective-permute-start | bytes 2359304 | tf_op jit(solution)/shard_map/ppermute | solution.py:251
  129.4 24.7 %collective-permute-start.28 = (f32[1,12,32,256]{3,2,1,0:T(8,128)S(1)}, f32[1,12,32,256]{3,2,1,0:T(8,128)S(1)}, u32[]{:S(2)}, u32[]{:S(2)}) collective-permute-start(f32[1,12,32,256]{3,2,1,0:T(8,128)S(1)} %dynamic-slice_add_fusion.1), channel_id=1, source_target_pairs={{0,4},{1,5},{2,6},{3,7},{4,0},{5,1},{6,2},{7,3},{8,12},{9,13},{10,... | collective-permute-start | bytes 1179656 | tf_op jit(solution)/shard_map/ppermute | solution.py:251
  156.0 20.8 %collective-permute-start.30 = (f32[1,12,32,256]{3,2,1,0:T(8,128)S(1)}, f32[1,12,32,256]{3,2,1,0:T(8,128)S(1)}, u32[]{:S(2)}, u32[]{:S(2)}) collective-permute-start(f32[1,12,32,256]{3,2,1,0:T(8,128)S(1)} %dynamic-slice_add_fusion), channel_id=1, source_target_pairs={{0,4},{1,5},{2,6},{3,7},{4,0},{5,1},{6,2},{7,3},{8,12},{9,13},{10,... | collective-permute-start | bytes 1179656 | tf_op jit(solution)/shard_map/ppermute | solution.py:251
  196.2 11.3 %collective-permute-start.47 = (f32[4,32,256]{2,1,0:T(8,128)S(1)}, f32[4,32,256]{2,1,0:T(8,128)S(1)}, u32[]{:S(2)}, u32[]{:S(2)}) collective-permute-start(f32[4,32,256]{2,1,0:T(8,128)S(1)} %add_add_fusion.1), channel_id=1, source_target_pairs={{0,4},{1,5},{2,6},{3,7},{4,0},{5,1},{6,2},{7,3},{8,12},{9,13},{10,... | collective-permute-start | bytes 393224 | tf_op jit(solution)/shard_map/ppermute | solution.py:251
  197.2 10.9 %collective-permute-start.48 = (f32[4,32,256]{2,1,0:T(8,128)S(1)}, f32[4,32,256]{2,1,0:T(8,128)S(1)}, u32[]{:S(2)}, u32[]{:S(2)}) collective-permute-start(f32[4,32,256]{2,1,0:T(8,128)S(1)} %add_add_fusion.1), channel_id=1, source_target_pairs={{0,6},{1,7},{2,4},{3,5},{4,2},{5,3},{6,0},{7,1},{8,14},{9,15},{10,... | collective-permute-start | bytes 393224 | tf_op jit(solution)/shard_map/ppermute | solution.py:251
  199.8 11.3 %collective-permute-start.42 = (f32[2,32,256]{2,1,0:T(8,128)S(1)}, f32[2,32,256]{2,1,0:T(8,128)S(1)}, u32[]{:S(2)}, u32[]{:S(2)}) collective-permute-start(f32[2,32,256]{2,1,0:T(8,128)S(1)} %add_add_fusion.2), channel_id=1, source_target_pairs={{0,24},{8,16},{16,8},{24,0},{1,25},{9,17},{17,9},{25,1},{2,26},{10... | collective-permute-start | bytes 196616 | tf_op jit(solution)/shard_map/ppermute | solution.py:248
  200.8 10.9 %collective-permute-start.43 = (f32[2,32,256]{2,1,0:T(8,128)S(1)}, f32[2,32,256]{2,1,0:T(8,128)S(1)}, u32[]{:S(2)}, u32[]{:S(2)}) collective-permute-start(f32[2,32,256]{2,1,0:T(8,128)S(1)} %add_add_fusion.2), channel_id=1, source_target_pairs={{0,16},{8,24},{16,0},{24,8},{1,17},{9,25},{17,1},{25,9},{2,18},{10... | collective-permute-start | bytes 196616 | tf_op jit(solution)/shard_map/ppermute | solution.py:248
  (60 other events, 445.9 us)

commit v5 on v4

--- a/solution.py
+++ b/solution.py
@@ -442,9 +442,9 @@
             state[b] = stages[stage][1](b, state[b])
         for group, stage in now_crossing:
             crossing[group] = cross_stages[stage][1](group, crossing[group])
-        if phase == 0:
+        if phase == 1:
             shared = [lax.dynamic_index_in_dim(shared[k - 1], c ^ k, 2, keepdims=False) for k in range(1, g)]
-        elif phase == 1:
+        elif phase == 2:
             shared = [along_core(shared[k - 1], k) for k in range(1, g)]
         if done == 0:
             off, shares = finish(0, None, True, True)

time: 221 us -> 223 us (level)
  waiting for transfers between devices: 88.6 us -> 107 us
  Pallas kernels: 49.8 us -> 41.8 us
  starting transfers between devices: 62.7 us -> 55 us
    ppermute x27, waiting for transfers between devices: 18.7 us -> 35.9 us  [along_row(): return lax.ppermute(x, 'row', [(i, i ^ k) for i in range(n)])]
    pallas_call x3, Pallas kernels: 29.2 us -> 21.3 us  [product_stage(): pl.pallas_call(functools.partial(product_kernel, n, g, start), out_shape=...]
    ppermute x18, starting transfers between devices: 29.7 us -> 23 us  [along_z(): lax.ppermute(x, 'col', [(i * g + j, (i ^ m) * g + j) for i in range(n) fo...]
    squeeze x1, local copies, waits for them, and re-layouts: 4.91 us -> 2.5 us  [body(): lax.dynamic_index_in_dim(shared[k - 1], c ^ k, 2, keepdims=False)]
    unnamed x62 -> x64, local copies, waits for them, and re-layouts: 5.19 us -> 6.29 us
  transfers between devices with their start and end apart: 53 -> 53, of which waited for: 24 -> 28; matrix products, arithmetic and copies ran while one was open for 3% -> 2% of each run, Pallas kernels for 19% -> 15%
where the time goes in v5:
time: 223 us
  waiting for transfers between devices  107 us (48%)
  starting transfers between devices  55 us (25%)
  Pallas kernels  41.8 us (19%)
  local copies, waits for them, and re-layouts  8.86 us (4%)
  other arithmetic  8.35 us (4%)
    ppermute x18, waiting for transfers between devices, along_z(): lax.ppermute(x, 'col', [(i * g + j, (i ^ m) * g + j) for i in range(n) fo...  66.3 us
    ppermute x27, waiting for transfers between devices, along_row(): return lax.ppermute(x, 'row', [(i, i ^ k) for i in range(n)])  35.9 us
    ppermute x27, starting transfers between devices, along_row(): return lax.ppermute(x, 'row', [(i, i ^ k) for i in range(n)])  31.1 us
    ppermute x18, starting transfers between devices, along_z(): lax.ppermute(x, 'col', [(i * g + j, (i ^ m) * g + j) for i in range(n) fo...  23 us
    pallas_call x3, Pallas kernels, product_stage(): pl.pallas_call(functools.partial(product_kernel, n, g, start), out_shape=...  21.3 us
    pallas_call x3, Pallas kernels, finish(): pl.pallas_call(functools.partial(finish_kernel, g, halvings, with_off, wi...  11.7 us
    unnamed x64, local copies, waits for them, and re-layouts  6.29 us
    ppermute x8, waiting for transfers between devices, along_core(): lax.ppermute(x, 'col', [(i * g + j, i * g + (j ^ k)) for i in range(n) fo...  5.12 us
  transfers between devices with their start and end apart: 53, of which 28 were waited for; matrix products, arithmetic and copies ran while one was open for 2% of the time, Pallas kernels for 15%

profile of v5, /device:TPU:0, one launch (start us, length us, event | category | flops | bytes accessed | tf_op | source)
XLA Modules:
  0.0 222.6 jit_solution(14653414645615319346)
XLA Ops:
  1.3 4.5 %prepare.1 = (s32[6,24]{1,0:T(8,128)}, f32[6,6,32,256]{3,2,1,0:T(8,128)}, f32[12,8,256]{2,1,0:T(8,128)}, f32[12,8,256]{2,1,0:T(8,128)}, f32[12,8,256]{2,1,0:T(8,...) custom-call(s32[3]{0:T(128)} %pad_add_fusion.ids, ...), custom_call_target="tpu_custom_call" | custom-call | tf_op jit(solution)/shard_map/prepare/pallas_call | solution.py:256
  5.8 3.0 %collective-permute-start = (f32[12,8,256]{2,1,0:T(8,128)}, f32[12,8,256]{2,1,0:T(8,128)S(1)}, u32[]{:S(2)}, u32[]{:S(2)}) collective-permute-start(f32[12,8,256]{2,1,0:T(8,128)} %get-tuple-element.174), channel_id=1, source_target_pairs={{0,8},{8,0},{16,24},{24,16},{1,9},{9,1},{17,25},{25,17},{2,10},{10... | collective-permute-start | bytes 294920 | tf_op jit(solution)/shard_map/ppermute | solution.py:248
  12.1 2.5 %collective-permute-done.1 = f32[12,8,256]{2,1,0:T(8,128)S(1)} collective-permute-done((f32[12,8,256]{2,1,0:T(8,128)}, f32[12,8,256]{2,1,0:T(8,128)S(1)}, u32[]{:S(2)}, u32[]{:S(2)}) %collective-permute-start.1) | collective-permute-done | bytes 98336 | tf_op jit(solution)/shard_map/ppermute | solution.py:248
  18.6 2.6 %collective-permute-start.4 = (f32[12,8,256]{2,1,0:T(8,128)S(1)}, f32[12,8,256]{2,1,0:T(8,128)S(1)}, u32[]{:S(2)}, u32[]{:S(2)}) collective-permute-start(f32[12,8,256]{2,1,0:T(8,128)S(1)} %get-tuple-element.193), channel_id=1, source_target_pairs={{0,4},{1,5},{2,6},{3,7},{4,0},{5,1},{6,2},{7,3},{8,12},{9,13},{10,... | collective-permute-start | bytes 294920 | tf_op jit(solution)/shard_map/ppermute | solution.py:251
  24.9 2.5 %dynamic-slice_bitcast_fusion = f32[8,4,32,1024]{3,2,1,0:T(8,128)S(1)} fusion(f32[8,4,2,32,1024]{4,3,2,1,0:T(8,128)} %bitcast.42, s32[]{:T(128)S(6)} %select_n.558), kind=kLoop, calls=%fused_computation | loop fusion | bytes 8388612 | tf_op jit(solution)/shard_map/jit(dynamic_index_in_dim)/squeeze | solution.py:446
  28.3 3.0 %collective-permute-done.7 = f32[24,8,256]{2,1,0:T(8,128)S(1)} collective-permute-done((f32[24,8,256]{2,1,0:T(8,128)}, f32[24,8,256]{2,1,0:T(8,128)S(1)}, u32[]{:S(2)}, u32[]{:S(2)}) %collective-permute-start.7) | collective-permute-done | bytes 196640 | tf_op jit(solution)/shard_map/ppermute | solution.py:248
  32.3 3.5 %collective-permute-start.13 = (f32[24,8,256]{2,1,0:T(8,128)S(1)}, f32[24,8,256]{2,1,0:T(8,128)S(1)}, u32[]{:S(2)}, u32[]{:S(2)}) collective-permute-start(f32[24,8,256]{2,1,0:T(8,128)S(1)} %get-tuple-element.212), channel_id=1, source_target_pairs={{0,4},{1,5},{2,6},{3,7},{4,0},{5,1},{6,2},{7,3},{8,12},{9,13},{10,... | collective-permute-start | bytes 589832 | tf_op jit(solution)/shard_map/ppermute | solution.py:251
  37.9 5.0 %collective-permute-done.12 = f32[24,8,256]{2,1,0:T(8,128)S(1)} collective-permute-done((f32[24,8,256]{2,1,0:T(8,128)S(1)}, f32[24,8,256]{2,1,0:T(8,128)S(1)}, u32[]{:S(2)}, u32[]{:S(2)}) %collective-permute-start.12) | collective-permute-done | bytes 196640 | tf_op jit(solution)/shard_map/ppermute | solution.py:251
  45.3 2.3 %collective-permute-start.14 = (f32[24,8,256]{2,1,0:T(8,128)S(1)}, f32[24,8,256]{2,1,0:T(8,128)S(1)}, u32[]{:S(2)}, u32[]{:S(2)}) collective-permute-start(f32[24,8,256]{2,1,0:T(8,128)S(1)} %get-tuple-element.213), channel_id=1, source_target_pairs={{0,6},{1,7},{2,4},{3,5},{4,2},{5,3},{6,0},{7,1},{8,14},{9,15},{10,... | collective-permute-start | bytes 589832 | tf_op jit(solution)/shard_map/ppermute | solution.py:251
  47.6 5.2 %collective-permute-done.14 = f32[24,8,256]{2,1,0:T(8,128)S(1)} collective-permute-done((f32[24,8,256]{2,1,0:T(8,128)S(1)}, f32[24,8,256]{2,1,0:T(8,128)S(1)}, u32[]{:S(2)}, u32[]{:S(2)}) %collective-permute-start.14) | collective-permute-done | bytes 196640 | tf_op jit(solution)/shard_map/ppermute | solution.py:251
  52.8 2.8 %collective-permute-done.10.rest_4_ = f32[4,12,8,256]{3,2,1,0:T(8,128)S(1)} collective-permute-done((f32[4,12,8,256]{3,2,1,0:T(8,128)S(1)}, f32[4,12,8,256]{3,2,1,0:T(8,128)S(1)}, u32[]{:S(2)}, u32[]{:S(2)}) %collective-permute-start.10) | collective-permute-done | bytes 393248 | tf_op jit(solution)/shard_map/ppermute | solution.py:248
  62.3 6.1 %product.3 = (f32[2,12,32,256]{3,2,1,0:T(8,128)}, f32[2,12,32,256]{3,2,1,0:T(8,128)}) custom-call(s32[3]{0:T(128)} %pad_add_fusion.ids, s32[6,24]{1,0:T(8,128)} %get-tuple-element.164.table, f32[8,4,2,32,1024]{4,3,2,1,0:T(8,128)} %bitcast.43, f32[8,4,32,1024]{3,2,1,0:T(8,128)} %copy-done, f32[4,12,8,256]{3,2,1,0:T(8,128)} %copy-done.3, ...), custom_call_target="tpu_custom_call" | custom-call | flops 1 | bytes 1 | tf_op jit(solution)/shard_map/product/pallas_call | solution.py:296
  69.5 9.1 %collective-permute-done.18.rest_4_ = f32[4,12,8,256]{3,2,1,0:T(8,128)S(1)} collective-permute-done((f32[4,12,8,256]{3,2,1,0:T(8,128)S(1)}, f32[4,12,8,256]{3,2,1,0:T(8,128)S(1)}, u32[]{:S(2)}, u32[]{:S(2)}) %collective-permute-start.18) | collective-permute-done | bytes 393248 | tf_op jit(solution)/shard_map/ppermute | solution.py:248
  84.2 9.1 %product.4 = (f32[2,12,32,256]{3,2,1,0:T(8,128)}, f32[2,12,32,256]{3,2,1,0:T(8,128)}) custom-call(s32[3]{0:T(128)} %pad_add_fusion.ids, s32[6,24]{1,0:T(8,128)} %get-tuple-element.164.table, f32[8,4,2,32,1024]{4,3,2,1,0:T(8,128)} %bitcast.44, f32[8,4,32,1024]{3,2,1,0:T(8,128)} %copy-done, f32[4,12,8,256]{3,2,1,0:T(8,128)} %copy-done.4, ...), custom_call_target="tpu_custom_call" | custom-call | flops 1 | bytes 1 | tf_op jit(solution)/shard_map/product/pallas_call | solution.py:296
  93.3 8.0 %collective-permute-done.23.rest_4_ = f32[4,12,8,256]{3,2,1,0:T(8,128)S(1)} collective-permute-done((f32[4,12,8,256]{3,2,1,0:T(8,128)S(1)}, f32[4,12,8,256]{3,2,1,0:T(8,128)S(1)}, u32[]{:S(2)}, u32[]{:S(2)}) %collective-permute-start.23) | collective-permute-done | bytes 393248 | tf_op jit(solution)/shard_map/ppermute | solution.py:248
  107.1 6.2 %product.5 = (f32[2,12,32,256]{3,2,1,0:T(8,128)}, f32[2,12,32,256]{3,2,1,0:T(8,128)}) custom-call(s32[3]{0:T(128)} %pad_add_fusion.ids, s32[6,24]{1,0:T(8,128)} %get-tuple-element.164.table, f32[8,4,2,32,1024]{4,3,2,1,0:T(8,128)} %bitcast.45, f32[8,4,32,1024]{3,2,1,0:T(8,128)} %copy-done, f32[4,12,8,256]{3,2,1,0:T(8,128)} %copy-done.5, ...), custom_call_target="tpu_custom_call" | custom-call | flops 1 | bytes 1 | tf_op jit(solution)/shard_map/product/pallas_call | solution.py:296
  113.2 16.2 %collective-permute-done.25.rest_1_ = f32[1,12,32,256]{3,2,1,0:T(8,128)S(1)} collective-permute-done((f32[1,12,32,256]{3,2,1,0:T(8,128)S(1)}, f32[1,12,32,256]{3,2,1,0:T(8,128)S(1)}, u32[]{:S(2)}, u32[]{:S(2)}) %collective-permute-start.25) | collective-permute-done | bytes 393248 | tf_op jit(solution)/shard_map/ppermute | solution.py:251
  133.1 4.3 %finish.3 = (f32[6,8,32,256]{3,2,1,0:T(8,128)}, f32[2,128,256]{2,1,0:T(8,128)}, f32[2,128,256]{2,1,0:T(8,128)}) custom-call(s32[3]{0:T(128)} %pad_add_fusion.ids, s32[6,24]{1,0:T(8,128)} %get-tuple-element.164.table, f32[2,12,32,256]{3,2,1,0:T(8,128)} %get-tuple-element.290.base, f32[2,12,32,256]{3,2,1,0:T(8,128)} %copy-done.9, ...), custom_call_target="tpu_custom_call" | custom-call | flops 1 | bytes 1 | tf_op jit(solution)/shard_map/finish/pallas_call | solution.py:383
  137.4 18.7 %collective-permute-done.28.rest_1_ = f32[1,12,32,256]{3,2,1,0:T(8,128)S(1)} collective-permute-done((f32[1,12,32,256]{3,2,1,0:T(8,128)S(1)}, f32[1,12,32,256]{3,2,1,0:T(8,128)S(1)}, u32[]{:S(2)}, u32[]{:S(2)}) %collective-permute-start.28) | collective-permute-done | bytes 393248 | tf_op jit(solution)/shard_map/ppermute | solution.py:251
  164.7 4.3 %finish.4 = (f32[6,8,32,256]{3,2,1,0:T(8,128)}, f32[2,128,256]{2,1,0:T(8,128)}, f32[2,128,256]{2,1,0:T(8,128)}) custom-call(s32[3]{0:T(128)} %pad_add_fusion.ids, s32[6,24]{1,0:T(8,128)} %get-tuple-element.164.table, f32[2,12,32,256]{3,2,1,0:T(8,128)} %get-tuple-element.308.base, f32[2,12,32,256]{3,2,1,0:T(8,128)} %copy-done.8, ...), custom_call_target="tpu_custom_call", output_to_operand_aliasing={{0}: (7, {})} | custom-call | flops 1 | bytes 1 | tf_op jit(solution)/shard_map/finish/pallas_call | solution.py:383
  169.0 10.2 %collective-permute-done.30.rest_1_ = f32[1,12,32,256]{3,2,1,0:T(8,128)S(1)} collective-permute-done((f32[1,12,32,256]{3,2,1,0:T(8,128)S(1)}, f32[1,12,32,256]{3,2,1,0:T(8,128)S(1)}, u32[]{:S(2)}, u32[]{:S(2)}) %collective-permute-start.30) | collective-permute-done | bytes 393248 | tf_op jit(solution)/shard_map/ppermute | solution.py:251
  180.0 4.3 %last_diag.1 = (f32[2,128,256]{2,1,0:T(8,128)}, f32[2,128,256]{2,1,0:T(8,128)}) custom-call(s32[3]{0:T(128)} %pad_add_fusion.ids, f32[2,12,32,256]{3,2,1,0:T(8,128)} %get-tuple-element.316.base, f32[2,12,32,256]{3,2,1,0:T(8,128)} %copy-done.2, f32[1,12,32,256]{3,2,1,0:T(8,128)} %copy-done.10, f32[6,6,32,256]{3,2,1,0:T(8,128)} %get-tuple-element.293.rest_2_, ...), custom_call_target="tpu_custom_call" | custom-call | flops 1 | bytes 1 | tf_op jit(solution)/shard_map/last_diag/pallas_call | solution.py:409
  193.0 3.1 %finish.5 = f32[6,8,32,256]{3,2,1,0:T(8,128)} custom-call(s32[3]{0:T(128)} %pad_add_fusion.ids, s32[6,24]{1,0:T(8,128)} %get-tuple-element.164.table, f32[2,12,32,256]{3,2,1,0:T(8,128)} %get-tuple-element.316.base, f32[2,12,32,256]{3,2,1,0:T(8,128)} %copy-done.2, f32[1,12,32,256]{3,2,1,0:T(8,128)} %copy-done.10, ...), custom_call_target="tpu_custom_call", output_to_operand_aliasing={{}: (7, {})} | custom-call | flops 1 | bytes 1 | tf_op jit(solution)/shard_map/finish/pallas_call | solution.py:383
  203.8 6.3 %collective-permute-done.47 = f32[4,32,256]{2,1,0:T(8,128)S(1)} collective-permute-done((f32[4,32,256]{2,1,0:T(8,128)S(1)}, f32[4,32,256]{2,1,0:T(8,128)S(1)}, u32[]{:S(2)}, u32[]{:S(2)}) %collective-permute-start.47) | collective-permute-done | bytes 131104 | tf_op jit(solution)/shard_map/ppermute | solution.py:251
  (188 shorter events, 78.6 us)
Async XLA Ops:
  31.5 24.0 %collective-permute-start.15 = (f32[8,4,32,1024]{3,2,1,0:T(8,128)S(1)}, f32[8,4,32,1024]{3,2,1,0:T(8,128)S(1)}, u32[]{:S(2)}, u32[]{:S(2)}) collective-permute-start(f32[8,4,32,1024]{3,2,1,0:T(8,128)S(1)} %dynamic-slice_bitcast_fusion), channel_id=1, source_target_pairs={{0,1},{1,0},{2,3},{3,2},{4,5},{5,4},{6,7},{7,6},{8,9},{9,8},{10,11... | collective-permute-start | bytes 12582920 | tf_op jit(solution)/shard_map/ppermute | solution.py:254
  31.6 11.3 %collective-permute-start.12 = (f32[24,8,256]{2,1,0:T(8,128)S(1)}, f32[24,8,256]{2,1,0:T(8,128)S(1)}, u32[]{:S(2)}, u32[]{:S(2)}) collective-permute-start(f32[24,8,256]{2,1,0:T(8,128)S(1)} %get-tuple-element.211), channel_id=1, source_target_pairs={{0,2},{1,3},{2,0},{3,1},{4,6},{5,7},{6,4},{7,5},{8,10},{9,11},{10,... | collective-permute-start | bytes 589832 | tf_op jit(solution)/shard_map/ppermute | solution.py:251
  32.3 13.0 %collective-permute-start.13 = (f32[24,8,256]{2,1,0:T(8,128)S(1)}, f32[24,8,256]{2,1,0:T(8,128)S(1)}, u32[]{:S(2)}, u32[]{:S(2)}) collective-permute-start(f32[24,8,256]{2,1,0:T(8,128)S(1)} %get-tuple-element.212), channel_id=1, source_target_pairs={{0,4},{1,5},{2,6},{3,7},{4,0},{5,1},{6,2},{7,3},{8,12},{9,13},{10,... | collective-permute-start | bytes 589832 | tf_op jit(solution)/shard_map/ppermute | solution.py:251
  35.8 17.0 %collective-permute-start.9 = (f32[4,12,8,256]{3,2,1,0:T(8,128)S(1)}, f32[4,12,8,256]{3,2,1,0:T(8,128)S(1)}, u32[]{:S(2)}, u32[]{:S(2)}) collective-permute-start(f32[4,12,8,256]{3,2,1,0:T(8,128)S(1)} %pad_maximum_fusion.5.rest_2_), channel_id=1, source_target_pairs={{0,8},{8,0},{16,24},{24,16},{1,9},{9,1},{17,25},{25,17},{2,10},{10... | collective-permute-start | bytes 1179656 | tf_op jit(solution)/shard_map/ppermute | solution.py:248
  36.5 19.1 %collective-permute-start.10 = (f32[4,12,8,256]{3,2,1,0:T(8,128)S(1)}, f32[4,12,8,256]{3,2,1,0:T(8,128)S(1)}, u32[]{:S(2)}, u32[]{:S(2)}) collective-permute-start(f32[4,12,8,256]{3,2,1,0:T(8,128)S(1)} %pad_maximum_fusion.5.rest_2_), channel_id=1, source_target_pairs={{0,16},{8,24},{16,0},{24,8},{1,17},{9,25},{17,1},{25,9},{2,18},{10... | collective-permute-start | bytes 1179656 | tf_op jit(solution)/shard_map/ppermute | solution.py:248
  42.9 12.7 %collective-permute-start.11 = (f32[4,12,8,256]{3,2,1,0:T(8,128)S(1)}, f32[4,12,8,256]{3,2,1,0:T(8,128)S(1)}, u32[]{:S(2)}, u32[]{:S(2)}) collective-permute-start(f32[4,12,8,256]{3,2,1,0:T(8,128)S(1)} %pad_maximum_fusion.5.rest_2_), channel_id=1, source_target_pairs={{0,24},{8,16},{16,8},{24,0},{1,25},{9,17},{17,9},{25,1},{2,26},{10... | collective-permute-start | bytes 1179656 | tf_op jit(solution)/shard_map/ppermute | solution.py:248
  57.6 11.9 %collective-permute-start.17 = (f32[4,12,8,256]{3,2,1,0:T(8,128)S(1)}, f32[4,12,8,256]{3,2,1,0:T(8,128)S(1)}, u32[]{:S(2)}, u32[]{:S(2)}) collective-permute-start(f32[4,12,8,256]{3,2,1,0:T(8,128)S(1)} %pad_maximum_fusion.6.rest_2_), channel_id=1, source_target_pairs={{0,8},{8,0},{16,24},{24,16},{1,9},{9,1},{17,25},{25,17},{2,10},{10... | collective-permute-start | bytes 1179656 | tf_op jit(solution)/shard_map/ppermute | solution.py:248
  58.9 19.7 %collective-permute-start.18 = (f32[4,12,8,256]{3,2,1,0:T(8,128)S(1)}, f32[4,12,8,256]{3,2,1,0:T(8,128)S(1)}, u32[]{:S(2)}, u32[]{:S(2)}) collective-permute-start(f32[4,12,8,256]{3,2,1,0:T(8,128)S(1)} %pad_maximum_fusion.6.rest_2_), channel_id=1, source_target_pairs={{0,16},{8,24},{16,0},{24,8},{1,17},{9,25},{17,1},{25,9},{2,18},{10... | collective-permute-start | bytes 1179656 | tf_op jit(solution)/shard_map/ppermute | solution.py:248
  59.5 19.1 %collective-permute-start.19 = (f32[4,12,8,256]{3,2,1,0:T(8,128)S(1)}, f32[4,12,8,256]{3,2,1,0:T(8,128)S(1)}, u32[]{:S(2)}, u32[]{:S(2)}) collective-permute-start(f32[4,12,8,256]{3,2,1,0:T(8,128)S(1)} %pad_maximum_fusion.6.rest_2_), channel_id=1, source_target_pairs={{0,24},{8,16},{16,8},{24,0},{1,25},{9,17},{17,9},{25,1},{2,26},{10... | collective-permute-start | bytes 1179656 | tf_op jit(solution)/shard_map/ppermute | solution.py:248
  80.2 21.1 %collective-permute-start.20 = (f32[2,12,32,256]{3,2,1,0:T(8,128)}, f32[2,12,32,256]{3,2,1,0:T(8,128)S(1)}, u32[]{:S(2)}, u32[]{:S(2)}) collective-permute-start(f32[2,12,32,256]{3,2,1,0:T(8,128)} %get-tuple-element.248), channel_id=1, source_target_pairs={{0,2},{1,3},{2,0},{3,1},{4,6},{5,7},{6,4},{7,5},{8,10},{9,11},{10,... | collective-permute-start | bytes 2359304 | tf_op jit(solution)/shard_map/ppermute | solution.py:251
  80.7 12.6 %collective-permute-start.22 = (f32[4,12,8,256]{3,2,1,0:T(8,128)S(1)}, f32[4,12,8,256]{3,2,1,0:T(8,128)S(1)}, u32[]{:S(2)}, u32[]{:S(2)}) collective-permute-start(f32[4,12,8,256]{3,2,1,0:T(8,128)S(1)} %pad_maximum_fusion.7.rest_2_), channel_id=1, source_target_pairs={{0,8},{8,0},{16,24},{24,16},{1,9},{9,1},{17,25},{25,17},{2,10},{10... | collective-permute-start | bytes 1179656 | tf_op jit(solution)/shard_map/ppermute | solution.py:248
  82.0 19.3 %collective-permute-start.23 = (f32[4,12,8,256]{3,2,1,0:T(8,128)S(1)}, f32[4,12,8,256]{3,2,1,0:T(8,128)S(1)}, u32[]{:S(2)}, u32[]{:S(2)}) collective-permute-start(f32[4,12,8,256]{3,2,1,0:T(8,128)S(1)} %pad_maximum_fusion.7.rest_2_), channel_id=1, source_target_pairs={{0,16},{8,24},{16,0},{24,8},{1,17},{9,25},{17,1},{25,9},{2,18},{10... | collective-permute-start | bytes 1179656 | tf_op jit(solution)/shard_map/ppermute | solution.py:248
  82.7 18.7 %collective-permute-start.24 = (f32[4,12,8,256]{3,2,1,0:T(8,128)S(1)}, f32[4,12,8,256]{3,2,1,0:T(8,128)S(1)}, u32[]{:S(2)}, u32[]{:S(2)}) collective-permute-start(f32[4,12,8,256]{3,2,1,0:T(8,128)S(1)} %pad_maximum_fusion.7.rest_2_), channel_id=1, source_target_pairs={{0,24},{8,16},{16,8},{24,0},{1,25},{9,17},{17,9},{25,1},{2,26},{10... | collective-permute-start | bytes 1179656 | tf_op jit(solution)/shard_map/ppermute | solution.py:248
  103.0 27.9 %collective-permute-start.26 = (f32[2,12,32,256]{3,2,1,0:T(8,128)S(1)}, f32[2,12,32,256]{3,2,1,0:T(8,128)S(1)}, u32[]{:S(2)}, u32[]{:S(2)}) collective-permute-start(f32[2,12,32,256]{3,2,1,0:T(8,128)S(1)} %copy-done.31), channel_id=1, source_target_pairs={{0,2},{1,3},{2,0},{3,1},{4,6},{5,7},{6,4},{7,5},{8,10},{9,11},{10,... | collective-permute-start | bytes 2359304 | tf_op jit(solution)/shard_map/ppermute | solution.py:251
  104.1 25.4 %collective-permute-start.25 = (f32[1,12,32,256]{3,2,1,0:T(8,128)S(1)}, f32[1,12,32,256]{3,2,1,0:T(8,128)S(1)}, u32[]{:S(2)}, u32[]{:S(2)}) collective-permute-start(f32[1,12,32,256]{3,2,1,0:T(8,128)S(1)} %dynamic-slice_add_fusion.2), channel_id=1, source_target_pairs={{0,4},{1,5},{2,6},{3,7},{4,0},{5,1},{6,2},{7,3},{8,12},{9,13},{10,... | collective-permute-start | bytes 1179656 | tf_op jit(solution)/shard_map/ppermute | solution.py:251
  130.9 27.3 %collective-permute-start.29 = (f32[2,12,32,256]{3,2,1,0:T(8,128)}, f32[2,12,32,256]{3,2,1,0:T(8,128)S(1)}, u32[]{:S(2)}, u32[]{:S(2)}) collective-permute-start(f32[2,12,32,256]{3,2,1,0:T(8,128)} %get-tuple-element.289), channel_id=1, source_target_pairs={{0,2},{1,3},{2,0},{3,1},{4,6},{5,7},{6,4},{7,5},{8,10},{9,11},{10,... | collective-permute-start | bytes 2359304 | tf_op jit(solution)/shard_map/ppermute | solution.py:251
  131.3 24.7 %collective-permute-start.28 = (f32[1,12,32,256]{3,2,1,0:T(8,128)S(1)}, f32[1,12,32,256]{3,2,1,0:T(8,128)S(1)}, u32[]{:S(2)}, u32[]{:S(2)}) collective-permute-start(f32[1,12,32,256]{3,2,1,0:T(8,128)S(1)} %dynamic-slice_add_fusion.1), channel_id=1, source_target_pairs={{0,4},{1,5},{2,6},{3,7},{4,0},{5,1},{6,2},{7,3},{8,12},{9,13},{10,... | collective-permute-start | bytes 1179656 | tf_op jit(solution)/shard_map/ppermute | solution.py:251
  158.4 20.8 %collective-permute-start.30 = (f32[1,12,32,256]{3,2,1,0:T(8,128)S(1)}, f32[1,12,32,256]{3,2,1,0:T(8,128)S(1)}, u32[]{:S(2)}, u32[]{:S(2)}) collective-permute-start(f32[1,12,32,256]{3,2,1,0:T(8,128)S(1)} %dynamic-slice_add_fusion), channel_id=1, source_target_pairs={{0,4},{1,5},{2,6},{3,7},{4,0},{5,1},{6,2},{7,3},{8,12},{9,13},{10,... | collective-permute-start | bytes 1179656 | tf_op jit(solution)/shard_map/ppermute | solution.py:251
  188.5 10.0 %collective-permute-start.38 = (f32[4,32,256]{2,1,0:T(8,128)S(1)}, f32[4,32,256]{2,1,0:T(8,128)S(1)}, u32[]{:S(2)}, u32[]{:S(2)}) collective-permute-start(f32[4,32,256]{2,1,0:T(8,128)S(1)} %get-tuple-element.347), channel_id=1, source_target_pairs={{0,24},{8,16},{16,8},{24,0},{1,25},{9,17},{17,9},{25,1},{2,26},{10... | collective-permute-start | bytes 393224 | tf_op jit(solution)/shard_map/ppermute | solution.py:248
  191.9 10.2 %collective-permute-start.41 = (f32[2,32,256]{2,1,0:T(8,128)S(1)}, f32[2,32,256]{2,1,0:T(8,128)S(1)}, u32[]{:S(2)}, u32[]{:S(2)}) collective-permute-start(f32[2,32,256]{2,1,0:T(8,128)S(1)} %add_add_fusion.3), channel_id=1, source_target_pairs={{0,6},{1,7},{2,4},{3,5},{4,2},{5,3},{6,0},{7,1},{8,14},{9,15},{10,... | collective-permute-start | bytes 196616 | tf_op jit(solution)/shard_map/ppermute | solution.py:251
  198.6 11.5 %collective-permute-start.47 = (f32[4,32,256]{2,1,0:T(8,128)S(1)}, f32[4,32,256]{2,1,0:T(8,128)S(1)}, u32[]{:S(2)}, u32[]{:S(2)}) collective-permute-start(f32[4,32,256]{2,1,0:T(8,128)S(1)} %add_add_fusion.1), channel_id=1, source_target_pairs={{0,4},{1,5},{2,6},{3,7},{4,0},{5,1},{6,2},{7,3},{8,12},{9,13},{10,... | collective-permute-start | bytes 393224 | tf_op jit(solution)/shard_map/ppermute | solution.py:251
  199.6 10.6 %collective-permute-start.48 = (f32[4,32,256]{2,1,0:T(8,128)S(1)}, f32[4,32,256]{2,1,0:T(8,128)S(1)}, u32[]{:S(2)}, u32[]{:S(2)}) collective-permute-start(f32[4,32,256]{2,1,0:T(8,128)S(1)} %add_add_fusion.1), channel_id=1, source_target_pairs={{0,6},{1,7},{2,4},{3,5},{4,2},{5,3},{6,0},{7,1},{8,14},{9,15},{10,... | collective-permute-start | bytes 393224 | tf_op jit(solution)/shard_map/ppermute | solution.py:251
  202.2 11.5 %collective-permute-start.42 = (f32[2,32,256]{2,1,0:T(8,128)S(1)}, f32[2,32,256]{2,1,0:T(8,128)S(1)}, u32[]{:S(2)}, u32[]{:S(2)}) collective-permute-start(f32[2,32,256]{2,1,0:T(8,128)S(1)} %add_add_fusion.2), channel_id=1, source_target_pairs={{0,24},{8,16},{16,8},{24,0},{1,25},{9,17},{17,9},{25,1},{2,26},{10... | collective-permute-start | bytes 196616 | tf_op jit(solution)/shard_map/ppermute | solution.py:248
  203.2 10.6 %collective-permute-start.43 = (f32[2,32,256]{2,1,0:T(8,128)S(1)}, f32[2,32,256]{2,1,0:T(8,128)S(1)}, u32[]{:S(2)}, u32[]{:S(2)}) collective-permute-start(f32[2,32,256]{2,1,0:T(8,128)S(1)} %add_add_fusion.2), channel_id=1, source_target_pairs={{0,16},{8,24},{16,0},{24,8},{1,17},{9,25},{17,1},{25,9},{2,18},{10... | collective-permute-start | bytes 196616 | tf_op jit(solution)/shard_map/ppermute | solution.py:248
  (61 other events, 452.2 us)
